TPU v7x, 32 devices: a whole 2x2x4 slice. The times are simulated.
32 devices in a mesh: shard: 4 (over z), seq: 8 (over y, x, core).
Axes of the slice: x: 2, y: 2, z: 4, core: 2. Of those that a mesh axis runs over, the one named last changes fastest.
Arguments:
- inputs: bfloat16 [4, 1536, 2048], P('shard', 'seq'), may hold values from -6 to 6
- positions: int32 [4, 1536], P('shard', 'seq'), may hold values from 0 to 1535, as said below
- attn_gain: bfloat16 [2048], P('shard'), may hold values from 0.5 to 1.5
- w_query: bfloat16 [2048, 2048], P('shard', 'seq'), may hold values from -0.125 to 0.125
- w_key: bfloat16 [2048, 2048], P('shard', 'seq'), may hold values from -0.125 to 0.125
- w_value: bfloat16 [2048, 2048], P('shard', 'seq'), may hold values from -0.125 to 0.125
- w_output: bfloat16 [2048, 2048], P('seq', 'shard'), may hold values from -0.75 to 0.75
- mlp_gain: bfloat16 [2048], P('shard'), may hold values from 0.5 to 1.5
- w_gate: bfloat16 [2048, 8192], P('shard', 'seq'), may hold values from -0.125 to 0.125
- w_up: bfloat16 [2048, 8192], P('shard', 'seq'), may hold values from -0.125 to 0.125
- w_down: bfloat16 [8192, 2048], P('seq', 'shard'), may hold values from -0.0625 to 0.0625
- cotangent: bfloat16 [4, 1536, 2048], P('shard', 'seq'), may hold values from -6 to 6
Outputs:
- output: bfloat16 [4, 1536, 2048], P('shard', 'seq')
- d_inputs: bfloat16 [4, 1536, 2048], P('shard', 'seq')
- d_attn_gain: float32 [2048], P('shard')
- d_w_query: float32 [2048, 2048], P('shard', 'seq')
- d_w_key: float32 [2048, 2048], P('shard', 'seq')
- d_w_value: float32 [2048, 2048], P('shard', 'seq')
- d_w_output: float32 [2048, 2048], P('seq', 'shard')
- d_mlp_gain: float32 [2048], P('shard')
- d_w_gate: float32 [2048, 8192], P('shard', 'seq')
- d_w_up: float32 [2048, 8192], P('shard', 'seq')
- d_w_down: float32 [8192, 2048], P('seq', 'shard')
Inputs may be any that keep to these rules, and one draw needn't show every extreme that they name: `positions`: within each sequence documents begin at places drawn from the seed, the first at token 0; a token's id is its offset from the start of its document. One sequence, drawn from the seed, is a single document of all 1536 tokens.
All inputs are finite; a program needn't handle non-finite values.
Results may differ from a plain program's by a relative error of at most 0.02.
Values may be sent and summed in bfloat16 or wider, within the bound.
A program may use at most 256 MiB of HBM per device.

v0:
```python
import math

import jax
import jax.numpy as jnp
from jax import lax
from jax.sharding import PartitionSpec as P

HD = 64


epsilon = 1e-05
theta_base = 130000.0
masked_score = -1e30


def product(left, right):
    return jnp.dot(left, right, preferred_element_type=jnp.float32)


def product_left_t(left, right):
    return lax.dot_general(
        left, right, (((0,), (0,)), ((), ())), preferred_element_type=jnp.float32
    )


def product_right_t(left, right):
    return lax.dot_general(
        left, right, (((1,), (1,)), ((), ())), preferred_element_type=jnp.float32
    )


def inverse_rms(values):
    return lax.rsqrt(jnp.mean(values * values, axis=-1, keepdims=True) + epsilon)


def norm_backward(values, inverse, gain, d_normed):
    scaled = d_normed * gain
    cubed = inverse * inverse * inverse
    d_values = inverse * scaled - values * cubed * jnp.mean(scaled * values, axis=-1, keepdims=True)
    d_gain = jnp.sum(d_normed * values * inverse, axis=0)
    return (d_values, d_gain)


def rotation_tables(position_ids, head_size):
    half = head_size // 2
    freqs = theta_base ** (-(jnp.arange(half, dtype=jnp.float32) * 2.0) / head_size)
    angles = position_ids.astype(jnp.float32)[:, None] * freqs[None, :]
    return (jnp.cos(angles), jnp.sin(angles))


def rotate(values, cosine, sine, head_size):
    row_count = values.shape[0]
    shaped = values.reshape(row_count, -1, head_size)
    half = head_size // 2
    first_half = shaped[..., :half]
    second_half = shaped[..., half:]
    cos_rows = cosine[:, None, :]
    sin_rows = sine[:, None, :]
    turned = jnp.concatenate(
        [
            first_half * cos_rows - second_half * sin_rows,
            second_half * cos_rows + first_half * sin_rows,
        ],
        axis=-1,
    )
    return turned.reshape(row_count, -1)


def attention_forward(queries, keys, values, head_size):
    length, width = queries.shape
    heads = width // head_size
    block_rows = min(512, length)
    blocks = length // block_rows
    score_scale = 1.0 / math.sqrt(head_size)
    query_blocks = queries.reshape(blocks, block_rows, heads, head_size)
    key_heads = keys.reshape(length, heads, head_size)
    value_heads = values.reshape(length, heads, head_size)
    key_index = jnp.arange(length, dtype=jnp.int32)

    def one_block(inputs):
        index, query_block = inputs
        scores = (
            jnp.einsum("qhd,khd->hqk", query_block, key_heads, preferred_element_type=jnp.float32)
            * score_scale
        )
        row_index = index * block_rows + jnp.arange(block_rows, dtype=jnp.int32)
        allowed = row_index[:, None] >= key_index[None, :]
        scores = jnp.where(allowed[None], scores, masked_score)
        largest = jnp.max(scores, axis=-1, keepdims=True)
        expo = jnp.exp(scores - largest)
        totals = jnp.sum(expo, axis=-1, keepdims=True)
        probs_low = (expo / totals).astype(jnp.bfloat16)
        mixed = jnp.einsum(
            "hqk,khd->qhd", probs_low, value_heads, preferred_element_type=jnp.float32
        )
        return (mixed.astype(jnp.bfloat16), largest + jnp.log(totals))

    mixed, log_totals = lax.map(one_block, (jnp.arange(blocks, dtype=jnp.int32), query_blocks))
    return (mixed.reshape(length, width), log_totals)


def attention_backward(queries, keys, values, log_totals, d_mixed, head_size):
    length, width = queries.shape
    heads = width // head_size
    block_rows = min(512, length)
    blocks = length // block_rows
    score_scale = 1.0 / math.sqrt(head_size)
    query_blocks = queries.reshape(blocks, block_rows, heads, head_size)
    grad_blocks = d_mixed.reshape(blocks, block_rows, heads, head_size)
    key_heads = keys.reshape(length, heads, head_size)
    value_heads = values.reshape(length, heads, head_size)
    key_index = jnp.arange(length, dtype=jnp.int32)

    def one_block(carry, inputs):
        d_keys, d_values = carry
        index, query_block, grad_block, log_block = inputs
        scores = (
            jnp.einsum("qhd,khd->hqk", query_block, key_heads, preferred_element_type=jnp.float32)
            * score_scale
        )
        row_index = index * block_rows + jnp.arange(block_rows, dtype=jnp.int32)
        allowed = row_index[:, None] >= key_index[None, :]
        probs = jnp.where(allowed[None], jnp.exp(scores - log_block), 0.0)
        probs_low = probs.astype(jnp.bfloat16)
        d_values = d_values + jnp.einsum(
            "hqk,qhd->khd", probs_low, grad_block, preferred_element_type=jnp.float32
        )
        d_probs = jnp.einsum(
            "qhd,khd->hqk", grad_block, value_heads, preferred_element_type=jnp.float32
        )
        inner = jnp.sum(d_probs * probs, axis=-1, keepdims=True)
        d_scores = (probs * (d_probs - inner)).astype(jnp.bfloat16)
        d_query = (
            jnp.einsum("hqk,khd->qhd", d_scores, key_heads, preferred_element_type=jnp.float32)
            * score_scale
        )
        d_keys = (
            d_keys
            + jnp.einsum("hqk,qhd->khd", d_scores, query_block, preferred_element_type=jnp.float32)
            * score_scale
        )
        return ((d_keys, d_values), d_query)

    zeros = jnp.zeros((length, heads, head_size), jnp.float32)
    (d_keys, d_values), d_queries = lax.scan(
        one_block,
        (zeros, zeros),
        (jnp.arange(blocks, dtype=jnp.int32), query_blocks, grad_blocks, log_totals),
    )
    return (
        d_queries.reshape(length, width).astype(jnp.bfloat16),
        d_keys.reshape(length, width).astype(jnp.bfloat16),
        d_values.reshape(length, width).astype(jnp.bfloat16),
    )


def seq_partials(term, row_count):
    return lax.psum_scatter(
        term(jnp.int32(0), row_count * lax.axis_size("seq")).astype(jnp.bfloat16),
        "seq",
        scatter_dimension=0,
        tiled=True,
    ).astype(jnp.float32)


def body(
    inputs,
    positions,
    attn_gain,
    w_query,
    w_key,
    w_value,
    w_output,
    mlp_gain,
    w_gate,
    w_up,
    w_down,
    cotangent,
):
    tokens = inputs.shape[1]
    head_size = HD
    input_rows = inputs[0].astype(jnp.float32)
    grad_rows = cotangent[0]
    position_rows = positions[0]
    (
        query_cols,
        key_cols,
        value_cols,
        output_rows,
        gate_cols,
        up_cols,
        down_rows,
        gain_one,
        gain_two,
    ) = (
        lax.all_gather(w_query, "shard", axis=0, tiled=True),
        lax.all_gather(w_key, "shard", axis=0, tiled=True),
        lax.all_gather(w_value, "shard", axis=0, tiled=True),
        lax.all_gather(w_output, "shard", axis=1, tiled=True),
        lax.all_gather(w_gate, "shard", axis=0, tiled=True),
        lax.all_gather(w_up, "shard", axis=0, tiled=True),
        lax.all_gather(w_down, "shard", axis=1, tiled=True),
        lax.all_gather(attn_gain, "shard", axis=0, tiled=True),
        lax.all_gather(mlp_gain, "shard", axis=0, tiled=True),
    )
    gain_first = gain_one.astype(jnp.float32)
    gain_second = gain_two.astype(jnp.float32)
    inverse_one = inverse_rms(input_rows)
    normed_one = (input_rows * inverse_one * gain_first).astype(jnp.bfloat16)

    def project_rotate(normed, weight, cosine, sine):
        return rotate(product(normed, weight), cosine, sine, head_size).astype(jnp.bfloat16)

    query_full, key_full, value_full, output_full = (
        lax.all_gather(query_cols, "seq", axis=1, tiled=True),
        lax.all_gather(key_cols, "seq", axis=1, tiled=True),
        lax.all_gather(value_cols, "seq", axis=1, tiled=True),
        lax.all_gather(output_rows, "seq", axis=0, tiled=True),
    )
    cosine, sine = rotation_tables(position_rows, head_size)
    query_tok = project_rotate(normed_one, query_full, cosine, sine)
    key_tok = project_rotate(normed_one, key_full, cosine, sine)
    value_tok = product(normed_one, value_full).astype(jnp.bfloat16)
    query_head, key_head, value_head = (
        lax.all_to_all(query_tok, "seq", split_axis=1, concat_axis=0, tiled=True),
        lax.all_to_all(key_tok, "seq", split_axis=1, concat_axis=0, tiled=True),
        lax.all_to_all(value_tok, "seq", split_axis=1, concat_axis=0, tiled=True),
    )
    mixed_head, log_totals = attention_forward(query_head, key_head, value_head, head_size)
    mixed_tok = lax.all_to_all(mixed_head, "seq", split_axis=0, concat_axis=1, tiled=True)
    attn_out = product(mixed_tok, output_full)
    hidden_state = input_rows + attn_out
    inverse_two = inverse_rms(hidden_state)
    normed_two = (hidden_state * inverse_two * gain_second).astype(jnp.bfloat16)
    normed_all_two, grad_all = (
        lax.all_gather(normed_two, "seq", axis=0, tiled=True),
        lax.all_gather(grad_rows, "seq", axis=0, tiled=True),
    )
    gate_pre = product(normed_all_two, gate_cols)
    up_pre = product(normed_all_two, up_cols)
    gate_sigmoid = jax.nn.sigmoid(gate_pre)
    gate_silu = gate_pre * gate_sigmoid
    activ = (gate_silu * up_pre).astype(jnp.bfloat16)

    def down_term(start, count):
        return product(activ, down_rows)

    mlp_out = seq_partials(down_term, tokens)
    output = (hidden_state + mlp_out).astype(jnp.bfloat16)
    d_activ = product_right_t(grad_all, down_rows)
    d_gate = (d_activ * up_pre * gate_sigmoid * (1.0 + gate_pre * (1.0 - gate_sigmoid))).astype(
        jnp.bfloat16
    )
    d_up = (d_activ * gate_silu).astype(jnp.bfloat16)
    grad_gate = product_left_t(normed_all_two, d_gate)
    grad_up = product_left_t(normed_all_two, d_up)
    grad_down = product_left_t(activ, grad_all)

    def normed_term(start, count):
        return product_right_t(d_gate, gate_cols) + product_right_t(d_up, up_cols)

    d_normed_two = seq_partials(normed_term, tokens)
    d_norm_two, gain_grad_two = norm_backward(hidden_state, inverse_two, gain_second, d_normed_two)
    d_hidden = grad_rows.astype(jnp.float32) + d_norm_two
    d_attn = d_hidden.astype(jnp.bfloat16)
    grad_output_full = product_left_t(mixed_tok, d_attn)
    d_mixed_tok = product_right_t(d_attn, output_full).astype(jnp.bfloat16)
    d_mixed_head = lax.all_to_all(d_mixed_tok, "seq", split_axis=1, concat_axis=0, tiled=True)
    d_query_head, d_key_head, d_value_head = attention_backward(
        query_head, key_head, value_head, log_totals, d_mixed_head, head_size
    )
    d_query_tok, d_key_tok, d_value_tok = (
        lax.all_to_all(d_query_head, "seq", split_axis=0, concat_axis=1, tiled=True),
        lax.all_to_all(d_key_head, "seq", split_axis=0, concat_axis=1, tiled=True),
        lax.all_to_all(d_value_head, "seq", split_axis=0, concat_axis=1, tiled=True),
    )
    d_query = rotate(d_query_tok.astype(jnp.float32), cosine, -sine, head_size).astype(jnp.bfloat16)
    d_key = rotate(d_key_tok.astype(jnp.float32), cosine, -sine, head_size).astype(jnp.bfloat16)
    grad_query_full = product_left_t(normed_one, d_query)
    grad_key_full = product_left_t(normed_one, d_key)
    grad_value_full = product_left_t(normed_one, d_value_tok)
    d_normed_one = (
        product_right_t(d_query, query_full)
        + product_right_t(d_key, key_full)
        + product_right_t(d_value_tok, value_full)
    )
    grad_query, grad_key, grad_value, grad_output = (
        lax.psum_scatter(
            grad_query_full.astype(jnp.bfloat16), "seq", scatter_dimension=1, tiled=True
        ).astype(jnp.float32),
        lax.psum_scatter(
            grad_key_full.astype(jnp.bfloat16), "seq", scatter_dimension=1, tiled=True
        ).astype(jnp.float32),
        lax.psum_scatter(
            grad_value_full.astype(jnp.bfloat16), "seq", scatter_dimension=1, tiled=True
        ).astype(jnp.float32),
        lax.psum_scatter(
            grad_output_full.astype(jnp.bfloat16), "seq", scatter_dimension=0, tiled=True
        ).astype(jnp.float32),
    )
    d_norm_one, gain_grad_one = norm_backward(input_rows, inverse_one, gain_first, d_normed_one)
    d_inputs = (d_hidden + d_norm_one).astype(jnp.bfloat16)
    gain_sum_one, gain_sum_two = lax.psum((gain_grad_one, gain_grad_two), "seq")
    results = (
        lax.psum_scatter(
            grad_query.astype(jnp.bfloat16), "shard", scatter_dimension=0, tiled=True
        ).astype(jnp.float32),
        lax.psum_scatter(
            grad_key.astype(jnp.bfloat16), "shard", scatter_dimension=0, tiled=True
        ).astype(jnp.float32),
        lax.psum_scatter(
            grad_value.astype(jnp.bfloat16), "shard", scatter_dimension=0, tiled=True
        ).astype(jnp.float32),
        lax.psum_scatter(
            grad_output.astype(jnp.bfloat16), "shard", scatter_dimension=1, tiled=True
        ).astype(jnp.float32),
        lax.psum_scatter(
            grad_gate.astype(jnp.bfloat16), "shard", scatter_dimension=0, tiled=True
        ).astype(jnp.float32),
        lax.psum_scatter(
            grad_up.astype(jnp.bfloat16), "shard", scatter_dimension=0, tiled=True
        ).astype(jnp.float32),
        lax.psum_scatter(
            grad_down.astype(jnp.bfloat16), "shard", scatter_dimension=1, tiled=True
        ).astype(jnp.float32),
        lax.psum_scatter(
            gain_sum_one.astype(jnp.bfloat16), "shard", scatter_dimension=0, tiled=True
        ).astype(jnp.float32),
        lax.psum_scatter(
            gain_sum_two.astype(jnp.bfloat16), "shard", scatter_dimension=0, tiled=True
        ).astype(jnp.float32),
    )
    return (
        output[None],
        d_inputs[None],
        results[7],
        results[0],
        results[1],
        results[2],
        results[3],
        results[8],
        results[4],
        results[5],
        results[6],
    )


def solution(mesh):
    in_specs = (
        P("shard", "seq", None),
        P("shard", "seq"),
        P("shard"),
        P("shard", "seq"),
        P("shard", "seq"),
        P("shard", "seq"),
        P("seq", "shard"),
        P("shard"),
        P("shard", "seq"),
        P("shard", "seq"),
        P("seq", "shard"),
        P("shard", "seq", None),
    )
    out_specs = (
        P("shard", "seq", None),
        P("shard", "seq", None),
        P("shard"),
        P("shard", "seq"),
        P("shard", "seq"),
        P("shard", "seq"),
        P("seq", "shard"),
        P("shard"),
        P("shard", "seq"),
        P("shard", "seq"),
        P("seq", "shard"),
    )
    return jax.shard_map(body, mesh=mesh, in_specs=in_specs, out_specs=out_specs, check_vma=False)
```

profile of v0, /device:TPU:0, one launch (start us, length us, event | category | flops | bytes accessed | tf_op | source)
XLA Modules:
  0.0 1646.7 jit_solution(4252797177175899941)
XLA Ops:
  10.0 30.2 %all-gather.21.cloned.1.call-done = bf16[2048,256]{1,0:T(8,128)(2,1)} async-done(((bf16[512,256]{1,0:T(8,128)(2,1)}), bf16[2048,256]{1,0:T(8,128)(2,1)}) %all-gather.21.cloned.1.call-update) | async-done | bytes 1048592 | tf_op jit(solution)/shard_map/all_gather | solution.py:197
  40.3 29.0 %all-gather.17.cloned.1.call-done = bf16[2048,256]{1,0:T(8,128)(2,1)} async-done(((bf16[512,256]{1,0:T(8,128)(2,1)}), bf16[2048,256]{1,0:T(8,128)(2,1)}) %all-gather.17.cloned.1.call-update) | async-done | bytes 1048592 | tf_op jit(solution)/shard_map/all_gather | solution.py:196
  69.4 29.0 %all-gather.25.cloned.1.call-done = bf16[2048,256]{1,0:T(8,128)(2,1)} async-done(((bf16[512,256]{1,0:T(8,128)(2,1)}), bf16[2048,256]{1,0:T(8,128)(2,1)}) %all-gather.25.cloned.1.call-update) | async-done | bytes 1048592 | tf_op jit(solution)/shard_map/all_gather | solution.py:198
  98.4 28.8 %all-gather.29.cloned.1.call-done = bf16[256,2048]{1,0:T(8,128)(2,1)} async-done(((bf16[256,512]{1,0:T(8,128)(2,1)}), bf16[256,2048]{1,0:T(8,128)(2,1)}) %all-gather.29.cloned.1.call-update) | async-done | bytes 1048592 | tf_op jit(solution)/shard_map/all_gather | solution.py:199
  140.9 43.6 %all-gather.23.cloned.1.call-done = bf16[2048,2048]{1,0:T(8,128)(2,1)} async-done(((bf16[2048,256]{1,0:T(8,128)(2,1)}), bf16[2048,2048]{1,0:T(8,128)(2,1)}) %all-gather.23.cloned.1.call-update) | async-done | bytes 8388624 | tf_op jit(solution)/shard_map/all_gather | solution.py:216
  196.9 45.3 %all-gather.19.cloned.1.call-done = bf16[2048,2048]{1,0:T(8,128)(2,1)} async-done(((bf16[2048,256]{1,0:T(8,128)(2,1)}), bf16[2048,2048]{1,0:T(8,128)(2,1)}) %all-gather.19.cloned.1.call-update) | async-done | bytes 8388624 | tf_op jit(solution)/shard_map/all_gather | solution.py:215
  349.8 38.9 %while.28 = (s32[]{:T(128)}, bf16[3,512,4,64]{1,3,2,0:T(8,128)(2,1)}, f32[3,4,512,1]{2,1,3,0:T(4,128)S(1)}, s32[3]{0:T(128)S(1)}, bf16[3,512,4,64]{1,3,2,0:T(8,1...) while((s32[]{:T(128)}, ...), condition=%wide.region_4.5_spmd.clone, body=%wide.region_1.4_spmd.clone.sunk | while | flops 843971072 | bytes 43061888 | solution.py:98
  424.0 37.8 %all-gather.35.cloned.1.call-done = bf16[2048,1024]{1,0:T(8,128)(2,1)} async-done(((bf16[512,1024]{1,0:T(8,128)(2,1)}), bf16[2048,1024]{1,0:T(8,128)(2,1)}) %all-gather.35.cloned.1.call-update) | async-done | bytes 4194320 | tf_op jit(solution)/shard_map/all_gather | solution.py:200
  461.7 46.4 %all-gather.33.cloned.1.call-done = bf16[1536,2048]{1,0:T(8,128)(2,1)} async-done(((bf16[192,2048]{1,0:T(8,128)(2,1)}), bf16[1536,2048]{1,0:T(8,128)(2,1)}) %all-gather.33.cloned.1.call-update) | async-done | bytes 6291472 | tf_op jit(solution)/shard_map/all_gather | solution.py:236
  519.7 70.8 %all-gather.37.cloned.1.call-done = bf16[2048,1024]{1,0:T(8,128)(2,1)} async-done(((bf16[512,1024]{1,0:T(8,128)(2,1)}), bf16[2048,1024]{1,0:T(8,128)(2,1)}) %all-gather.37.cloned.1.call-update) | async-done | bytes 4194320 | tf_op jit(solution)/shard_map/all_gather | solution.py:201
  602.2 69.1 %all-gather.39.cloned.1.call-done = bf16[1024,2048]{1,0:T(8,128)(2,1)} async-done(((bf16[1024,512]{1,0:T(8,128)(2,1)}), bf16[1024,2048]{1,0:T(8,128)(2,1)}) %all-gather.39.cloned.1.call-update) | async-done | bytes 4194320 | tf_op jit(solution)/shard_map/all_gather | solution.py:202
  671.2 46.0 %all-gather.41.cloned.1.call-done = bf16[1,1536,2048]{2,1,0:T(8,128)(2,1)} async-done(((bf16[1,192,2048]{2,1,0:T(8,128)(2,1)}), bf16[1,1536,2048]{2,1,0:T(8,128)(2,1)}) %all-gather.41.cloned.1.call-update) | async-done | bytes 6291472 | tf_op jit(solution)/shard_map/all_gather | solution.py:237
  770.2 50.6 %reduce-scatter.16.cloned.1.call-done = bf16[192,2048]{1,0:T(8,128)(2,1)} async-done(((bf16[1536,2048]{1,0:T(8,128)(2,1)}), bf16[192,2048]{1,0:T(8,128)(2,1)}) %reduce-scatter.16.cloned.1.call-update) | async-done | bytes 786448 | tf_op jit(solution)/shard_map/reduce_scatter | solution.py:158
  823.0 63.2 %reduce-scatter.14.cloned.1.call-done = bf16[192,2048]{1,0:T(8,128)(2,1)} async-done(((bf16[1536,2048]{1,0:T(8,128)(2,1)}), bf16[192,2048]{1,0:T(8,128)(2,1)}) %reduce-scatter.14.cloned.1.call-update) | async-done | bytes 786448 | tf_op jit(solution)/shard_map/reduce_scatter | solution.py:158
  920.9 86.6 %while.29 = (s32[]{:T(128)}, f32[1536,4,64]{0,2,1:T(8,128)S(1)}, f32[1536,4,64]{0,2,1:T(8,128)}, bf16[3,512,4,64]{1,3,2,0:T(8,128)(2,1)}, bf16[3,512,4,64]{1,3,2...) while((s32[]{:T(128)}, f32[1536,4,64]{0,2,1:T(8,128)S(1)}, ...), condition=%wide.region_11.12_spmd.clone, body=%wide.region_9.11_spmd.clone.sunk | while | flops 2044459520 | bytes 206879472 | solution.py:145
  1107.8 24.2 %all_to_all.113 = bf16[8,192,256]{2,1,0:T(8,128)(2,1)S(1)} all-to-all(bf16[8,192,256]{2,1,0:T(8,128)(2,1)} %copy.64), channel_id=1, replica_groups=mesh['shard'=4,'seq'=8] {'seq'}, dimensions={0} | all-to-all | bytes 1572864 | tf_op jit(solution)/shard_map/all_to_all | solution.py:275
  1139.2 70.9 %reduce-scatter.18.cloned.1.call-done = bf16[2048,256]{1,0:T(8,128)(2,1)} async-done(((bf16[2048,2048]{1,0:T(8,128)(2,1)}), bf16[2048,256]{1,0:T(8,128)(2,1)}) %reduce-scatter.18.cloned.1.call-update) | async-done | bytes 1048592 | tf_op jit(solution)/shard_map/reduce_scatter | solution.py:288
  1211.7 77.6 %reduce-scatter.34.cloned.1.call-done = bf16[512,1024]{1,0:T(8,128)(2,1)} async-done(((bf16[2048,1024]{1,0:T(8,128)(2,1)}), bf16[512,1024]{1,0:T(8,128)(2,1)}) %reduce-scatter.34.cloned.1.call-update) | async-done | bytes 1048592 | tf_op jit(solution)/shard_map/reduce_scatter | solution.py:317
  1292.0 76.7 %reduce-scatter.36.cloned.1.call-done = bf16[512,1024]{1,0:T(8,128)(2,1)} async-done(((bf16[2048,1024]{1,0:T(8,128)(2,1)}), bf16[512,1024]{1,0:T(8,128)(2,1)}) %reduce-scatter.36.cloned.1.call-update) | async-done | bytes 1048592 | tf_op jit(solution)/shard_map/reduce_scatter | solution.py:320
  1371.5 76.9 %reduce-scatter.38.cloned.1.call-done = bf16[1024,512]{1,0:T(8,128)(2,1)} async-done(((bf16[1024,2048]{1,0:T(8,128)(2,1)}), bf16[1024,512]{1,0:T(8,128)(2,1)}) %reduce-scatter.38.cloned.1.call-update) | async-done | bytes 1048592 | tf_op jit(solution)/shard_map/reduce_scatter | solution.py:323
  1459.0 64.7 %reduce-scatter.26.cloned.1.call-done = bf16[2048,256]{1,0:T(8,128)(2,1)} async-done(((bf16[2048,2048]{1,0:T(8,128)(2,1)}), bf16[2048,256]{1,0:T(8,128)(2,1)}) %reduce-scatter.26.cloned.1.call-update) | async-done | bytes 1048592 | tf_op jit(solution)/shard_map/reduce_scatter | solution.py:294
  1538.6 23.5 %all-reduce.2 = (bf16[2048]{0:T(1024)(128)(2,1)S(1)}, bf16[2048]{0:T(1024)(128)(2,1)S(1)}) all-reduce(f32[2048]{0:T(1024)S(1)} %get-tuple-element.205, f32[2048]{0:T(1024)S(1)} %copy-done.23), channel_id=1, replica_groups=mesh['shard'=4,'seq'=8] {'seq'}, use_global_device_ids=true, to_apply=%region_14.15 | all-reduce | flops 4096 | bytes 24576 | tf_op jit(solution)/shard_map/psum | solution.py:303
  1583.5 26.4 %reduce-scatter.20.cloned.1.call-done = bf16[512,256]{1,0:T(8,128)(2,1)} async-done(((bf16[2048,256]{1,0:T(8,128)(2,1)}), bf16[512,256]{1,0:T(8,128)(2,1)}) %reduce-scatter.20.cloned.1.call-update) | async-done | bytes 262160 | tf_op jit(solution)/shard_map/reduce_scatter | solution.py:305
  1611.8 26.2 %reduce-scatter.28.cloned.1.call-done = bf16[512,256]{1,0:T(8,128)(2,1)} async-done(((bf16[2048,256]{1,0:T(8,128)(2,1)}), bf16[512,256]{1,0:T(8,128)(2,1)}) %reduce-scatter.28.cloned.1.call-update) | async-done | bytes 262160 | tf_op jit(solution)/shard_map/reduce_scatter | solution.py:311
  (287 shorter events, 570.1 us)
Async XLA Ops:
  8.7 89.6 %all-gather.25.cloned.1.call-start = ((), (), s32[]{:S(2)}) async-start(), calls=%async_computation.25 | async-start | bytes 1310720 | tf_op jit(solution)/shard_map/all_gather | solution.py:198
  9.4 117.8 %all-gather.29.cloned.1.call-start = ((), (), s32[]{:S(2)}) async-start(), calls=%async_computation.27 | async-start | bytes 1310720 | tf_op jit(solution)/shard_map/all_gather | solution.py:199
  10.0 174.5 %all-gather.23.cloned.1.call-start = ((), (), s32[]{:S(2)}) async-start(), calls=%async_computation.24 | async-start | bytes 9437184 | tf_op jit(solution)/shard_map/all_gather | solution.py:216
  40.3 201.9 %all-gather.19.cloned.1.call-start = ((), (), s32[]{:S(2)}) async-start(), calls=%async_computation.22 | async-start | bytes 9437184 | tf_op jit(solution)/shard_map/all_gather | solution.py:215
  69.3 244.1 %all-gather.27.cloned.1.call-start = ((), (), s32[]{:S(2)}) async-start(), calls=%async_computation.26 | async-start | bytes 9437184 | tf_op jit(solution)/shard_map/all_gather | solution.py:217
  98.4 316.6 %all-gather.31.cloned.1.call-start = ((), (), s32[]{:S(2)}) async-start(), calls=%async_computation.28 | async-start | bytes 9437184 | tf_op jit(solution)/shard_map/all_gather | solution.py:218
  324.1 137.6 %all-gather.35.cloned.1.call-start = ((), (), s32[]{:S(2)}) async-start(), calls=%async_computation.30 | async-start | bytes 5242880 | tf_op jit(solution)/shard_map/all_gather | solution.py:200
  400.2 107.9 %all-gather.33.cloned.1.call-start = ((), (), s32[]{:S(2)}) async-start(), calls=%async_computation.29 | async-start | bytes 7077888 | tf_op jit(solution)/shard_map/all_gather | solution.py:236
  421.7 168.8 %all-gather.37.cloned.1.call-start = ((), (), s32[]{:S(2)}) async-start(), calls=%async_computation.31 | async-start | bytes 5242880 | tf_op jit(solution)/shard_map/all_gather | solution.py:201
  422.4 248.8 %all-gather.39.cloned.1.call-start = ((), (), s32[]{:S(2)}) async-start(), calls=%async_computation.32 | async-start | bytes 5242880 | tf_op jit(solution)/shard_map/all_gather | solution.py:202
  423.0 294.2 %all-gather.41.cloned.1.call-start = ((), (), s32[]{:S(2)}) async-start(), calls=%async_computation.46 | async-start | bytes 7077888 | tf_op jit(solution)/shard_map/all_gather | solution.py:237
  423.7 397.1 %reduce-scatter.16.cloned.1.call-start = ((), (), s32[]{:S(2)}) async-start(), calls=%async_computation.34 | async-start | bytes 7077888 | tf_op jit(solution)/shard_map/reduce_scatter | solution.py:158
  758.9 127.3 %reduce-scatter.14.cloned.1.call-start = ((), (), s32[]{:S(2)}) async-start(), calls=%async_computation.33 | async-start | bytes 7077888 | tf_op jit(solution)/shard_map/reduce_scatter | solution.py:158
  901.0 236.9 %reduce-scatter.30.cloned.1.call-start = ((), (), s32[]{:S(2)}) async-start(), calls=%async_computation.41 | async-start | bytes 9437184 | tf_op jit(solution)/shard_map/reduce_scatter | solution.py:297
  1031.7 106.9 %reduce-scatter.22.cloned.1.call-start = ((), (), s32[]{:S(2)}) async-start(), calls=%async_computation.37 | async-start | bytes 9437184 | tf_op jit(solution)/shard_map/reduce_scatter | solution.py:291
  1057.5 152.6 %reduce-scatter.18.cloned.1.call-start = ((), (), s32[]{:S(2)}) async-start(), calls=%async_computation.35 | async-start | bytes 9437184 | tf_op jit(solution)/shard_map/reduce_scatter | solution.py:288
  1066.2 223.1 %reduce-scatter.34.cloned.1.call-start = ((), (), s32[]{:S(2)}) async-start(), calls=%async_computation.43 | async-start | bytes 5242880 | tf_op jit(solution)/shard_map/reduce_scatter | solution.py:317
  1078.6 290.1 %reduce-scatter.36.cloned.1.call-start = ((), (), s32[]{:S(2)}) async-start(), calls=%async_computation.44 | async-start | bytes 5242880 | tf_op jit(solution)/shard_map/reduce_scatter | solution.py:320
  1090.1 358.3 %reduce-scatter.38.cloned.1.call-start = ((), (), s32[]{:S(2)}) async-start(), calls=%async_computation.45 | async-start | bytes 5242880 | tf_op jit(solution)/shard_map/reduce_scatter | solution.py:323
  1101.7 422.0 %reduce-scatter.26.cloned.1.call-start = ((), (), s32[]{:S(2)}) async-start(), calls=%async_computation.39 | async-start | bytes 9437184 | tf_op jit(solution)/shard_map/reduce_scatter | solution.py:294
  1137.8 441.1 %reduce-scatter.32.cloned.1.call-start = ((), (), s32[]{:S(2)}) async-start(), calls=%async_computation.42 | async-start | bytes 1310720 | tf_op jit(solution)/shard_map/reduce_scatter | solution.py:314
  1138.6 443.2 %reduce-scatter.24.cloned.1.call-start = ((), (), s32[]{:S(2)}) async-start(), calls=%async_computation.38 | async-start | bytes 1310720 | tf_op jit(solution)/shard_map/reduce_scatter | solution.py:308
  1139.2 470.8 %reduce-scatter.20.cloned.1.call-start = ((), (), s32[]{:S(2)}) async-start(), calls=%async_computation.36 | async-start | bytes 1310720 | tf_op jit(solution)/shard_map/reduce_scatter | solution.py:305
  1210.1 427.8 %reduce-scatter.28.cloned.1.call-start = ((), (), s32[]{:S(2)}) async-start(), calls=%async_computation.40 | async-start | bytes 1310720 | tf_op jit(solution)/shard_map/reduce_scatter | solution.py:311
  (45 other events, 1577.6 us)
Sparse Core Ops, SparseCore 0:
  9.6 30.6 all-gather.20
  41.8 27.4 all-gather.16
  70.9 27.4 all-gather.24
  99.8 27.4 all-gather.28
  128.9 55.4 all-gather.22
  186.2 55.9 all-gather.18
  244.1 69.3 all-gather.26
  315.3 63.8 all-gather.30
  380.8 80.8 all-gather.34
  464.0 44.0 all-gather.32
  509.7 80.7 all-gather.36
  591.9 79.2 all-gather.38
  673.1 44.0 all-gather.40
  759.0 61.7 reduce-scatter.15
  824.4 61.7 reduce-scatter.13
  908.8 72.6 reduce-scatter.29
  1057.6 77.9 reduce-scatter.21
  1139.0 71.0 reduce-scatter.17
  1212.5 76.7 reduce-scatter.33
  1291.4 77.2 reduce-scatter.35
  1371.1 77.2 reduce-scatter.37
  1451.9 71.7 reduce-scatter.25
  1526.1 27.0 reduce-scatter.31
  1555.4 26.3 reduce-scatter.23
  (2 shorter events, 51.5 us)
where the time goes:
time: 1660 us; the launch traced here: 1650 us
  waiting for transfers between devices  1090 us (66%)
  matrix products  275 us (17%)
  blocking collectives  84.6 us (5%)
  local copies, waits for them, and re-layouts  81.6 us (5%)
  other arithmetic  62.3 us (4%)
  starting transfers between devices  29.5 us (2%)
    reduce_scatter x2, waiting for transfers between devices, seq_partials(): lax.psum_scatter(term(jnp.int32(0), row_count * lax.axis_size('seq')).ast...  114 us
    reduce_scatter x1, waiting for transfers between devices, body(): lax.psum_scatter(grad_gate.astype(jnp.bfloat16), 'shard', scatter_dimensi...  77.6 us
    reduce_scatter x1, waiting for transfers between devices, body(): lax.psum_scatter(grad_down.astype(jnp.bfloat16), 'shard', scatter_dimensi...  76.9 us
    reduce_scatter x1, waiting for transfers between devices, body(): lax.psum_scatter(grad_up.astype(jnp.bfloat16), 'shard', scatter_dimension...  76.7 us
    dot_general x7, matrix products, product_right_t(): lax.dot_general(left, right, (((1,), (1,)), ((), ())), preferred_element_...  71.1 us
    reduce_scatter x1, waiting for transfers between devices, body(): lax.psum_scatter(grad_query_full.astype(jnp.bfloat16), 'seq', scatter_dim...  70.9 us
    all_gather x1, waiting for transfers between devices, body(): lax.all_gather(w_up, 'shard', axis=0, tiled=True)  70.8 us
    all_gather x1, waiting for transfers between devices, body(): lax.all_gather(w_down, 'shard', axis=1, tiled=True)  69.1 us
  transfers between devices with their start and end apart: 33, of which 28 were waited for; matrix products, arithmetic and copies ran while one was open for 22% of the time, Pallas kernels for 0%

commit v1 on v0

--- a/solution.py
+++ b/solution.py
@@ -179,169 +179,93 @@
 ):
     tokens = inputs.shape[1]
     head_size = HD
+    cols = w_query.shape[1]
     input_rows = inputs[0].astype(jnp.float32)
     grad_rows = cotangent[0]
-    position_rows = positions[0]
-    (
-        query_cols,
-        key_cols,
-        value_cols,
-        output_rows,
-        gate_cols,
-        up_cols,
-        down_rows,
-        gain_one,
-        gain_two,
-    ) = (
-        lax.all_gather(w_query, "shard", axis=0, tiled=True),
-        lax.all_gather(w_key, "shard", axis=0, tiled=True),
-        lax.all_gather(w_value, "shard", axis=0, tiled=True),
-        lax.all_gather(w_output, "shard", axis=1, tiled=True),
-        lax.all_gather(w_gate, "shard", axis=0, tiled=True),
-        lax.all_gather(w_up, "shard", axis=0, tiled=True),
-        lax.all_gather(w_down, "shard", axis=1, tiled=True),
-        lax.all_gather(attn_gain, "shard", axis=0, tiled=True),
-        lax.all_gather(mlp_gain, "shard", axis=0, tiled=True),
-    )
-    gain_first = gain_one.astype(jnp.float32)
-    gain_second = gain_two.astype(jnp.float32)
+    gains = lax.all_gather(jnp.stack([attn_gain, mlp_gain]), "shard", axis=1, tiled=True)
+    gain_first = gains[0].astype(jnp.float32)
+    gain_second = gains[1].astype(jnp.float32)
+    position_all = lax.all_gather(positions[0], "seq", axis=0, tiled=True)
     inverse_one = inverse_rms(input_rows)
     normed_one = (input_rows * inverse_one * gain_first).astype(jnp.bfloat16)
-
-    def project_rotate(normed, weight, cosine, sine):
-        return rotate(product(normed, weight), cosine, sine, head_size).astype(jnp.bfloat16)
-
-    query_full, key_full, value_full, output_full = (
-        lax.all_gather(query_cols, "seq", axis=1, tiled=True),
-        lax.all_gather(key_cols, "seq", axis=1, tiled=True),
-        lax.all_gather(value_cols, "seq", axis=1, tiled=True),
-        lax.all_gather(output_rows, "seq", axis=0, tiled=True),
-    )
-    cosine, sine = rotation_tables(position_rows, head_size)
-    query_tok = project_rotate(normed_one, query_full, cosine, sine)
-    key_tok = project_rotate(normed_one, key_full, cosine, sine)
-    value_tok = product(normed_one, value_full).astype(jnp.bfloat16)
-    query_head, key_head, value_head = (
-        lax.all_to_all(query_tok, "seq", split_axis=1, concat_axis=0, tiled=True),
-        lax.all_to_all(key_tok, "seq", split_axis=1, concat_axis=0, tiled=True),
-        lax.all_to_all(value_tok, "seq", split_axis=1, concat_axis=0, tiled=True),
-    )
+    normed_all_one = lax.all_gather(normed_one, "seq", axis=0, tiled=True)
+    attn_cols = lax.all_gather(
+        jnp.concatenate([w_query, w_key, w_value], axis=1), "shard", axis=0, tiled=True
+    )
+    output_rows = lax.all_gather(w_output, "shard", axis=1, tiled=True)
+    gate_cols = lax.all_gather(w_gate, "shard", axis=0, tiled=True)
+    up_cols = lax.all_gather(w_up, "shard", axis=0, tiled=True)
+    down_rows = lax.all_gather(w_down, "shard", axis=1, tiled=True)
+    grad_all = lax.all_gather(grad_rows, "seq", axis=0, tiled=True)
+
+    cosine, sine = rotation_tables(position_all, head_size)
+    projected = product(normed_all_one, attn_cols)
+    query_head = rotate(projected[:, :cols], cosine, sine, head_size).astype(jnp.bfloat16)
+    key_head = rotate(projected[:, cols : 2 * cols], cosine, sine, head_size).astype(jnp.bfloat16)
+    value_head = projected[:, 2 * cols :].astype(jnp.bfloat16)
     mixed_head, log_totals = attention_forward(query_head, key_head, value_head, head_size)
-    mixed_tok = lax.all_to_all(mixed_head, "seq", split_axis=0, concat_axis=1, tiled=True)
-    attn_out = product(mixed_tok, output_full)
+    attn_out = seq_partials(lambda start, count: product(mixed_head, output_rows), tokens)
     hidden_state = input_rows + attn_out
     inverse_two = inverse_rms(hidden_state)
     normed_two = (hidden_state * inverse_two * gain_second).astype(jnp.bfloat16)
-    normed_all_two, grad_all = (
-        lax.all_gather(normed_two, "seq", axis=0, tiled=True),
-        lax.all_gather(grad_rows, "seq", axis=0, tiled=True),
-    )
+    normed_all_two = lax.all_gather(normed_two, "seq", axis=0, tiled=True)
     gate_pre = product(normed_all_two, gate_cols)
     up_pre = product(normed_all_two, up_cols)
     gate_sigmoid = jax.nn.sigmoid(gate_pre)
     gate_silu = gate_pre * gate_sigmoid
     activ = (gate_silu * up_pre).astype(jnp.bfloat16)
-
-    def down_term(start, count):
-        return product(activ, down_rows)
-
-    mlp_out = seq_partials(down_term, tokens)
+    mlp_out = seq_partials(lambda start, count: product(activ, down_rows), tokens)
     output = (hidden_state + mlp_out).astype(jnp.bfloat16)
     d_activ = product_right_t(grad_all, down_rows)
     d_gate = (d_activ * up_pre * gate_sigmoid * (1.0 + gate_pre * (1.0 - gate_sigmoid))).astype(
         jnp.bfloat16
     )
     d_up = (d_activ * gate_silu).astype(jnp.bfloat16)
+    d_normed_two = seq_partials(
+        lambda start, count: product_right_t(d_gate, gate_cols) + product_right_t(d_up, up_cols),
+        tokens,
+    )
     grad_gate = product_left_t(normed_all_two, d_gate)
     grad_up = product_left_t(normed_all_two, d_up)
     grad_down = product_left_t(activ, grad_all)
-
-    def normed_term(start, count):
-        return product_right_t(d_gate, gate_cols) + product_right_t(d_up, up_cols)
-
-    d_normed_two = seq_partials(normed_term, tokens)
     d_norm_two, gain_grad_two = norm_backward(hidden_state, inverse_two, gain_second, d_normed_two)
     d_hidden = grad_rows.astype(jnp.float32) + d_norm_two
-    d_attn = d_hidden.astype(jnp.bfloat16)
-    grad_output_full = product_left_t(mixed_tok, d_attn)
-    d_mixed_tok = product_right_t(d_attn, output_full).astype(jnp.bfloat16)
-    d_mixed_head = lax.all_to_all(d_mixed_tok, "seq", split_axis=1, concat_axis=0, tiled=True)
+    d_attn = lax.all_gather(d_hidden.astype(jnp.bfloat16), "seq", axis=0, tiled=True)
+    d_mixed_head = product_right_t(d_attn, output_rows).astype(jnp.bfloat16)
+    grad_output = product_left_t(mixed_head, d_attn)
     d_query_head, d_key_head, d_value_head = attention_backward(
         query_head, key_head, value_head, log_totals, d_mixed_head, head_size
     )
-    d_query_tok, d_key_tok, d_value_tok = (
-        lax.all_to_all(d_query_head, "seq", split_axis=0, concat_axis=1, tiled=True),
-        lax.all_to_all(d_key_head, "seq", split_axis=0, concat_axis=1, tiled=True),
-        lax.all_to_all(d_value_head, "seq", split_axis=0, concat_axis=1, tiled=True),
-    )
-    d_query = rotate(d_query_tok.astype(jnp.float32), cosine, -sine, head_size).astype(jnp.bfloat16)
-    d_key = rotate(d_key_tok.astype(jnp.float32), cosine, -sine, head_size).astype(jnp.bfloat16)
-    grad_query_full = product_left_t(normed_one, d_query)
-    grad_key_full = product_left_t(normed_one, d_key)
-    grad_value_full = product_left_t(normed_one, d_value_tok)
-    d_normed_one = (
-        product_right_t(d_query, query_full)
-        + product_right_t(d_key, key_full)
-        + product_right_t(d_value_tok, value_full)
-    )
-    grad_query, grad_key, grad_value, grad_output = (
-        lax.psum_scatter(
-            grad_query_full.astype(jnp.bfloat16), "seq", scatter_dimension=1, tiled=True
-        ).astype(jnp.float32),
-        lax.psum_scatter(
-            grad_key_full.astype(jnp.bfloat16), "seq", scatter_dimension=1, tiled=True
-        ).astype(jnp.float32),
-        lax.psum_scatter(
-            grad_value_full.astype(jnp.bfloat16), "seq", scatter_dimension=1, tiled=True
-        ).astype(jnp.float32),
-        lax.psum_scatter(
-            grad_output_full.astype(jnp.bfloat16), "seq", scatter_dimension=0, tiled=True
-        ).astype(jnp.float32),
-    )
+    d_query = rotate(d_query_head.astype(jnp.float32), cosine, -sine, head_size)
+    d_key = rotate(d_key_head.astype(jnp.float32), cosine, -sine, head_size)
+    d_qkv = jnp.concatenate(
+        [d_query.astype(jnp.bfloat16), d_key.astype(jnp.bfloat16), d_value_head], axis=1
+    )
+    d_normed_one = seq_partials(lambda start, count: product_right_t(d_qkv, attn_cols), tokens)
+    grad_attn = product_left_t(normed_all_one, d_qkv)
     d_norm_one, gain_grad_one = norm_backward(input_rows, inverse_one, gain_first, d_normed_one)
     d_inputs = (d_hidden + d_norm_one).astype(jnp.bfloat16)
-    gain_sum_one, gain_sum_two = lax.psum((gain_grad_one, gain_grad_two), "seq")
-    results = (
-        lax.psum_scatter(
-            grad_query.astype(jnp.bfloat16), "shard", scatter_dimension=0, tiled=True
-        ).astype(jnp.float32),
-        lax.psum_scatter(
-            grad_key.astype(jnp.bfloat16), "shard", scatter_dimension=0, tiled=True
-        ).astype(jnp.float32),
-        lax.psum_scatter(
-            grad_value.astype(jnp.bfloat16), "shard", scatter_dimension=0, tiled=True
-        ).astype(jnp.float32),
-        lax.psum_scatter(
-            grad_output.astype(jnp.bfloat16), "shard", scatter_dimension=1, tiled=True
-        ).astype(jnp.float32),
-        lax.psum_scatter(
-            grad_gate.astype(jnp.bfloat16), "shard", scatter_dimension=0, tiled=True
-        ).astype(jnp.float32),
-        lax.psum_scatter(
-            grad_up.astype(jnp.bfloat16), "shard", scatter_dimension=0, tiled=True
-        ).astype(jnp.float32),
-        lax.psum_scatter(
-            grad_down.astype(jnp.bfloat16), "shard", scatter_dimension=1, tiled=True
-        ).astype(jnp.float32),
-        lax.psum_scatter(
-            gain_sum_one.astype(jnp.bfloat16), "shard", scatter_dimension=0, tiled=True
-        ).astype(jnp.float32),
-        lax.psum_scatter(
-            gain_sum_two.astype(jnp.bfloat16), "shard", scatter_dimension=0, tiled=True
-        ).astype(jnp.float32),
-    )
+    gain_sums = lax.psum(jnp.stack([gain_grad_one, gain_grad_two]), "seq")
+
+    def shard_sum(grad, dimension):
+        return lax.psum_scatter(
+            grad.astype(jnp.bfloat16), "shard", scatter_dimension=dimension, tiled=True
+        ).astype(jnp.float32)
+
+    attn_sum = shard_sum(grad_attn, 0)
+    gain_out = lax.psum_scatter(gain_sums, "shard", scatter_dimension=1, tiled=True)
     return (
         output[None],
         d_inputs[None],
-        results[7],
-        results[0],
-        results[1],
-        results[2],
-        results[3],
-        results[8],
-        results[4],
-        results[5],
-        results[6],
+        gain_out[0],
+        attn_sum[:, :cols],
+        attn_sum[:, cols : 2 * cols],
+        attn_sum[:, 2 * cols :],
+        shard_sum(grad_output, 1),
+        gain_out[1],
+        shard_sum(grad_gate, 0),
+        shard_sum(grad_up, 0),
+        shard_sum(grad_down, 1),
     )
 
 

time: 1660 us -> 1250 us (0.75)
  waiting for transfers between devices: 1090 us -> 869 us
  local copies, waits for them, and re-layouts: 81.6 us -> 22.5 us
  blocking collectives: 84.6 us -> 35.1 us
  matrix products: 275 us -> 227 us
  starting transfers between devices: 29.5 us -> 0.98 us
    reduce_scatter x11 -> x5, waiting for transfers between devices: 420 us -> 190 us  [shard_sum(): lax.psum_scatter(grad.astype(jnp.bfloat16), 'shard', scatter_dimension=di...]
    reduce_scatter x2 -> x4, waiting for transfers between devices: 114 us -> 248 us  [seq_partials(): lax.psum_scatter(term(jnp.int32(0), row_count * lax.axis_size('seq')).ast...]
    all_gather x13 -> x9, waiting for transfers between devices: 497 us -> 402 us  [the longest x1 76.2 us: body(): up_cols = lax.all_gather(w_up, 'shard', axis=0, tiled=True)]
    all_to_all x7 -> x0, waiting for transfers between devices: 56.6 us -> none  [the longest x1 18.4 us: body(): lax.all_to_all(query_tok, 'seq', split_axis=1, concat_axis=0, tiled=True)]
    all_to_all x7 -> x0, starting transfers between devices: 27.1 us -> none  [the longest x1 4.5 us: body(): lax.all_to_all(value_tok, 'seq', split_axis=1, concat_axis=0, tiled=True)]
    dot_general x2 -> x0, local copies, waits for them, and re-layouts: 24.8 us -> none  [product(): return jnp.dot(left, right, preferred_element_type=jnp.float32)]
    all_to_all x1 -> x0, blocking collectives: 24.2 us -> none  [body(): lax.all_to_all(d_value_head, 'seq', split_axis=0, concat_axis=1, tiled=True)]
    unnamed x26 -> x20, waiting for transfers between devices: 6.11 us -> 29.2 us
  transfers between devices with their start and end apart: 33 -> 19, of which waited for: 28 -> 17; matrix products, arithmetic and copies ran while one was open for 22% -> 21% of each run, Pallas kernels for 0% -> 0%
where the time goes in v1:
time: 1250 us; the launch traced here: 1240 us
  waiting for transfers between devices  869 us (70%)
  matrix products  227 us (18%)
  other arithmetic  68.5 us (5%)
  blocking collectives  35.1 us (3%)
  local copies, waits for them, and re-layouts  22.5 us (2%)
  between operations  15.4 us (1%)
    reduce_scatter x4, waiting for transfers between devices, seq_partials(): lax.psum_scatter(term(jnp.int32(0), row_count * lax.axis_size('seq')).ast...  248 us
    reduce_scatter x5, waiting for transfers between devices, shard_sum(): lax.psum_scatter(grad.astype(jnp.bfloat16), 'shard', scatter_dimension=di...  190 us
    all_gather x1, waiting for transfers between devices, body(): up_cols = lax.all_gather(w_up, 'shard', axis=0, tiled=True)  76.2 us
    all_gather x1, waiting for transfers between devices, body(): gate_cols = lax.all_gather(w_gate, 'shard', axis=0, tiled=True)  70.7 us
    all_gather x1, waiting for transfers between devices, body(): down_rows = lax.all_gather(w_down, 'shard', axis=1, tiled=True)  69.3 us
    dot_general x5, matrix products, product_right_t(): lax.dot_general(left, right, (((1,), (1,)), ((), ())), preferred_element_...  57.3 us
    dot_general x5, matrix products, product(): return jnp.dot(left, right, preferred_element_type=jnp.float32)  49.2 us
    dot_general x5, matrix products, product_left_t(): lax.dot_general(left, right, (((0,), (0,)), ((), ())), preferred_element_...  48.7 us
  transfers between devices with their start and end apart: 19, of which 17 were waited for; matrix products, arithmetic and copies ran while one was open for 21% of the time, Pallas kernels for 0%

profile of v1, /device:TPU:0, one launch (start us, length us, event | category | flops | bytes accessed | tf_op | source)
XLA Modules:
  0.0 1243.6 jit_solution(13873038670721492341)
XLA Ops:
  10.8 13.6 %all_gather.33 = bf16[2,2048]{1,0:T(2,128)(2,1)S(1)} all-gather(bf16[2,512]{1,0:T(2,128)(2,1)S(1)} %pad_maximum_fusion.9), channel_id=1, replica_groups=mesh['shard'=4,'seq'=8] {'shard'}, dimensions={1}, use_global_device_ids=true | all-gather | bytes 10240 | tf_op jit(solution)/shard_map/all_gather | solution.py:185
  40.6 35.8 %all-gather.14.cloned.1.call-done = bf16[2048,768]{1,0:T(8,128)(2,1)} async-done(((bf16[512,768]{1,0:T(8,128)(2,1)}), bf16[2048,768]{1,0:T(8,128)(2,1)}) %all-gather.14.cloned.1.call-update) | async-done | bytes 3145744 | tf_op jit(solution)/shard_map/all_gather | solution.py:192
  76.4 46.7 %all-gather.12.cloned.1.call-done = bf16[1536,2048]{1,0:T(8,128)(2,1)} async-done(((bf16[192,2048]{1,0:T(8,128)(2,1)}), bf16[1536,2048]{1,0:T(8,128)(2,1)}) %all-gather.12.cloned.1.call-update) | async-done | bytes 6291472 | tf_op jit(solution)/shard_map/all_gather | solution.py:191
  132.7 37.3 %while.28 = (s32[]{:T(128)}, bf16[3,512,4,64]{1,3,2,0:T(8,128)(2,1)S(1)}, f32[3,4,512,1]{2,1,3,0:T(4,128)S(1)}, s32[3]{0:T(128)S(1)}, bf16[3,512,4,64]{1,3,2,0:T...) while((s32[]{:T(128)}, ...), condition=%wide.region_4.5_spmd.clone, body=%wide.region_1.4_spmd.clone.sunk | while | flops 843971072 | bytes 43061388 | solution.py:98
  178.0 61.0 %reduce-scatter.13.cloned.1.call-done = bf16[192,2048]{1,0:T(8,128)(2,1)} async-done(((bf16[1536,2048]{1,0:T(8,128)(2,1)}), bf16[192,2048]{1,0:T(8,128)(2,1)}) %reduce-scatter.13.cloned.1.call-update) | async-done | bytes 786448 | tf_op jit(solution)/shard_map/reduce_scatter | solution.py:158
  245.1 76.2 %all-gather.22.cloned.1.call-done = bf16[2048,1024]{1,0:T(8,128)(2,1)} async-done(((bf16[512,1024]{1,0:T(8,128)(2,1)}), bf16[2048,1024]{1,0:T(8,128)(2,1)}) %all-gather.22.cloned.1.call-update) | async-done | bytes 4194320 | tf_op jit(solution)/shard_map/all_gather | solution.py:197
  321.3 46.6 %all-gather.18.cloned.1.call-done = bf16[1536,2048]{1,0:T(8,128)(2,1)} async-done(((bf16[192,2048]{1,0:T(8,128)(2,1)}), bf16[1536,2048]{1,0:T(8,128)(2,1)}) %all-gather.18.cloned.1.call-update) | async-done | bytes 6291472 | tf_op jit(solution)/shard_map/all_gather | solution.py:211
  379.6 70.7 %all-gather.20.cloned.1.call-done = bf16[2048,1024]{1,0:T(8,128)(2,1)} async-done(((bf16[512,1024]{1,0:T(8,128)(2,1)}), bf16[2048,1024]{1,0:T(8,128)(2,1)}) %all-gather.20.cloned.1.call-update) | async-done | bytes 4194320 | tf_op jit(solution)/shard_map/all_gather | solution.py:196
  461.9 69.3 %all-gather.24.cloned.1.call-done = bf16[1024,2048]{1,0:T(8,128)(2,1)} async-done(((bf16[1024,512]{1,0:T(8,128)(2,1)}), bf16[1024,2048]{1,0:T(8,128)(2,1)}) %all-gather.24.cloned.1.call-update) | async-done | bytes 4194320 | tf_op jit(solution)/shard_map/all_gather | solution.py:198
  531.3 46.1 %all-gather.28.cloned.1.call-done = bf16[1,1536,2048]{2,1,0:T(8,128)(2,1)} async-done(((bf16[1,192,2048]{2,1,0:T(8,128)(2,1)}), bf16[1,1536,2048]{2,1,0:T(8,128)(2,1)}) %all-gather.28.cloned.1.call-update) | async-done | bytes 6291472 | tf_op jit(solution)/shard_map/all_gather | solution.py:199
  577.4 18.2 %multiply_convert_fusion.1 = (bf16[1536,1024]{1,0:T(8,128)(2,1)}, bf16[1536,1024]{1,0:T(8,128)(2,1)}, bf16[1536,1024]{1,0:T(8,128)(2,1)}) fusion(f32[1536,1024]{1,0:T(8,128)} %fusion.77, f32[1536,1024]{1,0:T(8,128)} %fusion.78, bf16[1024,2048]{1,0:T(8,128)(2,1)} %all-gather.24.cloned.1.call-done, bf16[1,1536,2048]{2,1,0:T(8,128)(2,1)} %all-gather.28.cloned.1.call-done), kind=kOutput, calls=%fused_computation.57 | convolution fusion | flops 6466043904 | bytes 32505856 | tf_op jit(solution)/shard_map/dot_general | solution.py:27
  595.6 12.2 fusion.79
  607.8 12.4 add_convert_fusion
  620.2 61.8 %reduce-scatter.17.cloned.1.call-done = bf16[192,2048]{1,0:T(8,128)(2,1)} async-done(((bf16[1536,2048]{1,0:T(8,128)(2,1)}), bf16[192,2048]{1,0:T(8,128)(2,1)}) %reduce-scatter.17.cloned.1.call-update) | async-done | bytes 786448 | tf_op jit(solution)/shard_map/reduce_scatter | solution.py:158
  710.0 12.0 convolution_convert_fusion.4
  745.4 73.8 %while.29 = (s32[]{:T(128)}, f32[1536,4,64]{0,2,1:T(8,128)S(1)}, f32[1536,4,64]{0,2,1:T(8,128)}, bf16[3,512,4,64]{1,3,2,0:T(8,128)(2,1)}, bf16[3,512,4,64]{1,3,2...) while((s32[]{:T(128)}, f32[1536,4,64]{0,2,1:T(8,128)S(1)}, ...), condition=%wide.region_12.13_spmd.clone, body=%wide.region_10.12_spmd.clone.sunk | while | flops 2044459520 | bytes 128233816 | solution.py:145
  864.4 27.0 %reduce-scatter.27.cloned.1.call-done = bf16[512,1024]{1,0:T(8,128)(2,1)} async-done(((bf16[2048,1024]{1,0:T(8,128)(2,1)}), bf16[512,1024]{1,0:T(8,128)(2,1)}) %reduce-scatter.27.cloned.1.call-update) | async-done | bytes 1048592 | tf_op jit(solution)/shard_map/reduce_scatter | solution.py:251
  894.2 76.6 %reduce-scatter.25.cloned.1.call-done = bf16[512,1024]{1,0:T(8,128)(2,1)} async-done(((bf16[2048,1024]{1,0:T(8,128)(2,1)}), bf16[512,1024]{1,0:T(8,128)(2,1)}) %reduce-scatter.25.cloned.1.call-update) | async-done | bytes 1048592 | tf_op jit(solution)/shard_map/reduce_scatter | solution.py:251
  973.6 27.2 %reduce-scatter.23.cloned.1.call-done = bf16[256,512]{1,0:T(8,128)(2,1)} async-done(((bf16[256,2048]{1,0:T(8,128)(2,1)}), bf16[256,512]{1,0:T(8,128)(2,1)}) %reduce-scatter.23.cloned.1.call-update) | async-done | bytes 262160 | tf_op jit(solution)/shard_map/reduce_scatter | solution.py:251
  1002.6 59.2 %reduce-scatter.21.cloned.1.call-done = bf16[512,768]{1,0:T(8,128)(2,1)} async-done(((bf16[2048,768]{1,0:T(8,128)(2,1)}), bf16[512,768]{1,0:T(8,128)(2,1)}) %reduce-scatter.21.cloned.1.call-update) | async-done | bytes 786448 | tf_op jit(solution)/shard_map/reduce_scatter | solution.py:251
  1064.2 62.7 %reduce-scatter.19.cloned.1.call-done = bf16[192,2048]{1,0:T(8,128)(2,1)} async-done(((bf16[1536,2048]{1,0:T(8,128)(2,1)}), bf16[192,2048]{1,0:T(8,128)(2,1)}) %reduce-scatter.19.cloned.1.call-update) | async-done | bytes 786448 | tf_op jit(solution)/shard_map/reduce_scatter | solution.py:158
  1129.9 62.3 %reduce-scatter.15.cloned.1.call-done = bf16[192,2048]{1,0:T(8,128)(2,1)} async-done(((bf16[1536,2048]{1,0:T(8,128)(2,1)}), bf16[192,2048]{1,0:T(8,128)(2,1)}) %reduce-scatter.15.cloned.1.call-update) | async-done | bytes 786448 | tf_op jit(solution)/shard_map/reduce_scatter | solution.py:158
  1196.1 25.6 %reduce-scatter.31.cloned.1.call-done = f32[512,2]{1,0:T(8,128)} async-done(((f32[2048,2]{1,0:T(8,128)}), f32[512,2]{1,0:T(8,128)}) %reduce-scatter.31.cloned.1.call-update) | async-done | bytes 4112
  1222.8 13.4 %psum.8 = f32[2,512]{1,0:T(2,128)S(1)} all-reduce(f32[2,512]{1,0:T(2,128)S(1)} %copy.41), channel_id=1, replica_groups=mesh['shard'=4,'seq'=8] {'seq'}, use_global_device_ids=true, to_apply=%region_17.18 | all-reduce | flops 1024 | bytes 8192 | tf_op jit(solution)/shard_map/psum | solution.py:248
  (263 shorter events, 287.1 us)
Async XLA Ops:
  7.2 69.2 %all-gather.14.cloned.1.call-start = ((), (), s32[]{:S(2)}) async-start(), calls=%async_computation.11 | async-start | bytes 3932160 | tf_op jit(solution)/shard_map/all_gather | solution.py:192
  9.4 113.7 %all-gather.12.cloned.1.call-start = ((), (), s32[]{:S(2)}) async-start(), calls=%async_computation.10 | async-start | bytes 7077888 | tf_op jit(solution)/shard_map/all_gather | solution.py:191
  28.7 142.4 %all-gather.16.cloned.1.call-start = ((), (), s32[]{:S(2)}) async-start(), calls=%async_computation.12 | async-start | bytes 1310720 | tf_op jit(solution)/shard_map/all_gather | solution.py:195
  29.4 209.6 %reduce-scatter.13.cloned.1.call-start = ((), (), s32[]{:S(2)}) async-start(), calls=%async_computation.13 | async-start | bytes 7077888 | tf_op jit(solution)/shard_map/reduce_scatter | solution.py:158
  177.1 144.2 %all-gather.22.cloned.1.call-start = ((), (), s32[]{:S(2)}) async-start(), calls=%async_computation.16 | async-start | bytes 5242880 | tf_op jit(solution)/shard_map/all_gather | solution.py:197
  177.7 190.2 %all-gather.18.cloned.1.call-start = ((), (), s32[]{:S(2)}) async-start(), calls=%async_computation.14 | async-start | bytes 7077888 | tf_op jit(solution)/shard_map/all_gather | solution.py:211
  240.5 443.9 %copy-start.28 = (f32[192]{0:T(256)}, f32[192]{0:T(256)S(1)}, u32[]{:S(2)}) copy-start(f32[192]{0:T(256)S(1)} %get-tuple-element.294) | copy-start | bytes 2308
  240.5 443.9 %copy-start.32 = (f32[192]{0:T(256)}, f32[192]{0:T(256)S(1)}, u32[]{:S(2)}) copy-start(f32[192]{0:T(256)S(1)} %get-tuple-element.293) | copy-start | bytes 2308
  242.8 207.4 %all-gather.20.cloned.1.call-start = ((), (), s32[]{:S(2)}) async-start(), calls=%async_computation.15 | async-start | bytes 5242880 | tf_op jit(solution)/shard_map/all_gather | solution.py:196
  243.6 287.7 %all-gather.24.cloned.1.call-start = ((), (), s32[]{:S(2)}) async-start(), calls=%async_computation.17 | async-start | bytes 5242880 | tf_op jit(solution)/shard_map/all_gather | solution.py:198
  244.3 333.1 %all-gather.28.cloned.1.call-start = ((), (), s32[]{:S(2)}) async-start(), calls=%async_computation.27 | async-start | bytes 7077888 | tf_op jit(solution)/shard_map/all_gather | solution.py:199
  245.1 437.0 %reduce-scatter.17.cloned.1.call-start = ((), (), s32[]{:S(2)}) async-start(), calls=%async_computation.19 | async-start | bytes 7077888 | tf_op jit(solution)/shard_map/reduce_scatter | solution.py:158
  620.2 112.5 %all-gather.26.cloned.1.call-start = ((), (), s32[]{:S(2)}) async-start(), calls=%async_computation.20 | async-start | bytes 7077888 | tf_op jit(solution)/shard_map/all_gather | solution.py:233
  687.1 174.5 %reduce-scatter.29.cloned.1.call-start = ((), (), s32[]{:S(2)}) async-start(), calls=%async_computation.26 | async-start | bytes 5242880 | tf_op jit(solution)/shard_map/reduce_scatter | solution.py:251
  698.4 193.0 %reduce-scatter.27.cloned.1.call-start = ((), (), s32[]{:S(2)}) async-start(), calls=%async_computation.25 | async-start | bytes 5242880 | tf_op jit(solution)/shard_map/reduce_scatter | solution.py:251
  710.0 260.9 %reduce-scatter.25.cloned.1.call-start = ((), (), s32[]{:S(2)}) async-start(), calls=%async_computation.24 | async-start | bytes 5242880 | tf_op jit(solution)/shard_map/reduce_scatter | solution.py:251
  722.0 278.7 %reduce-scatter.23.cloned.1.call-start = ((), (), s32[]{:S(2)}) async-start(), calls=%async_computation.23 | async-start | bytes 1310720 | tf_op jit(solution)/shard_map/reduce_scatter | solution.py:251
  827.2 234.7 %reduce-scatter.21.cloned.1.call-start = ((), (), s32[]{:S(2)}) async-start(), calls=%async_computation.22 | async-start | bytes 3932160 | tf_op jit(solution)/shard_map/reduce_scatter | solution.py:251
  841.2 285.7 %reduce-scatter.19.cloned.1.call-start = ((), (), s32[]{:S(2)}) async-start(), calls=%async_computation.21 | async-start | bytes 7077888 | tf_op jit(solution)/shard_map/reduce_scatter | solution.py:158
  850.3 342.0 %reduce-scatter.15.cloned.1.call-start = ((), (), s32[]{:S(2)}) async-start(), calls=%async_computation.18 | async-start | bytes 7077888 | tf_op jit(solution)/shard_map/reduce_scatter | solution.py:158
  861.5 360.2 %reduce-scatter.31.cloned.1.call-start = ((), (), s32[]{:S(2)}) async-start(), calls=%async_computation.28 | async-start | bytes 1310720
  894.2 232.7 %copy-start.5 = (bf16[1,192,2048]{2,1,0:T(8,128)(2,1)S(1)}, bf16[1,192,2048]{2,1,0:T(8,128)(2,1)}, u32[]{:S(2)}) copy-start(bf16[1,192,2048]{2,1,0:T(8,128)(2,1)} %param.16) | copy-start | bytes 2359300
  894.2 232.7 %copy-start.26 = (f32[1,2048]{1,0:T(1,128)S(1)}, f32[1,2048]{1,0:T(1,128)}, u32[]{:S(2)}) copy-start(f32[1,2048]{1,0:T(1,128)} %copy-done.25) | copy-start | bytes 24580
  894.2 232.7 %copy-start.31 = (f32[192]{0:T(256)S(1)}, f32[192]{0:T(256)}, u32[]{:S(2)}) copy-start(f32[192]{0:T(256)} %copy-done.30) | copy-start | bytes 2308
  (47 other events, 2253.8 us)
Sparse Core Ops, SparseCore 0:
  10.2 66.1 all-gather.13
  78.9 44.1 all-gather.11
  124.7 27.9 all-gather.15
  177.2 61.7 reduce-scatter.12
  240.5 80.7 all-gather.21
  323.8 44.0 all-gather.17
  369.5 80.7 all-gather.19
  451.9 79.2 all-gather.23
  533.3 44.0 all-gather.27
  620.3 61.7 reduce-scatter.16
  687.2 45.4 all-gather.25
  734.9 76.7 reduce-scatter.28
  814.1 77.2 reduce-scatter.26
  893.5 77.2 reduce-scatter.24
  973.1 27.6 reduce-scatter.22
  1002.9 58.8 reduce-scatter.20
  1065.1 61.7 reduce-scatter.18
  1130.5 61.7 reduce-scatter.14
  1194.6 27.1 reduce-scatter.30

commit v2 on v1

v2 whole, which is shorter than its diff:
```python
import math

import jax
import jax.numpy as jnp
from jax import lax
from jax.experimental import pallas as pl
from jax.experimental.pallas import tpu as pltpu
from jax.sharding import PartitionSpec as P

HD = 64
epsilon = 1e-05
theta_base = 130000.0
bf16 = jnp.bfloat16
f32 = jnp.float32
VMEM = pltpu.VMEM
DMA = pltpu.SemaphoreType.DMA


def dot_nn(a, b):
    return jnp.dot(a, b, preferred_element_type=f32)


def dot_nt(a, b):
    return lax.dot_general(a, b, (((1,), (1,)), ((), ())), preferred_element_type=f32)


def in_vmem():
    return pl.BlockSpec(memory_space=VMEM)


def in_any():
    return pl.BlockSpec(memory_space=pl.ANY)


def kernel_params(collective_id=None, limit=60):
    if collective_id is None:
        return pltpu.CompilerParams(vmem_limit_bytes=limit << 20)
    return pltpu.CompilerParams(
        collective_id=collective_id, has_side_effects=True, vmem_limit_bytes=limit << 20
    )


def popcount(mask):
    return bin(mask).count("1")


def chip_masks(size):
    return sorted(range(0, size, 2), key=lambda m: (popcount(m), m))


def chip_bits(size):
    return [1 << b for b in range(1, size.bit_length() - 1)]


def last_hop(mask, core):
    set_bits = [1 << b for b in range(1, mask.bit_length()) if mask >> b & 1]
    return set_bits[-1] if core == 0 else set_bits[0]


def seq_neighbours(size):
    return [1] + chip_bits(size)


def entry_barrier(seq_size=0, shard_size=0):
    barrier = pltpu.get_barrier_semaphore()
    count = 0
    if seq_size:
        me = lax.axis_index("seq")
        for mask in seq_neighbours(seq_size):
            pl.semaphore_signal(
                barrier, inc=1, device_id={"seq": jnp.bitwise_xor(me, mask)},
                device_id_type=pl.DeviceIdType.MESH,
            )
            count += 1
    if shard_size:
        mine = lax.axis_index("shard")
        for step in range(1, shard_size):
            pl.semaphore_signal(
                barrier, inc=1, device_id={"shard": lax.rem(mine + step, shard_size)},
                device_id_type=pl.DeviceIdType.MESH,
            )
            count += 1
    pl.semaphore_wait(barrier, count)


class SeqGather:
    def __init__(self, size, all_ref, send_sem, recv_sem, own=None):
        self.size, self.all_ref = size, all_ref
        self.send_sem, self.recv_sem = send_sem, recv_sem
        self.me = lax.axis_index("seq")
        self.core = lax.rem(self.me, 2)
        self.own = own

    def copy(self, arrives, hop):
        block = jnp.bitwise_xor(self.me, arrives ^ hop)
        src = self.all_ref.at[block]
        if arrives == hop and self.own is not None:
            src = self.own
        return pltpu.make_async_remote_copy(
            src_ref=src,
            dst_ref=self.all_ref.at[block],
            send_sem=self.send_sem.at[arrives],
            recv_sem=self.recv_sem.at[arrives],
            device_id={"seq": jnp.bitwise_xor(self.me, hop)},
            device_id_type=pl.DeviceIdType.MESH,
        )

    def wait_recv(self, mask):
        block = self.all_ref.at[jnp.bitwise_xor(self.me, mask)]
        pltpu.make_async_remote_copy(
            src_ref=block,
            dst_ref=block,
            send_sem=self.send_sem.at[mask],
            recv_sem=self.recv_sem.at[mask],
            device_id={"seq": jnp.bitwise_xor(self.me, 1)},
            device_id_type=pl.DeviceIdType.MESH,
        ).wait_recv()

    def start(self):
        for hop in reversed(seq_neighbours(self.size)):
            self.copy(hop, hop).start()

    def forward(self, mask):
        self.wait_recv(mask)
        for core in (0, 1):
            for hop in chip_bits(self.size):
                if not mask & hop and last_hop(mask | hop, core) == hop:

                    @pl.when(self.core == core)
                    def _():
                        self.copy(mask | hop, hop).start()

        self.copy(mask | 1, 1).start()

    def finish(self):
        for mask in chip_masks(self.size):
            self.wait_recv(mask | 1)
        for mask in range(1, self.size):
            self.copy(mask, 1 if mask & 1 else mask & -mask).wait_send()

    def run(self):
        self.start()
        for mask in chip_masks(self.size)[1:]:
            self.forward(mask)
        self.finish()


class SeqScatter:
    def __init__(self, size, terms, arrived, send_sem, recv_sem):
        self.size, self.terms, self.arrived = size, terms, arrived
        self.send_sem, self.recv_sem = send_sem, recv_sem
        self.me = lax.axis_index("seq")
        self.core = lax.rem(self.me, 2)
        self.order = chip_masks(size)[::-1]

    def copy(self, mask, hop):
        if mask & 1:
            src = self.terms.at[mask // 2, 1 - self.core]
        else:
            src = self.terms.at[mask // 2, self.core]
        return pltpu.make_async_remote_copy(
            src_ref=src,
            dst_ref=self.arrived.at[mask],
            send_sem=self.send_sem.at[mask],
            recv_sem=self.recv_sem.at[mask],
            device_id={"seq": jnp.bitwise_xor(self.me, hop)},
            device_id_type=pl.DeviceIdType.MESH,
        )

    def chip(self, mask):
        return jnp.bitwise_xor(self.me, mask) // 2

    def send_sibling(self, mask):
        self.copy(mask | 1, 1).start()

    def add(self, mask, source, write):
        rows = self.terms.shape[2]
        step = 32 if rows % 32 == 0 else 16

        @pl.loop(0, rows // step)
        def _(i):
            part = pl.ds(pl.multiple_of(i * step, step), step)
            total = self.terms[mask // 2, self.core, part, :].astype(f32)
            for s in source:
                total = total + self.arrived[s, part, :].astype(f32)
            write(part, total)

    def merge(self, mask, result=None):
        def keep(part, total):
            if mask:
                self.terms[mask // 2, self.core, part, :] = total.astype(bf16)
            else:
                result[part, :] = total

        self.copy(mask | 1, 1).wait_recv()
        for core in (0, 1):
            further = [
                mask | hop
                for hop in chip_bits(self.size)
                if not mask & hop and last_hop(mask | hop, core) == hop
            ]

            @pl.when(self.core == core)
            def _():
                for m in further:
                    self.copy(m, 1).wait_recv()
                self.add(mask, [mask | 1] + further, keep)
                if mask:
                    self.copy(mask, last_hop(mask, core)).start()

    def finish(self):
        for mask in range(1, self.size):
            self.copy(mask, 1).wait_send()


class LineGather:
    def __init__(self, size, own, out, send_sem, recv_sem, copy_sem):
        self.size, self.own, self.out = size, own, out
        self.send_sem, self.recv_sem, self.copy_sem = send_sem, recv_sem, copy_sem
        self.k = lax.axis_index("shard")

    def sent(self, way, step):
        block = self.k - step if way == 0 else self.k + step
        valid = (
            jnp.logical_and(self.k < self.size - 1, block >= 0)
            if way == 0
            else jnp.logical_and(self.k > 0, block <= self.size - 1)
        )
        safe = jnp.clip(block, 0, self.size - 1)
        target = jnp.clip(self.k + 1 if way == 0 else self.k - 1, 0, self.size - 1)
        src = self.own if step == 0 else self.out.at[safe]
        return valid, pltpu.make_async_remote_copy(
            src_ref=src,
            dst_ref=self.out.at[safe],
            send_sem=self.send_sem.at[way, step],
            recv_sem=self.recv_sem.at[way, step],
            device_id={"shard": target},
            device_id_type=pl.DeviceIdType.MESH,
        )

    def received(self, way, step):
        block = self.k - 1 - step if way == 0 else self.k + 1 + step
        valid = block >= 0 if way == 0 else block <= self.size - 1
        safe = jnp.clip(block, 0, self.size - 1)
        return valid, pltpu.make_async_remote_copy(
            src_ref=self.own,
            dst_ref=self.out.at[safe],
            send_sem=self.send_sem.at[way, step],
            recv_sem=self.recv_sem.at[way, step],
            device_id={"shard": lax.rem(self.k + 1, self.size)},
            device_id_type=pl.DeviceIdType.MESH,
        )

    def local(self):
        return pltpu.make_async_copy(self.own, self.out.at[self.k], self.copy_sem)

    def step(self, step):
        if step == 0:
            self.local().start()
        for way in (0, 1):
            if step > 0:
                valid, copy = self.received(way, step - 1)

                @pl.when(valid)
                def _():
                    copy.wait_recv()

            if step < self.size - 1:
                valid, copy = self.sent(way, step)

                @pl.when(valid)
                def _():
                    copy.start()

    def finish(self):
        self.local().wait()
        for step in range(self.size - 1):
            for way in (0, 1):
                valid, copy = self.sent(way, step)

                @pl.when(valid)
                def _():
                    copy.wait_send()


def inverse_rms(values):
    return lax.rsqrt(jnp.mean(values * values, axis=-1, keepdims=True) + epsilon)


def group_a(seq_size, shard_size, x, gains, table, cot, wq, wk, wv):
    rows, width = x.shape
    part, cols = wq.shape

    def kernel(
        x_ref, gains_ref, table_ref, cot_ref, wq_ref, wk_ref, wv_ref,
        normed_ref, table_all, cot_all, gains_all, wq_all, wk_all, wv_all,
        ns, nr, ts, tr, cs, cr, gs, gr, ws, wr, wc, cc,
    ):
        me = lax.axis_index("seq")
        mine = lax.axis_index("shard")
        entry_barrier(seq_size, shard_size)

        def gain_copy(step):
            return pltpu.make_async_remote_copy(
                src_ref=gains_ref,
                dst_ref=gains_all.at[mine],
                send_sem=gs.at[step],
                recv_sem=gr.at[step],
                device_id={"shard": lax.rem(mine + step, shard_size)},
                device_id_type=pl.DeviceIdType.MESH,
            )

        def gain_arrival(step):
            return pltpu.make_async_remote_copy(
                src_ref=gains_ref,
                dst_ref=gains_all.at[lax.rem(mine + shard_size - step, shard_size)],
                send_sem=gs.at[step],
                recv_sem=gr.at[step],
                device_id={"shard": lax.rem(mine + step, shard_size)},
                device_id_type=pl.DeviceIdType.MESH,
            )

        for step in range(1, shard_size):
            gain_copy(step).start()
        lines = [
            LineGather(shard_size, own, out, ws.at[i], wr.at[i], wc.at[i])
            for i, (own, out) in enumerate(
                ((wq_ref, wq_all), (wk_ref, wk_all), (wv_ref, wv_all))
            )
        ]
        for line in lines:
            line.step(0)
        gains_all[mine] = gains_ref[...]
        table_all[me] = table_ref[...]
        own_cot = pltpu.make_async_copy(cot_ref, cot_all.at[me], cc)
        own_cot.start()
        tables = SeqGather(seq_size, table_all, ts, tr)
        normed = SeqGather(seq_size, normed_ref, ns, nr)
        cots = SeqGather(seq_size, cot_all, cs, cr, own=cot_ref)
        tables.start()
        for step in range(1, shard_size):
            gain_arrival(step).wait_recv()
        values = x_ref[...].astype(f32)
        scaled = values * inverse_rms(values)
        for z in range(shard_size):
            lanes = slice(z * part, (z + 1) * part)
            normed_ref[me, :, lanes] = (scaled[:, lanes] * gains_all[z, 0:1, :]).astype(bf16)
        normed.start()
        cots.start()
        masks = chip_masks(seq_size)[1:]
        for line in lines:
            line.step(1)
        for mask in masks:
            tables.forward(mask)
        for mask in masks:
            normed.forward(mask)
        for step in range(2, shard_size):
            for line in lines:
                line.step(step)
            if step == 2:
                for mask in masks:
                    cots.forward(mask)
        for step in range(1, shard_size):
            gain_copy(step).wait_send()
        tables.finish()
        normed.finish()
        own_cot.wait()
        cots.finish()
        for line in lines:
            line.finish()

    weight = jax.ShapeDtypeStruct((shard_size, part, cols), bf16)
    return pl.pallas_call(
        kernel,
        name="gather_tokens",
        out_shape=[
            jax.ShapeDtypeStruct((seq_size, rows, width), bf16),
            jax.ShapeDtypeStruct((seq_size, rows, table.shape[1]), f32),
            jax.ShapeDtypeStruct((seq_size, rows, width), bf16),
            jax.ShapeDtypeStruct((shard_size,) + gains.shape, f32),
            weight,
            weight,
            weight,
        ],
        in_specs=[in_vmem()] * 7,
        out_specs=[in_vmem(), in_vmem(), in_any(), in_vmem(), in_vmem(), in_vmem(), in_vmem()],
        scratch_shapes=[DMA((seq_size,))] * 6
        + [DMA((shard_size,))] * 2
        + [DMA((3, 2, shard_size - 1))] * 2
        + [DMA((3,)), DMA],
        compiler_params=kernel_params(1),
    )(x, gains, table, cot, wq, wk, wv)


def head_lanes(head, shape):
    lane = lax.broadcasted_iota(jnp.int32, shape, 1)
    return lane < HD if head == 0 else lane >= HD


def turn(values, table, back):
    count = values.shape[1] // HD
    cosine = jnp.concatenate([table[:, :HD]] * count, axis=1)
    sine = jnp.concatenate([table[:, HD:]] * count, axis=1)
    lane = lax.broadcasted_iota(jnp.int32, values.shape, 1)
    half = HD // 2
    width = values.shape[1]
    partner = jnp.where(
        lane % HD < half,
        pltpu.roll(values, width - half, 1),
        pltpu.roll(values, half, 1),
    )
    if back:
        return values * cosine - partner * sine
    return values * cosine + partner * sine


def attend(normed, table, wq, wk, wv):
    length, width = normed.shape
    cols = wq.shape[1]
    rows = 512 if length % 512 == 0 else length
    block = 256 if length % 256 == 0 else length
    scale = 1.0 / math.sqrt(HD)
    pair = 2 * HD

    def kernel(n_ref, t_ref, wq_ref, wk_ref, wv_ref, q_ref, k_ref, v_ref, o_ref, lse_ref):
        @pl.loop(0, length // rows)
        def _(i):
            part = pl.ds(pl.multiple_of(i * rows, rows), rows)
            tokens = n_ref[part, :]
            tab = t_ref[part, :]
            q = turn(dot_nn(tokens, wq_ref[...]), tab, False).astype(bf16)
            q_ref[part, :] = q * jnp.asarray(scale, bf16)
            k_ref[part, :] = turn(dot_nn(tokens, wk_ref[...]), tab, False).astype(bf16)
            v_ref[part, :] = dot_nn(tokens, wv_ref[...]).astype(bf16)

        @pl.loop(0, cols // pair)
        def _(hp):
            lanes = pl.ds(pl.multiple_of(hp * pair, pair), pair)
            for i in range(length // block):
                first, last = i * block, (i + 1) * block
                q2 = q_ref[first:last, lanes]
                out = None
                for head in (0, 1):
                    keep = head_lanes(head, q2.shape)
                    qm = jnp.where(keep, q2, jnp.zeros_like(q2))
                    s = dot_nt(qm, k_ref[:last, lanes])
                    r = lax.broadcasted_iota(jnp.int32, (block, block), 0)
                    c = lax.broadcasted_iota(jnp.int32, (block, block), 1)
                    tail = jnp.where(c <= r, s[:, first:], -1e30)
                    s = tail if i == 0 else jnp.concatenate([s[:, :first], tail], axis=1)
                    m = jnp.max(s, axis=1, keepdims=True)
                    p = jnp.exp(s - m)
                    total = jnp.sum(p, axis=1, keepdims=True)
                    low = (p * (1.0 / total)).astype(bf16)
                    o = dot_nn(low, v_ref[:last, lanes])
                    out = o if head == 0 else jnp.where(keep, o, out)
                    lse = jnp.transpose(jnp.broadcast_to(m + jnp.log(total), (block, 128)))
                    lse_ref[pl.ds(hp * 2 + head, 1), first:last] = lse[0:1, :]
                o_ref[first:last, lanes] = out.astype(bf16)

    head_array = jax.ShapeDtypeStruct((length, cols), bf16)
    return pl.pallas_call(
        kernel,
        name="attend",
        out_shape=[head_array] * 4
        + [jax.ShapeDtypeStruct((max(8, cols // HD), length), f32)],
        in_specs=[in_vmem()] * 5,
        out_specs=[in_vmem()] * 5,
        compiler_params=kernel_params(),
        cost_estimate=pl.CostEstimate(
            flops=6 * length * width * cols + 2 * length * length * cols,
            bytes_accessed=2 * length * width,
            transcendentals=length * length * cols // HD // 2,
        ),
    )(normed, table, wq, wk, wv)


def attend_back(d_attn, wo, mixed, q, k, v, lse, table, normed, wq, wk, wv):
    length, width = d_attn.shape
    cols = q.shape[1]
    shards, _, part = wo.shape
    rows = 512 if length % 512 == 0 else length
    block = 256 if length % 256 == 0 else length
    scale = 1.0 / math.sqrt(HD)
    pair = 2 * HD

    def kernel(
        da_ref, wo_ref, mixed_ref, q_ref, k_ref, v_ref, lse_ref, t_ref, n_ref,
        dq_ref, dk_ref, dv_ref, gq_ref, gk_ref, gv_ref, go_ref,
        do_ref, kt_ref, dk_acc, dv_acc, xt_ref,
    ):
        @pl.loop(0, length // rows)
        def _(i):
            r = pl.ds(pl.multiple_of(i * rows, rows), rows)
            total = dot_nt(da_ref[r, :part], wo_ref[0])
            for z in range(1, shards):
                total += dot_nt(da_ref[r, z * part : (z + 1) * part], wo_ref[z])
            do_ref[r, :] = total.astype(bf16)

        kt_ref[...] = jnp.transpose(k_ref[...])

        @pl.loop(0, cols // pair)
        def _(hp):
            lanes = pl.ds(pl.multiple_of(hp * pair, pair), pair)
            dk_acc[...] = jnp.zeros_like(dk_acc)
            dv_acc[...] = jnp.zeros_like(dv_acc)
            for i in range(length // block):
                first, last = i * block, (i + 1) * block
                q2 = q_ref[first:last, lanes]
                do2 = do_ref[first:last, lanes]
                keys = k_ref[:last, lanes]
                values = v_ref[:last, lanes]
                dqt = None
                dk_add, dv_add = None, None
                for head in (0, 1):
                    keep = head_lanes(head, q2.shape)
                    qm = jnp.where(keep, q2, jnp.zeros_like(q2))
                    dom = jnp.where(keep, do2, jnp.zeros_like(do2))
                    st = dot_nt(keys, qm)
                    row = lse_ref[pl.ds(hp * 2 + head, 1), first:last]
                    p = jnp.exp(st - row)
                    r = lax.broadcasted_iota(jnp.int32, (block, block), 0)
                    c = lax.broadcasted_iota(jnp.int32, (block, block), 1)
                    tail = jnp.where(r <= c, p[first:], 0.0)
                    p = tail if i == 0 else jnp.concatenate([p[:first], tail], axis=0)
                    dp = dot_nt(values, dom)
                    inner = jnp.sum(dp * p, axis=0, keepdims=True)
                    ds = (p * (dp - inner)).astype(bf16)
                    dv_one = dot_nn(p.astype(bf16), dom)
                    dk_one = dot_nn(ds, qm)
                    dv_add = dv_one if head == 0 else dv_add + dv_one
                    dk_add = dk_one if head == 0 else dk_add + dk_one
                    dqt_one = dot_nn(kt_ref[lanes, :last], ds)
                    if head == 0:
                        dqt = dqt_one
                    else:
                        sub = lax.broadcasted_iota(jnp.int32, dqt.shape, 0)
                        dqt = jnp.where(sub < HD, dqt, dqt_one)
                dk_acc[:last, :] += dk_add
                dv_acc[:last, :] += dv_add
                dq = (jnp.transpose(dqt) * scale).astype(bf16).astype(f32)
                dq_ref[first:last, lanes] = turn(dq, t_ref[first:last, :], True).astype(bf16)
            dv_ref[:, lanes] = dv_acc[...].astype(bf16)

            @pl.loop(0, length // rows)
            def _(i):
                r = pl.ds(pl.multiple_of(i * rows, rows), rows)
                dk = dk_acc[r, :].astype(bf16).astype(f32)
                dk_ref[r, lanes] = turn(dk, t_ref[r, :], True).astype(bf16)

        for source, out in ((dq_ref, gq_ref), (dk_ref, gk_ref), (dv_ref, gv_ref)):
            xt_ref[...] = jnp.transpose(source[...])
            for z in range(shards):
                out[z] = dot_nn(xt_ref[...], n_ref[:, z * part : (z + 1) * part]).astype(bf16)
        xt_ref[...] = jnp.transpose(mixed_ref[...])
        for z in range(shards):
            go_ref[z] = dot_nn(xt_ref[...], da_ref[:, z * part : (z + 1) * part]).astype(bf16)

    head_array = jax.ShapeDtypeStruct((length, cols), bf16)
    grad = jax.ShapeDtypeStruct((shards, cols, part), bf16)
    return pl.pallas_call(
        kernel,
        name="attend_back",
        out_shape=[head_array] * 3 + [grad] * 4,
        in_specs=[in_vmem()] * 9,
        out_specs=[in_vmem()] * 7,
        scratch_shapes=[
            VMEM((length, cols), bf16),
            VMEM((cols, length), bf16),
            VMEM((length, pair), f32),
            VMEM((length, pair), f32),
            VMEM((cols, length), bf16),
        ],
        compiler_params=kernel_params(),
        cost_estimate=pl.CostEstimate(
            flops=10 * length * width * cols + 5 * length * length * cols,
            bytes_accessed=4 * length * width,
            transcendentals=length * length * cols // HD // 2,
        ),
    )(d_attn, wo, mixed, q, k, v, lse, table, normed)


def merge_attention(seq_size, shard_size, mixed, wo, x, gains_all):
    rows, width = x.shape
    cols = mixed.shape[1]
    part = wo.shape[2]
    chips = seq_size // 2

    def kernel(
        mixed_ref, wo_ref, x_ref, gains_ref, hidden_ref, normed_all,
        terms, arrived, normed_ref, ss, sr, ns, nr, own_sem,
    ):
        me = lax.axis_index("seq")
        entry_barrier(seq_size)
        scatter = SeqScatter(seq_size, terms, arrived, ss, sr)

        def compute(mask):
            start = pl.multiple_of(scatter.chip(mask) * (2 * rows), 2 * rows)
            tokens = mixed_ref[pl.ds(start, 2 * rows), :]
            for z in range(shard_size):
                terms[mask // 2, :, :, z * part : (z + 1) * part] = (
                    dot_nn(tokens, wo_ref[z]).astype(bf16).reshape(2, rows, part)
                )

        for mask in scatter.order:
            compute(mask)
            scatter.send_sibling(mask)
        for mask in scatter.order:
            scatter.merge(mask, hidden_ref)
        hidden = hidden_ref[...] + x_ref[...].astype(f32)
        hidden_ref[...] = hidden
        scaled = hidden * inverse_rms(hidden)
        for z in range(shard_size):
            lanes = slice(z * part, (z + 1) * part)
            normed_ref[:, lanes] = (scaled[:, lanes] * gains_ref[z, 1:2, :]).astype(bf16)
        gather = SeqGather(seq_size, normed_all, ns, nr, own=normed_ref)
        gather.start()
        own = pltpu.make_async_copy(normed_ref, normed_all.at[me], own_sem)
        own.start()
        for mask in chip_masks(seq_size)[1:]:
            gather.forward(mask)
        own.wait()
        gather.finish()
        scatter.finish()

    return pl.pallas_call(
        kernel,
        name="merge_attention",
        out_shape=[
            jax.ShapeDtypeStruct((rows, width), f32),
            jax.ShapeDtypeStruct((seq_size, rows, width), bf16),
        ],
        in_specs=[in_vmem()] * 4,
        out_specs=[in_vmem(), in_any()],
        scratch_shapes=[
            VMEM((chips, 2, rows, width), bf16),
            VMEM((seq_size, rows, width), bf16),
            VMEM((rows, width), bf16),
        ]
        + [DMA((seq_size,))] * 4
        + [DMA],
        compiler_params=kernel_params(2),
    )(mixed, wo, x, gains_all)


def mlp_chunk(normed, cot, wg, wu, wd):
    length, width = normed.shape
    hidden = wg.shape[1]
    shards, _, part = wd.shape
    rows = 512 if length % 512 == 0 else length
    block = 256 if hidden % 256 == 0 else hidden

    def kernel(
        n_ref, c_ref, wg_ref, wu_ref, wd_ref,
        a_ref, dg_ref, du_ref, gg_ref, gu_ref, gd_ref, xt_ref,
    ):
        for f in range(hidden // block):
            lanes = slice(f * block, (f + 1) * block)

            @pl.loop(0, length // rows)
            def _(i):
                r = pl.ds(pl.multiple_of(i * rows, rows), rows)
                tokens = n_ref[r, :]
                gate = dot_nn(tokens, wg_ref[:, lanes])
                up = dot_nn(tokens, wu_ref[:, lanes])
                d_act = dot_nt(c_ref[r, :part], wd_ref[0, lanes, :])
                for z in range(1, shards):
                    d_act += dot_nt(c_ref[r, z * part : (z + 1) * part], wd_ref[z, lanes, :])
                sig = jax.nn.sigmoid(gate)
                silu = gate * sig
                a_ref[r, lanes] = (silu * up).astype(bf16)
                dg_ref[r, lanes] = (d_act * up * (sig * (1.0 + gate * (1.0 - sig)))).astype(bf16)
                du_ref[r, lanes] = (d_act * silu).astype(bf16)

            for left, right, out in (
                (dg_ref, n_ref, gg_ref),
                (du_ref, n_ref, gu_ref),
                (a_ref, c_ref, gd_ref),
            ):
                xt_ref[...] = jnp.transpose(left[:, lanes])
                for z in range(shards):
                    out[z, lanes, :] = dot_nn(
                        xt_ref[...], right[:, z * part : (z + 1) * part]
                    ).astype(bf16)

    act = jax.ShapeDtypeStruct((length, hidden), bf16)
    grad = jax.ShapeDtypeStruct((shards, hidden, part), bf16)
    return pl.pallas_call(
        kernel,
        name="mlp_chunk",
        out_shape=[act] * 3 + [grad] * 3,
        in_specs=[in_vmem()] * 5,
        out_specs=[in_vmem()] * 6,
        scratch_shapes=[VMEM((block, length), bf16)],
        compiler_params=kernel_params(),
        cost_estimate=pl.CostEstimate(
            flops=12 * length * width * hidden,
            bytes_accessed=4 * length * width,
            transcendentals=length * hidden,
        ),
    )(normed, cot, wg, wu, wd)


def norm_back(values, inverse, gain, d_normed):
    scaled = d_normed * gain
    d_values = inverse * scaled - values * (inverse * inverse * inverse) * jnp.mean(
        scaled * values, axis=-1, keepdims=True
    )
    return d_values, jnp.sum(d_normed * values * inverse, axis=0, keepdims=True)


def mlp_back(seq_size, shard_size, d_gate, d_up, wg, wu, hidden, cot, gains_all):
    rows, width = hidden.shape
    units = wg.shape[1]
    part = width // shard_size
    chips = seq_size // 2

    def kernel(
        dg_ref, du_ref, wg_ref, wu_ref, hidden_ref, cot_ref, gains_ref,
        d_hidden_ref, d_gain_ref, d_attn_all,
        terms, arrived, d_attn_ref, ss, sr, ns, nr, own_sem,
    ):
        me = lax.axis_index("seq")
        entry_barrier(seq_size)
        scatter = SeqScatter(seq_size, terms, arrived, ss, sr)

        def compute(mask):
            start = pl.multiple_of(scatter.chip(mask) * (2 * rows), 2 * rows)
            dg = dg_ref[pl.ds(start, 2 * rows), :]
            du = du_ref[pl.ds(start, 2 * rows), :]
            for z in range(shard_size):
                lanes = slice(z * part, (z + 1) * part)
                total = dot_nt(dg, wg_ref[lanes, :]) + dot_nt(du, wu_ref[lanes, :])
                terms[mask // 2, :, :, lanes] = total.astype(bf16).reshape(2, rows, part)

        previous = None
        for mask in scatter.order:
            compute(mask)
            scatter.send_sibling(mask)
            if previous is not None:
                scatter.merge(previous)
            previous = mask
        scatter.merge(previous, d_hidden_ref)
        values = hidden_ref[...]
        gain = jnp.concatenate([gains_ref[z, 1:2, :] for z in range(shard_size)], axis=1)
        d_values, d_gain = norm_back(values, inverse_rms(values), gain, d_hidden_ref[...])
        d_hidden = cot_ref[...].astype(f32) + d_values
        d_attn_ref[...] = d_hidden.astype(bf16)
        gather = SeqGather(seq_size, d_attn_all, ns, nr, own=d_attn_ref)
        gather.start()
        own = pltpu.make_async_copy(d_attn_ref, d_attn_all.at[me], own_sem)
        own.start()
        d_hidden_ref[...] = d_hidden
        d_gain_ref[...] = d_gain
        for mask in chip_masks(seq_size)[1:]:
            gather.forward(mask)
        own.wait()
        gather.finish()
        scatter.finish()

    return pl.pallas_call(
        kernel,
        name="mlp_back",
        out_shape=[
            jax.ShapeDtypeStruct((rows, width), f32),
            jax.ShapeDtypeStruct((1, width), f32),
            jax.ShapeDtypeStruct((seq_size, rows, width), bf16),
        ],
        in_specs=[in_vmem()] * 7,
        out_specs=[in_vmem(), in_vmem(), in_any()],
        scratch_shapes=[
            VMEM((chips, 2, rows, width), bf16),
            VMEM((seq_size, rows, width), bf16),
            VMEM((rows, width), bf16),
        ]
        + [DMA((seq_size,))] * 4
        + [DMA],
        compiler_params=kernel_params(3),
    )(d_gate, d_up, wg, wu, hidden, cot, gains_all)


def mlp_out(seq_size, shard_size, activ, wd, hidden):
    rows, width = hidden.shape
    part = width // shard_size
    chips = seq_size // 2

    def kernel(a_ref, wd_ref, hidden_ref, out_ref, terms, arrived, total_ref, ss, sr):
        entry_barrier(seq_size)
        scatter = SeqScatter(seq_size, terms, arrived, ss, sr)
        previous = None
        for mask in scatter.order:
            start = pl.multiple_of(scatter.chip(mask) * (2 * rows), 2 * rows)
            tokens = a_ref[pl.ds(start, 2 * rows), :]
            for z in range(shard_size):
                terms[mask // 2, :, :, z * part : (z + 1) * part] = (
                    dot_nn(tokens, wd_ref[z]).astype(bf16).reshape(2, rows, part)
                )
            scatter.send_sibling(mask)
            if previous is not None:
                scatter.merge(previous)
            previous = mask
        scatter.merge(previous, total_ref)
        out_ref[...] = (total_ref[...] + hidden_ref[...]).astype(bf16)
        scatter.finish()

    return pl.pallas_call(
        kernel,
        name="mlp_out",
        out_shape=jax.ShapeDtypeStruct((rows, width), bf16),
        in_specs=[in_vmem()] * 3,
        out_specs=in_vmem(),
        scratch_shapes=[
            VMEM((chips, 2, rows, width), bf16),
            VMEM((seq_size, rows, width), bf16),
            VMEM((rows, width), f32),
        ]
        + [DMA((seq_size,))] * 2,
        compiler_params=kernel_params(4),
    )(activ, wd, hidden)


def inputs_back(seq_size, shard_size, dq, dk, dv, wq, wk, wv, x, d_hidden, gains_all, d_gain_two):
    rows, width = x.shape
    part = width // shard_size
    chips = seq_size // 2

    def kernel(
        dq_ref, dk_ref, dv_ref, wq_ref, wk_ref, wv_ref, x_ref, d_hidden_ref, gains_ref, gain2_ref,
        out_ref, gain_ref,
        terms, arrived, total_ref, mine_ref, from_shard, line_ref, from_seq,
        ss, sr, gs, gr, hs, hr,
    ):
        me = lax.axis_index("seq")
        mine = lax.axis_index("shard")
        barrier = pltpu.get_barrier_semaphore()
        for step in range(1, seq_size):
            pl.semaphore_signal(
                barrier, inc=1, device_id={"seq": jnp.bitwise_xor(me, step)},
                device_id_type=pl.DeviceIdType.MESH,
            )
        for step in range(1, shard_size):
            pl.semaphore_signal(
                barrier, inc=1, device_id={"shard": lax.rem(mine + step, shard_size)},
                device_id_type=pl.DeviceIdType.MESH,
            )
        pl.semaphore_wait(barrier, seq_size + shard_size - 2)
        scatter = SeqScatter(seq_size, terms, arrived, ss, sr)

        previous = None
        for mask in scatter.order:
            start = pl.multiple_of(scatter.chip(mask) * (2 * rows), 2 * rows)
            pair = pl.ds(start, 2 * rows)
            for z in range(shard_size):
                lanes = slice(z * part, (z + 1) * part)
                total = (
                    dot_nt(dq_ref[pair, :], wq_ref[z])
                    + dot_nt(dk_ref[pair, :], wk_ref[z])
                    + dot_nt(dv_ref[pair, :], wv_ref[z])
                )
                terms[mask // 2, :, :, lanes] = total.astype(bf16).reshape(2, rows, part)
            scatter.send_sibling(mask)
            if previous is not None:
                scatter.merge(previous)
            previous = mask
        scatter.merge(previous, total_ref)
        values = x_ref[...].astype(f32)
        gain = jnp.concatenate([gains_ref[z, 0:1, :] for z in range(shard_size)], axis=1)
        d_values, d_gain = norm_back(values, inverse_rms(values), gain, total_ref[...])
        out_ref[...] = (d_hidden_ref[...] + d_values).astype(bf16)
        for z in range(shard_size):
            lanes = slice(z * part, (z + 1) * part)
            mine_ref[z, 0:1, :] = d_gain[:, lanes]
            mine_ref[z, 1:2, :] = gain2_ref[0:1, lanes]
            mine_ref[z, 2:, :] = jnp.zeros((6, part), f32)

        def to_shard(step):
            return pltpu.make_async_remote_copy(
                src_ref=mine_ref.at[lax.rem(mine + step, shard_size)],
                dst_ref=from_shard.at[step],
                send_sem=gs.at[step],
                recv_sem=gr.at[step],
                device_id={"shard": lax.rem(mine + step, shard_size)},
                device_id_type=pl.DeviceIdType.MESH,
            )

        for step in range(1, shard_size):
            to_shard(step).start()
        for step in range(1, shard_size):
            to_shard(step).wait()
        line_ref[...] = mine_ref[mine] + sum(from_shard[step] for step in range(1, shard_size))

        def to_seq(step):
            return pltpu.make_async_remote_copy(
                src_ref=line_ref,
                dst_ref=from_seq.at[step],
                send_sem=hs.at[step],
                recv_sem=hr.at[step],
                device_id={"seq": jnp.bitwise_xor(me, step)},
                device_id_type=pl.DeviceIdType.MESH,
            )

        for step in range(1, seq_size):
            to_seq(step).start()
        for step in range(1, seq_size):
            to_seq(step).wait()
        gain_ref[...] = line_ref[...] + sum(from_seq[step] for step in range(1, seq_size))
        scatter.finish()

    return pl.pallas_call(
        kernel,
        name="inputs_back",
        out_shape=[
            jax.ShapeDtypeStruct((rows, width), bf16),
            jax.ShapeDtypeStruct((8, part), f32),
        ],
        in_specs=[in_vmem()] * 10,
        out_specs=[in_vmem()] * 2,
        scratch_shapes=[
            VMEM((chips, 2, rows, width), bf16),
            VMEM((seq_size, rows, width), bf16),
            VMEM((rows, width), f32),
            VMEM((shard_size, 8, part), f32),
            VMEM((shard_size, 8, part), f32),
            VMEM((8, part), f32),
            VMEM((seq_size, 8, part), f32),
        ]
        + [DMA((seq_size,))] * 2
        + [DMA((shard_size,))] * 2
        + [DMA((seq_size,))] * 2,
        compiler_params=kernel_params(5),
    )(dq, dk, dv, wq, wk, wv, x, d_hidden, gains_all, d_gain_two)


def rotation_table(position_ids):
    half = HD // 2
    freqs = theta_base ** (-(jnp.arange(half, dtype=f32) * 2.0) / HD)
    angles = position_ids.astype(f32)[:, None] * freqs[None, :]
    cosine, sine = jnp.cos(angles), jnp.sin(angles)
    return jnp.concatenate([cosine, cosine, -sine, sine], axis=1)


def shard_gather(block):
    return lax.all_gather(block, "shard", axis=0, tiled=False)


def shard_sum(terms):
    return lax.psum_scatter(terms, "shard", scatter_dimension=0, tiled=False).astype(f32)


def body(
    inputs,
    positions,
    attn_gain,
    w_query,
    w_key,
    w_value,
    w_output,
    mlp_gain,
    w_gate,
    w_up,
    w_down,
    cotangent,
):
    seq_size, shard_size = lax.axis_size("seq"), lax.axis_size("shard")
    x, cot = inputs[0], cotangent[0]
    rows, width = x.shape
    length = rows * seq_size
    gains = jnp.pad(jnp.stack([attn_gain, mlp_gain]).astype(f32), ((0, 6), (0, 0)))
    table = rotation_table(positions[0])
    wo = shard_gather(w_output)
    wg = shard_gather(w_gate).reshape(width, -1)
    wu = shard_gather(w_up).reshape(width, -1)
    wd = shard_gather(w_down)
    normed_one, tables, cot_all, gains_all, wq, wk, wv = group_a(
        seq_size, shard_size, x, gains, table, cot, w_query, w_key, w_value
    )
    normed_one = normed_one.reshape(length, width)
    tables = tables.reshape(length, -1)
    cot_all = cot_all.reshape(length, width)
    q, k, v, mixed, lse = attend(
        normed_one, tables, wq.reshape(width, -1), wk.reshape(width, -1), wv.reshape(width, -1)
    )
    hidden, normed_two = merge_attention(seq_size, shard_size, mixed, wo, x, gains_all)
    normed_two = normed_two.reshape(length, width)
    activ, d_gate, d_up, g_gate, g_up, g_down = mlp_chunk(normed_two, cot_all, wg, wu, wd)
    d_hidden, d_gain_two, d_attn = mlp_back(
        seq_size, shard_size, d_gate, d_up, wg, wu, hidden, cot, gains_all
    )
    d_attn = d_attn.reshape(length, width)
    output = mlp_out(seq_size, shard_size, activ, wd, hidden)
    dq, dk, dv, g_query, g_key, g_value, g_output = attend_back(
        d_attn, wo, mixed, q, k, v, lse, tables, normed_one, wq, wk, wv
    )
    d_inputs, gain_sums = inputs_back(
        seq_size, shard_size, dq, dk, dv, wq, wk, wv, x, d_hidden, gains_all, d_gain_two
    )
    return (
        output[None],
        d_inputs[None],
        gain_sums[0],
        shard_sum(g_query).T,
        shard_sum(g_key).T,
        shard_sum(g_value).T,
        shard_sum(g_output),
        gain_sums[1],
        shard_sum(g_gate).T,
        shard_sum(g_up).T,
        shard_sum(g_down),
    )


def solution(mesh):
    in_specs = (
        P("shard", "seq", None),
        P("shard", "seq"),
        P("shard"),
        P("shard", "seq"),
        P("shard", "seq"),
        P("shard", "seq"),
        P("seq", "shard"),
        P("shard"),
        P("shard", "seq"),
        P("shard", "seq"),
        P("seq", "shard"),
        P("shard", "seq", None),
    )
    out_specs = (
        P("shard", "seq", None),
        P("shard", "seq", None),
        P("shard"),
        P("shard", "seq"),
        P("shard", "seq"),
        P("shard", "seq"),
        P("seq", "shard"),
        P("shard"),
        P("shard", "seq"),
        P("shard", "seq"),
        P("seq", "shard"),
    )
    return jax.shard_map(body, mesh=mesh, in_specs=in_specs, out_specs=out_specs, check_vma=False)
```

time: 1250 us -> 860 us (0.69)
  waiting for transfers between devices: 869 us -> 316 us
  Pallas kernels: 0 us -> 503 us
  matrix products: 227 us -> 0 us
  other arithmetic: 68.5 us -> 12.5 us
  blocking collectives: 35.1 us -> 0 us
  local copies, waits for them, and re-layouts: 22.5 us -> 9.79 us
    pallas_call x0 -> x8, Pallas kernels: none -> 503 us  [the longest x1 137 us: group_a(): pl.pallas_call(kernel, name='gather_tokens', out_shape=[jax.ShapeDtypeStr...]
    all_gather x9 -> x4, waiting for transfers between devices: 402 us -> 72.6 us  [shard_gather(): return lax.all_gather(block, 'shard', axis=0, tiled=False)]
    dot_general x36 -> x0, matrix products: 227 us -> none  [the longest x5 57.3 us: product_right_t(): lax.dot_general(left, right, (((1,), (1,)), ((), ())), preferred_element_...]
    reduce_scatter x9 -> x7, waiting for transfers between devices: 438 us -> 237 us  [shard_sum(): lax.psum_scatter(terms, 'shard', scatter_dimension=0, tiled=False)]
    convert_element_type x13 -> x3, other arithmetic: 34.8 us -> 4.64 us  [the longest x2 4.64 us: shard_sum(): lax.psum_scatter(terms, 'shard', scatter_dimension=0, tiled=False)]
    unnamed x20 -> x11, waiting for transfers between devices: 29.2 us -> 6.41 us
    reduce_sum x7 -> x0, other arithmetic: 17.4 us -> none  [the longest x3 10.6 us: one_block(): totals = jnp.sum(expo, axis=-1, keepdims=True)]
    all_gather x1 -> x0, blocking collectives: 13.6 us -> none  [body(): lax.all_gather(jnp.stack([attn_gain, mlp_gain]), 'shard', axis=1, tiled=T...]
  transfers between devices with their start and end apart: 19 -> 11, of which waited for: 17 -> 5; matrix products, arithmetic and copies ran while one was open for 21% -> 2% of each run, Pallas kernels for 0% -> 38%
where the time goes in v2:
time: 860 us; the launch traced here: 856 us
  Pallas kernels  503 us (58%)
  waiting for transfers between devices  316 us (37%)
  between operations  14.3 us (2%)
  other arithmetic  12.5 us (1%)
  local copies, waits for them, and re-layouts  9.79 us (1%)
    reduce_scatter x7, waiting for transfers between devices, shard_sum(): lax.psum_scatter(terms, 'shard', scatter_dimension=0, tiled=False)  237 us
    pallas_call x1, Pallas kernels, group_a(): pl.pallas_call(kernel, name='gather_tokens', out_shape=[jax.ShapeDtypeStr...  137 us
    pallas_call x1, Pallas kernels, mlp_back(): pl.pallas_call(kernel, name='mlp_back', out_shape=[jax.ShapeDtypeStruct((...  77.9 us
    all_gather x4, waiting for transfers between devices, shard_gather(): return lax.all_gather(block, 'shard', axis=0, tiled=False)  72.6 us
    pallas_call x1, Pallas kernels, merge_attention(): pl.pallas_call(kernel, name='merge_attention', out_shape=[jax.ShapeDtypeS...  70.6 us
    pallas_call x1, Pallas kernels, mlp_chunk(): pl.pallas_call(kernel, name='mlp_chunk', out_shape=[act] * 3 + [grad] * 3...  65.1 us
    pallas_call x1, Pallas kernels, inputs_back(): pl.pallas_call(kernel, name='inputs_back', out_shape=[jax.ShapeDtypeStruc...  50.7 us
    pallas_call x1, Pallas kernels, mlp_out(): pl.pallas_call(kernel, name='mlp_out', out_shape=jax.ShapeDtypeStruct((ro...  39.8 us
  transfers between devices with their start and end apart: 11, of which 5 were waited for; matrix products, arithmetic and copies ran while one was open for 2% of the time, Pallas kernels for 38%

profile of v2, /device:TPU:0, one launch (start us, length us, event | category | flops | bytes accessed | tf_op | source)
XLA Modules:
  0.0 856.0 jit_solution(2178137381035770768)
XLA Ops:
  12.0 137.2 %gather_tokens.1 = (bf16[8,192,2048]{2,1,0:T(8,128)(2,1)}, f32[8,192,128]{2,1,0:T(8,128)}, bf16[8,192,2048]{2,1,0:T(8,128)(2,1)}, f32[4,8,512]{2,1,0:T(8,128)}, ...) custom-call(bf16[192,2048]{1,0:T(8,128)(2,1)} %bitcast.48, ...), custom_call_target="tpu_custom_call" | custom-call | tf_op jit(solution)/shard_map/gather_tokens/pallas_call | solution.py:373
  149.2 25.7 %attend.1 = (bf16[1536,256]{1,0:T(8,128)(2,1)}, bf16[1536,256]{1,0:T(8,128)(2,1)}, bf16[1536,256]{1,0:T(8,128)(2,1)}, bf16[1536,256]{1,0:T(8,128)(2,1)}, f32[8,1536]{1,0:T(8,128)}) custom-call(bf16[1536,2048]{1,0:T(8,128)(2,1)} %bitcast.65, f32[1536,128]{1,0:T(8,128)} %bitcast.70, bf16[2048,256]{1,0:T(8,128)(2,1)} %bitcast.56, bf16[2048,256]{1,0:T(8,128)(2,1)} %bitcast.57, ...), custom_call_target="tpu_custom_call" | custom-call | flops 6039797760 | bytes 6291456 | tf_op jit(solution)/shard_map/attend/pallas_call | solution.py:462
  174.9 70.6 %merge_attention.1 = (f32[192,2048]{1,0:T(8,128)}, bf16[8,192,2048]{2,1,0:T(8,128)(2,1)}) custom-call(bf16[1536,256]{1,0:T(8,128)(2,1)} %get-tuple-element.48.mixed_ref, bf16[4,256,512]{2,1,0:T(8,128)(2,1)} %bitcast.59, bf16[192,2048]{1,0:T(8,128)(2,1)} %bitcast.49, f32[4,8,512]{2,1,0:T(8,128)} %get-tuple-element.49.gains_ref), custom_call_target="tpu_custom_call" | custom-call | tf_op jit(solution)/shard_map/merge_attention/pallas_call | solution.py:626
  245.6 72.6 %all-gather.15.cloned.1.call-done = bf16[4096,512]{1,0:T(8,128)(2,1)} async-done(((bf16[1024,512]{1,0:T(8,128)(2,1)}), bf16[4096,512]{1,0:T(8,128)(2,1)}) %all-gather.15.cloned.1.call-update) | async-done | bytes 4194320 | tf_op jit(solution)/shard_map/all_gather | solution.py:943
  318.2 65.1 %mlp_chunk.1 = (bf16[1536,1024]{1,0:T(8,128)(2,1)}, bf16[1536,1024]{1,0:T(8,128)(2,1)}, bf16[1536,1024]{1,0:T(8,128)(2,1)}, bf16[4,1024,512]{2,1,0:T(8,128)(2,1)...) custom-call(bf16[1536,2048]{1,0:T(8,128)(2,1)} %bitcast.69, bf16[1536,2048]{1,0:T(8,128)(2,1)} %bitcast.67, ...), custom_call_target="tpu_custom_call" | custom-call | flops 38654705664 | bytes 12582912 | tf_op jit(solution)/shard_map/mlp_chunk/pallas_call | solution.py:688
  383.3 77.9 %mlp_back.1 = (f32[192,2048]{1,0:T(8,128)}, f32[1,2048]{1,0:T(1,128)}, bf16[8,192,2048]{2,1,0:T(8,128)(2,1)}) custom-call(bf16[1536,1024]{1,0:T(8,128)(2,1)} %get-tuple-element.54.dg_ref, bf16[1536,1024]{1,0:T(8,128)(2,1)} %get-tuple-element.55.du_ref, bf16[2048,1024]{1,0:T(8,128)(2,1)} %all-gather.11.cloned.1.call-done.wg_ref, ...), custom_call_target="tpu_custom_call" | custom-call | tf_op jit(solution)/shard_map/mlp_back/pallas_call | solution.py:761
  461.2 36.1 %attend_back.1 = (bf16[1536,256]{1,0:T(8,128)(2,1)}, bf16[1536,256]{1,0:T(8,128)(2,1)}, bf16[1536,256]{1,0:T(8,128)(2,1)}, bf16[4,256,512]{2,1,0:T(8,128)(2,1)},...) custom-call(bf16[1536,2048]{1,0:T(8,128)(2,1)} %bitcast.68, ...), custom_call_target="tpu_custom_call" | custom-call | flops 11072962560 | bytes 12582912 | tf_op jit(solution)/shard_map/attend_back/pallas_call | solution.py:561
  501.5 39.8 %mlp_out.1 = bf16[192,2048]{1,0:T(8,128)(2,1)} custom-call(bf16[1536,1024]{1,0:T(8,128)(2,1)} %get-tuple-element.52.a_ref, bf16[4,1024,512]{2,1,0:T(8,128)(2,1)} %bitcast.52, f32[192,2048]{1,0:T(8,128)} %get-tuple-element.53.hidden_ref), custom_call_target="tpu_custom_call" | custom-call | tf_op jit(solution)/shard_map/mlp_out/pallas_call | solution.py:806
  541.2 50.7 %inputs_back.1 = (bf16[192,2048]{1,0:T(8,128)(2,1)}, f32[8,512]{1,0:T(8,128)}) custom-call(bf16[1536,256]{1,0:T(8,128)(2,1)} %get-tuple-element.61.dq_ref, bf16[1536,256]{1,0:T(8,128)(2,1)} %get-tuple-element.62.dk_ref, bf16[1536,256]{1,0:T(8,128)(2,1)} %get-tuple-element.63.dv_ref, bf16[4,512,256]{2,1,0:T(8,128)(2,1)} %get-tuple-element.45.wq_ref, ...), custom_call_target="tpu_custom_call" | custom-call | tf_op jit(solution)/shard_map/inputs_back/pallas_call | solution.py:909
  591.9 1.4 fusion.5
  593.3 1.0 convert_bitcast_fusion.2
  594.3 1.0 copy.31
  595.3 1.0 convert_bitcast_fusion.3
  597.3 1.0 convert_bitcast_fusion.4
  599.3 8.4 reduce-scatter.14.cloned.1.call-done
  607.8 1.8 bitcast_convert_fusion.1
  609.6 76.0 %reduce-scatter.18.cloned.1.call-done = bf16[1,1024,512]{2,1,0:T(8,128)(2,1)} async-done(((bf16[4,1024,512]{2,1,0:T(8,128)(2,1)}), bf16[1,1024,512]{2,1,0:T(8,128)(2,1)}) %reduce-scatter.18.cloned.1.call-update) | async-done | bytes 1048592 | tf_op jit(solution)/shard_map/reduce_scatter | solution.py:947
  685.5 1.5 convert_bitcast_fusion
  687.0 1.8 copy.33
  688.8 76.2 %reduce-scatter.16.cloned.1.call-done = bf16[1,1024,512]{2,1,0:T(8,128)(2,1)} async-done(((bf16[4,1024,512]{2,1,0:T(8,128)(2,1)}), bf16[1,1024,512]{2,1,0:T(8,128)(2,1)}) %reduce-scatter.16.cloned.1.call-update) | async-done | bytes 1048592 | tf_op jit(solution)/shard_map/reduce_scatter | solution.py:947
  765.1 1.5 convert_bitcast_fusion.1
  766.6 1.8 copy.32
  768.4 76.2 %reduce-scatter.20.cloned.1.call-done = bf16[1,1024,512]{2,1,0:T(8,128)(2,1)} async-done(((bf16[4,1024,512]{2,1,0:T(8,128)(2,1)}), bf16[1,1024,512]{2,1,0:T(8,128)(2,1)}) %reduce-scatter.20.cloned.1.call-update) | async-done | bytes 1048592 | tf_op jit(solution)/shard_map/reduce_scatter | solution.py:947
  844.6 2.8 bitcast_convert_fusion
  (49 shorter events, 12.5 us)
Async XLA Ops:
  7.2 2.9 copy-start.4
  7.2 2.9 copy-start.2
  7.2 2.9 copy-start.3
  7.2 167.7 %all-gather.9.cloned.1.call-start = ((), (), s32[]{:S(2)}) async-start(), calls=%async_computation.14 | async-start | bytes 1310720 | tf_op jit(solution)/shard_map/all_gather | solution.py:943
  7.9 237.6 %all-gather.11.cloned.1.call-start = ((), (), s32[]{:S(2)}) async-start(), calls=%async_computation.15 | async-start | bytes 5242880 | tf_op jit(solution)/shard_map/all_gather | solution.py:943
  8.7 236.9 %all-gather.13.cloned.1.call-start = ((), (), s32[]{:S(2)}) async-start(), calls=%async_computation.16 | async-start | bytes 5242880 | tf_op jit(solution)/shard_map/all_gather | solution.py:943
  9.4 308.8 %all-gather.15.cloned.1.call-start = ((), (), s32[]{:S(2)}) async-start(), calls=%async_computation.17 | async-start | bytes 5242880 | tf_op jit(solution)/shard_map/all_gather | solution.py:943
  10.0 583.3 %reduce-scatter.12.cloned.1.call-start = ((), (), s32[]{:S(2)}) async-start(), calls=%async_computation.9 | async-start | bytes 1310720 | tf_op jit(solution)/shard_map/reduce_scatter | solution.py:947
  497.4 98.0 %reduce-scatter.10.cloned.1.call-start = ((), (), s32[]{:S(2)}) async-start(), calls=%async_computation.8 | async-start | bytes 1310720 | tf_op jit(solution)/shard_map/reduce_scatter | solution.py:947
  497.9 99.4 %reduce-scatter.8.cloned.1.call-start = ((), (), s32[]{:S(2)}) async-start(), calls=%async_computation.7 | async-start | bytes 1310720 | tf_op jit(solution)/shard_map/reduce_scatter | solution.py:947
  498.7 109.1 %reduce-scatter.14.cloned.1.call-start = ((), (), s32[]{:S(2)}) async-start(), calls=%async_computation.10 | async-start | bytes 1310720 | tf_op jit(solution)/shard_map/reduce_scatter | solution.py:947
  499.4 186.1 %reduce-scatter.18.cloned.1.call-start = ((), (), s32[]{:S(2)}) async-start(), calls=%async_computation.12 | async-start | bytes 5242880 | tf_op jit(solution)/shard_map/reduce_scatter | solution.py:947
  500.2 264.9 %reduce-scatter.16.cloned.1.call-start = ((), (), s32[]{:S(2)}) async-start(), calls=%async_computation.11 | async-start | bytes 5242880 | tf_op jit(solution)/shard_map/reduce_scatter | solution.py:947
  500.8 343.9 %reduce-scatter.20.cloned.1.call-start = ((), (), s32[]{:S(2)}) async-start(), calls=%async_computation.13 | async-start | bytes 5242880 | tf_op jit(solution)/shard_map/reduce_scatter | solution.py:947
  766.6 80.9 %copy-start = (bf16[192,2048]{1,0:T(8,128)(2,1)S(1)}, bf16[192,2048]{1,0:T(8,128)(2,1)}, u32[]{:S(2)}) copy-start(bf16[192,2048]{1,0:T(8,128)(2,1)} %mlp_out.1) | copy-start | bytes 2359300
  768.4 80.0 %copy-start.1 = (bf16[192,2048]{1,0:T(8,128)(2,1)S(1)}, bf16[192,2048]{1,0:T(8,128)(2,1)}, u32[]{:S(2)}) copy-start(bf16[192,2048]{1,0:T(8,128)(2,1)} %get-tuple-element.66) | copy-start | bytes 2359300
Sparse Core Ops, SparseCore 0:
  9.6 43.6 all-gather.8
  54.8 100.9 all-gather.10
  157.4 79.9 all-gather.12
  238.8 79.2 all-gather.14
  497.5 24.6 reduce-scatter.11
  525.0 25.7 reduce-scatter.9
  553.7 25.7 reduce-scatter.7
  581.9 25.7 reduce-scatter.13
  610.1 75.4 reduce-scatter.17
  687.8 77.2 reduce-scatter.15
  767.4 77.2 reduce-scatter.19

commit v3 on v1

v3 whole, which is shorter than its diff:
```python
import math

import jax
import jax.numpy as jnp
from jax import lax
from jax.experimental import pallas as pl
from jax.experimental.pallas import tpu as pltpu
from jax.sharding import PartitionSpec as P

HD = 64
epsilon = 1e-05
theta_base = 130000.0
bf16 = jnp.bfloat16
f32 = jnp.float32
VMEM = pltpu.VMEM
DMA = pltpu.SemaphoreType.DMA
MESH = pl.DeviceIdType.MESH


def dot_nn(a, b):
    return jnp.dot(a, b, preferred_element_type=f32)


def dot_nt(a, b):
    return lax.dot_general(a, b, (((1,), (1,)), ((), ())), preferred_element_type=f32)


def in_vmem(count):
    return [pl.BlockSpec(memory_space=VMEM)] * count


def in_any(count):
    return [pl.BlockSpec(memory_space=pl.ANY)] * count


def array(shape, dtype=bf16):
    return jax.ShapeDtypeStruct(shape, dtype)


def kernel_params(collective_id=None, limit=62):
    if collective_id is None:
        return pltpu.CompilerParams(vmem_limit_bytes=limit << 20)
    return pltpu.CompilerParams(
        collective_id=collective_id, has_side_effects=True, vmem_limit_bytes=limit << 20
    )


def popcount(mask):
    return bin(mask).count("1")


def chip_masks(size):
    return sorted(range(0, size, 2), key=lambda m: (popcount(m), m))


def chip_bits(size):
    return [1 << b for b in range(1, size.bit_length() - 1)]


def last_hop(mask, core):
    set_bits = [1 << b for b in range(1, mask.bit_length()) if mask >> b & 1]
    return set_bits[-1] if core == 0 else set_bits[0]


def further_masks(mask, core, size):
    return [
        mask | hop
        for hop in chip_bits(size)
        if not mask & hop and last_hop(mask | hop, core) == hop
    ]


def seq_neighbours(size):
    return [1] + chip_bits(size)


def entry_barrier(seq_masks, shard_size):
    barrier = pltpu.get_barrier_semaphore()
    me, mine = lax.axis_index("seq"), lax.axis_index("shard")
    for mask in seq_masks:
        pl.semaphore_signal(
            barrier, inc=1, device_id={"seq": jnp.bitwise_xor(me, mask)}, device_id_type=MESH
        )
    for step in range(1, shard_size):
        pl.semaphore_signal(
            barrier, inc=1, device_id={"shard": lax.rem(mine + step, shard_size)},
            device_id_type=MESH,
        )
    pl.semaphore_wait(barrier, len(seq_masks) + max(shard_size - 1, 0))


class SeqGather:
    def __init__(self, size, out, rows, send_sem, recv_sem, own=None):
        self.size, self.out, self.rows = size, out, rows
        self.send_sem, self.recv_sem = send_sem, recv_sem
        self.me = lax.axis_index("seq")
        self.core = lax.rem(self.me, 2)
        self.own = own

    def block(self, index):
        return self.out.at[pl.ds(pl.multiple_of(index * self.rows, self.rows), self.rows), :]

    def copy(self, arrives, hop):
        block = self.block(jnp.bitwise_xor(self.me, arrives ^ hop))
        src = self.own if arrives == hop and self.own is not None else block
        return pltpu.make_async_remote_copy(
            src_ref=src,
            dst_ref=block,
            send_sem=self.send_sem.at[arrives],
            recv_sem=self.recv_sem.at[arrives],
            device_id={"seq": jnp.bitwise_xor(self.me, hop)},
            device_id_type=MESH,
        )

    def wait_recv(self, mask):
        block = self.block(jnp.bitwise_xor(self.me, mask))
        pltpu.make_async_remote_copy(
            src_ref=block,
            dst_ref=block,
            send_sem=self.send_sem.at[mask],
            recv_sem=self.recv_sem.at[mask],
            device_id={"seq": jnp.bitwise_xor(self.me, 1)},
            device_id_type=MESH,
        ).wait_recv()

    def start(self):
        for hop in reversed(seq_neighbours(self.size)):
            self.copy(hop, hop).start()

    def forward(self, mask):
        self.wait_recv(mask)
        for core in (0, 1):
            for more in further_masks(mask, core, self.size):

                @pl.when(self.core == core)
                def _():
                    self.copy(more, more ^ mask).start()

        self.copy(mask | 1, 1).start()

    def forwards(self):
        for mask in chip_masks(self.size)[1:]:
            self.forward(mask)

    def finish(self):
        for mask in chip_masks(self.size):
            self.wait_recv(mask | 1)
        for mask in range(1, self.size):
            self.copy(mask, 1 if mask & 1 else mask & -mask).wait_send()


def height(mask, core, size):
    return max([0] + [1 + height(m, core, size) for m in further_masks(mask, core, size)])


class SeqScatter:
    def __init__(self, size, terms, arrived, send_sem, recv_sem):
        self.size, self.terms, self.arrived = size, terms, arrived
        self.send_sem, self.recv_sem = send_sem, recv_sem
        self.me = lax.axis_index("seq")
        self.core = lax.rem(self.me, 2)
        self.masks = chip_masks(size)[::-1]
        self.order = [
            sorted(self.masks, key=lambda m: (height(m, core, size), -popcount(m)))
            for core in (0, 1)
        ]
        self.leaves = size // 4
        self.merged = 0

    def copy(self, mask, hop):
        core = 1 - self.core if mask & 1 else self.core
        return pltpu.make_async_remote_copy(
            src_ref=self.terms.at[mask // 2, core],
            dst_ref=self.arrived.at[mask - 1],
            send_sem=self.send_sem.at[mask],
            recv_sem=self.recv_sem.at[mask],
            device_id={"seq": jnp.bitwise_xor(self.me, hop)},
            device_id_type=MESH,
        )

    def tokens(self, mask, base=0):
        pair = 2 * self.terms.shape[2]
        start = jnp.bitwise_xor(self.me, mask) // 2 * pair + base
        return pl.ds(pl.multiple_of(start, pair), pair)

    def put(self, mask, lanes, total):
        rows = self.terms.shape[2]
        self.terms[mask // 2, :, :, lanes] = total.astype(bf16).reshape(2, rows, -1)

    def add(self, mask, source, write):
        rows = self.terms.shape[2]
        step = 32 if rows % 32 == 0 else 16

        @pl.loop(0, rows // step)
        def _(i):
            part = pl.ds(pl.multiple_of(i * step, step), step)
            total = self.terms[mask // 2, self.core, part, :].astype(f32)
            for s in source:
                total = total + self.arrived[s - 1, part, :].astype(f32)
            write(part, total)

    def merge(self, result=None):
        for core in (0, 1):
            mask = self.order[core][self.merged]
            further = further_masks(mask, core, self.size)

            def keep(part, total, mask=mask):
                if mask:
                    self.terms[mask // 2, self.core, part, :] = total.astype(bf16)
                else:
                    result[part, :] = total.astype(result.dtype)

            @pl.when(self.core == core)
            def _(mask=mask, further=further, keep=keep, core=core):
                for m in [mask | 1] + further:
                    self.copy(m, 1).wait_recv()
                self.add(mask, [mask | 1] + further, keep)
                if mask:
                    self.copy(mask, last_hop(mask, core)).start()

        self.merged += 1

    def send_terms(self, compute, merge=False):
        done = set()
        for mask in self.masks:
            compute(mask)
            self.copy(mask | 1, 1).start()
            if merge and self.merged < self.leaves:
                if all(order[self.merged] in done for order in self.order):
                    self.merge()
            done.add(mask)
        if merge:
            self.merge_leaves()

    def merge_leaves(self):
        while self.merged < self.leaves:
            self.merge()

    def merge_inner(self):
        while self.merged < len(self.masks) - 1:
            self.merge()

    def run(self, compute, result):
        self.send_terms(compute, merge=True)
        self.merge_inner()
        self.merge(result)

    def finish(self):
        for mask in range(1, self.size):
            self.copy(mask, 1).wait_send()


def scatter_scratch(seq_size, rows, width):
    return [
        VMEM((seq_size // 2, 2, rows, width), bf16),
        VMEM((seq_size - 1, rows, width), bf16),
        DMA((seq_size,)),
        DMA((seq_size,)),
    ]


class LineGather:
    def __init__(self, size, own, out, send_sem, recv_sem, copy_sem):
        self.size, self.own, self.out = size, own, out
        self.send_sem, self.recv_sem, self.copy_sem = send_sem, recv_sem, copy_sem
        self.k = lax.axis_index("shard")

    def sent(self, way, step):
        block = self.k - step if way == 0 else self.k + step
        valid = (
            jnp.logical_and(self.k < self.size - 1, block >= 0)
            if way == 0
            else jnp.logical_and(self.k > 0, block <= self.size - 1)
        )
        safe = jnp.clip(block, 0, self.size - 1)
        target = jnp.clip(self.k + 1 if way == 0 else self.k - 1, 0, self.size - 1)
        return valid, pltpu.make_async_remote_copy(
            src_ref=self.own if step == 0 else self.out.at[safe],
            dst_ref=self.out.at[safe],
            send_sem=self.send_sem.at[way, step],
            recv_sem=self.recv_sem.at[way, step],
            device_id={"shard": target},
            device_id_type=MESH,
        )

    def received(self, way, step):
        block = self.k - 1 - step if way == 0 else self.k + 1 + step
        valid = block >= 0 if way == 0 else block <= self.size - 1
        safe = jnp.clip(block, 0, self.size - 1)
        return valid, pltpu.make_async_remote_copy(
            src_ref=self.own,
            dst_ref=self.out.at[safe],
            send_sem=self.send_sem.at[way, step],
            recv_sem=self.recv_sem.at[way, step],
            device_id={"shard": lax.rem(self.k + 1, self.size)},
            device_id_type=MESH,
        )

    def local(self):
        return pltpu.make_async_copy(self.own, self.out.at[self.k], self.copy_sem)

    def step(self, step):
        if step == 0:
            self.local().start()
        if step == self.size - 1:
            self.local().wait()
        for way in (0, 1):
            if step > 0:
                valid, copy = self.received(way, step - 1)

                @pl.when(valid)
                def _():
                    copy.wait_recv()

            if step < self.size - 1:
                valid, copy = self.sent(way, step)

                @pl.when(valid)
                def _():
                    copy.start()

    def finish(self):
        for step in range(self.size - 1):
            for way in (0, 1):
                valid, copy = self.sent(way, step)

                @pl.when(valid)
                def _():
                    copy.wait_send()


class ShardExchange:
    def __init__(self, size, source, out, send_sem, recv_sem):
        self.size, self.source, self.out = size, source, out
        self.send_sem, self.recv_sem = send_sem, recv_sem
        self.k = lax.axis_index("shard")

    def copy(self, step):
        target = lax.rem(self.k + step, self.size)
        return pltpu.make_async_remote_copy(
            src_ref=self.source(target),
            dst_ref=self.out.at[self.k],
            send_sem=self.send_sem.at[step],
            recv_sem=self.recv_sem.at[step],
            device_id={"shard": target},
            device_id_type=MESH,
        )

    def arrival(self, step):
        return pltpu.make_async_remote_copy(
            src_ref=self.out.at[self.k],
            dst_ref=self.out.at[lax.rem(self.k + self.size - step, self.size)],
            send_sem=self.send_sem.at[step],
            recv_sem=self.recv_sem.at[step],
            device_id={"shard": lax.rem(self.k + step, self.size)},
            device_id_type=MESH,
        )

    def local(self):
        return pltpu.make_async_copy(
            self.source(self.k), self.out.at[self.k], self.send_sem.at[0]
        )

    def start(self):
        self.local().start()
        for step in range(1, self.size):
            self.copy(step).start()

    def wait_recv(self):
        self.local().wait()
        for step in range(1, self.size):
            self.arrival(step).wait_recv()

    def wait_send(self):
        for step in range(1, self.size):
            self.copy(step).wait_send()

    def wait(self):
        self.wait_recv()
        self.wait_send()


class PairReduce:
    def __init__(self, size, terms, first, middle_terms, second, sems):
        self.size, self.terms, self.first, self.second = size, terms, first, second
        self.middle_terms = middle_terms
        self.sems = sems
        self.k = lax.axis_index("shard")
        self.pairs = size // 2

    def swap(self, pair):
        target = 2 * pair + 1 - lax.rem(self.k, 2)
        return pltpu.make_async_remote_copy(
            src_ref=self.terms.at[target],
            dst_ref=self.first.at[pair],
            send_sem=self.sems.at[0, pair],
            recv_sem=self.sems.at[1, pair],
            device_id={"shard": jnp.bitwise_xor(self.k, 1)},
            device_id_type=MESH,
        )

    def cross(self, step):
        mine = self.k // 2
        pair = lax.rem(mine + step, self.pairs)
        target = 2 * pair + lax.rem(self.k, 2)
        return pair, target, pltpu.make_async_remote_copy(
            src_ref=self.middle_terms.at[step],
            dst_ref=self.second.at[step],
            send_sem=self.sems.at[2, step],
            recv_sem=self.sems.at[3, step],
            device_id={"shard": target},
            device_id_type=MESH,
        )

    def start(self):
        for pair in range(self.pairs):
            self.swap(pair).start()

    def middle(self):
        for pair in range(self.pairs):
            self.swap(pair).wait_recv()
        for step in range(1, self.pairs):
            pair, target, copy = self.cross(step)
            total = self.terms[target].astype(f32) + self.first[pair].astype(f32)
            self.middle_terms[step] = total.astype(bf16)
            copy.start()

    def total(self):
        for step in range(1, self.pairs):
            self.cross(step)[2].wait_recv()
        total = self.terms[self.k].astype(f32) + self.first[self.k // 2].astype(f32)
        for step in range(1, self.pairs):
            total = total + self.second[step].astype(f32)
        return total

    def finish(self):
        for pair in range(self.pairs):
            self.swap(pair).wait_send()
        for step in range(1, self.pairs):
            self.cross(step)[2].wait_send()


class PairSwap:
    def __init__(self, source, out, sems):
        mine = lax.axis_index("shard")
        self.copy = pltpu.make_async_remote_copy(
            src_ref=source,
            dst_ref=out,
            send_sem=sems.at[0],
            recv_sem=sems.at[1],
            device_id={"shard": jnp.bitwise_xor(mine, 1)},
            device_id_type=MESH,
        )


class Refs:
    def __init__(self, refs):
        self.refs = list(refs)

    def __call__(self, count):
        out, self.refs = self.refs[:count], self.refs[count:]
        return out


def inverse_rms(values):
    return lax.rsqrt(jnp.mean(values * values, axis=-1, keepdims=True) + epsilon)


def norm_back(values, inverse, gain, d_normed):
    scaled = d_normed * gain
    d_values = inverse * scaled - values * (inverse * inverse * inverse) * jnp.mean(
        scaled * values, axis=-1, keepdims=True
    )
    return d_values, jnp.sum(d_normed * values * inverse, axis=0, keepdims=True)


def head_lanes(head, shape):
    lane = lax.broadcasted_iota(jnp.int32, shape, 1)
    return lane < HD if head == 0 else lane >= HD


def turn(values, table, back):
    width = values.shape[1]
    cosine = jnp.concatenate([table[:, :HD]] * (width // HD), axis=1)
    sine = jnp.concatenate([table[:, HD:]] * (width // HD), axis=1)
    lane = lax.broadcasted_iota(jnp.int32, values.shape, 1)
    half = HD // 2
    partner = jnp.where(
        lane % HD < half,
        pltpu.roll(values, width - half, 1),
        pltpu.roll(values, half, 1),
    )
    if back:
        return values * cosine - partner * sine
    return values * cosine + partner * sine


def row_step(length, most):
    return most if length % most == 0 else length


def rows_at(index, step):
    return pl.ds(pl.multiple_of(index * step, step), step)


def weight_pieces(chunks):
    return [(c, kind) for c in range(chunks) for kind in ("gate", "up", "down")]


def piece_shape(kind, shards, part, block):
    return (shards, block, part) if kind == "down" else (shards, part, block)


def piece_source(kind, refs, chunk, block):
    ref = refs[kind]
    half = (ref.shape[0] if kind == "down" else ref.shape[1]) // 2

    def source(j):
        start = pl.multiple_of(lax.rem(j, 2) * half + chunk * block, block)
        if kind == "down":
            return ref.at[pl.ds(start, block), :]
        return ref.at[:, pl.ds(start, block)]

    return source


def split_masks(size):
    masks = chip_masks(size)[1:]
    return [m for m in masks if popcount(m) == 1], [m for m in masks if popcount(m) > 1]


def forward(x, gains, table, cot, attn_weights, mlp_weights, pieces, block):
    seq_size, shard_size = lax.axis_size("seq"), lax.axis_size("shard")
    rows, width = x.shape
    part, cols = attn_weights[0].shape
    length = rows * seq_size
    big = row_step(length, 512)
    query = row_step(length, 256 if length <= 2048 else 128)
    pair = 2 * HD
    scale = 1.0 / math.sqrt(HD)

    def kernel(*refs):
        take = Refs(refs)
        x_ref, gains_ref, table_ref, cot_ref = take(4)
        own_weights = take(4)
        mlp_refs = dict(zip(("gate", "up", "down"), take(3)))
        normed_all, table_all, gains_all = take(3)
        full_weights = take(4)
        q_ref, k_ref, v_ref, o_ref, lse_ref, hidden_ref = take(6)
        cot_all, cot_other, tok_all, tok_other = take(4)
        piece_refs = take(len(pieces))
        terms, arrived, ss, sr = take(4)
        normed_ref = take(1)[0]
        ns, nr, ts, tr, cs, cr, ds, dr, ms, mr = take(10)
        gs, gr, wo_s, wo_r, line_s, line_r, line_c, piece_s, piece_r, local_sem, swap_sem = take(11)

        me, mine = lax.axis_index("seq"), lax.axis_index("shard")
        entry_barrier(seq_neighbours(seq_size), shard_size)
        gain = ShardExchange(shard_size, lambda j: gains_ref, gains_all, gs, gr)
        gain.start()
        lines = [
            LineGather(shard_size, own, out, line_s.at[i], line_r.at[i], line_c.at[i])
            for i, (own, out) in enumerate(zip(own_weights[:3], full_weights))
        ]
        wq_all, wk_all, wv_all, wo_all = full_weights
        exchanges = [
            ShardExchange(
                shard_size, piece_source(kind, mlp_refs, c, block), out, piece_s.at[i], piece_r.at[i]
            )
            for i, ((c, kind), out) in enumerate(zip(pieces, piece_refs))
        ]
        mine_rows = rows_at(me, rows)
        own_cot = pltpu.make_async_copy(cot_ref, cot_all.at[mine_rows, :], local_sem.at[0])
        tables = SeqGather(seq_size, table_all, rows, ts, tr)
        normed = SeqGather(seq_size, normed_all, rows, ns, nr)
        cots = SeqGather(seq_size, cot_all, rows, cs, cr, own=cot_ref)
        cots_other = SeqGather(seq_size, cot_other, rows, ds, dr)
        swap_cot = PairSwap(cot_ref, cot_other.at[mine_rows, :], swap_sem.at[0]).copy
        wo_move = ShardExchange(shard_size, lambda j: own_weights[3], wo_all, wo_s, wo_r)
        if SWAP_FIRST:
            swap_cot.start()
        for line in lines:
            line.step(0)
        own_cot.start()
        table_all[mine_rows, :] = table_ref[...]
        tables.start()
        gain.wait_recv()
        values = x_ref[...].astype(f32)
        scaled = values * inverse_rms(values)
        for z in range(shard_size):
            lanes = slice(z * part, (z + 1) * part)
            normed_all[mine_rows, lanes] = (scaled[:, lanes] * gains_all[z, 0:1, :]).astype(bf16)
        normed.start()
        tables.forwards()
        for line in lines:
            line.step(1)
        near, far = split_masks(seq_size)
        for mask in near:
            normed.forward(mask)
        cots.start()
        for step in range(2, shard_size):
            for line in lines:
                line.step(step)
            if step == 2:
                wo_move.start()
                if not SWAP_FIRST:
                    swap_cot.start()
                for exchange in exchanges[:3]:
                    exchange.start()
                for mask in far:
                    normed.forward(mask)
        tables.finish()
        normed.finish()
        for mask in near:
            cots.forward(mask)
        if SWAP_FIRST:
            swap_cot.wait_recv()
            cots_other.start()

        wq, wk, wv = (w.reshape(width, cols) for w in (wq_all, wk_all, wv_all))

        @pl.loop(0, length // big)
        def _(i):
            r = rows_at(i, big)
            tokens = normed_all[r, :]
            tab = table_all[r, :]
            q = turn(dot_nn(tokens, wq[...]), tab, False).astype(bf16)
            q_ref[r, :] = q * jnp.asarray(scale, bf16)
            k_ref[r, :] = turn(dot_nn(tokens, wk[...]), tab, False).astype(bf16)
            v_ref[r, :] = dot_nn(tokens, wv[...]).astype(bf16)

        for mask in far:
            cots.forward(mask)

        @pl.loop(0, cols // pair)
        def _(hp):
            lanes = rows_at(hp, pair)
            for i in range(length // query):
                first, last = i * query, (i + 1) * query
                q2 = q_ref[first:last, lanes]
                out = None
                for head in (0, 1):
                    keep = head_lanes(head, q2.shape)
                    qm = jnp.where(keep, q2, jnp.zeros_like(q2))
                    s = dot_nt(qm, k_ref[:last, lanes])
                    r = lax.broadcasted_iota(jnp.int32, (query, query), 0)
                    c = lax.broadcasted_iota(jnp.int32, (query, query), 1)
                    tail = jnp.where(c <= r, s[:, first:], -1e30)
                    s = tail if i == 0 else jnp.concatenate([s[:, :first], tail], axis=1)
                    m = jnp.max(s, axis=1, keepdims=True)
                    p = jnp.exp(s - m)
                    total = jnp.sum(p, axis=1, keepdims=True)
                    low = (p * (1.0 / total)).astype(bf16)
                    o = dot_nn(low, v_ref[:last, lanes])
                    out = o if head == 0 else jnp.where(keep, o, out)
                    lse = jnp.transpose(jnp.broadcast_to(m + jnp.log(total), (query, 128)))
                    lse_ref[pl.ds(hp * 2 + head, 1), first:last] = lse[0:1, :]
                o_ref[first:last, lanes] = out.astype(bf16)

        for mask in near:
            if SWAP_FIRST:
                cots_other.forward(mask)
        wo_move.wait_recv()
        scatter = SeqScatter(seq_size, terms, arrived, ss, sr)

        def compute(mask):
            tokens = o_ref[scatter.tokens(mask), :]
            for z in range(shard_size):
                scatter.put(mask, slice(z * part, (z + 1) * part), dot_nn(tokens, wo_all[z]))

        scatter.run(compute, hidden_ref)
        for mask in far:
            if SWAP_FIRST:
                cots_other.forward(mask)
        hidden = hidden_ref[...] + x_ref[...].astype(f32)
        hidden_ref[...] = hidden
        scaled = hidden * inverse_rms(hidden)
        for z in range(shard_size):
            lanes = slice(z * part, (z + 1) * part)
            normed_ref[:, lanes] = (scaled[:, lanes] * gains_all[z, 1:2, :]).astype(bf16)
        swap_tok = PairSwap(normed_ref, tok_other, swap_sem.at[1]).copy
        swap_tok.start()
        toks = SeqGather(seq_size, tok_all, rows, ms, mr, own=normed_ref)
        toks.start()
        own_tok = pltpu.make_async_copy(normed_ref, tok_all.at[mine_rows, :], local_sem.at[1])
        own_tok.start()
        for exchange in exchanges[3:]:
            exchange.start()
        for mask in near:
            toks.forward(mask)
        if not SWAP_FIRST:
            swap_cot.wait_recv()
            cots_other.start()
        for mask in far:
            toks.forward(mask)
        if not SWAP_FIRST:
            cots_other.forwards()
        swap_cot.wait_send()
        wo_move.wait_send()
        gain.wait_send()
        scatter.finish()
        own_cot.wait()
        cots.finish()
        for line in lines:
            line.finish()
        swap_tok.wait()
        own_tok.wait()
        toks.finish()
        cots_other.finish()
        for exchange in exchanges:
            exchange.wait()

    weight = array((shard_size, part, cols))
    out_weight = array((shard_size, cols, part))
    heads = array((length, cols))
    tokens = array((length, width))
    shapes = [piece_shape(kind, shard_size, part, block) for _, kind in pieces]
    count = len(pieces)
    outs = pl.pallas_call(
        kernel,
        name="forward_attention",
        out_shape=[
            tokens,
            array((length, table.shape[1]), f32),
            array((shard_size,) + gains.shape, f32),
            weight,
            weight,
            weight,
            out_weight,
            heads,
            heads,
            heads,
            heads,
            array((max(8, cols // HD), length), f32),
            array((rows, width), f32),
            tokens,
            tokens,
            tokens,
            array((rows, width)),
        ]
        + [array(s) for s in shapes],
        in_specs=in_vmem(3) + in_any(1) + in_vmem(4) + in_any(3),
        out_specs=in_vmem(13) + in_any(4 + count),
        scratch_shapes=scatter_scratch(seq_size, rows, width)
        + [VMEM((rows, width), bf16)]
        + [DMA((seq_size,))] * 10
        + [DMA((shard_size,))] * 4
        + [DMA((3, 2, shard_size - 1))] * 2
        + [DMA((3,))]
        + [DMA((count, shard_size))] * 2
        + [DMA((2,)), DMA((2, 2))],
        compiler_params=kernel_params(1),
    )(x, gains, table, cot, *attn_weights, *mlp_weights)
    return outs[:17], list(outs[17:])


def mlp(tok, tok_other, cot, cot_other, pieces_in, mlp_weights, late, chunks, block, sums):
    seq_size, shard_size = lax.axis_size("seq"), lax.axis_size("shard")
    length, width = tok.shape
    rows = tok_other.shape[0]
    part = width // shard_size
    big = row_step(length, 512)
    steps = length // big
    pieces = weight_pieces(chunks)
    early = pieces[: len(pieces_in)]

    def kernel(*refs):
        take = Refs(refs)
        tok_ref, tok_swap = take(2)
        cots = take(2)
        early_refs = take(len(early))
        mlp_refs = dict(zip(("gate", "up", "down"), take(3)))
        act_ref, dg_ref, du_ref = take(3)
        grads = take(len(pieces))
        late_refs = take(len(late))
        sum_refs = take(sums)
        tok2, cot_rows, cot_cols, xt = take(4)
        weights = take(len(pieces))
        ts, tr, late_s, late_r, sum_s, sum_r, row_sem, col_sem, load_sem = take(9)

        me, mine = lax.axis_index("seq"), lax.axis_index("shard")
        entry_barrier(seq_neighbours(seq_size), shard_size)
        late_moves = [
            ShardExchange(
                shard_size, piece_source(kind, mlp_refs, c, block), out, late_s.at[i], late_r.at[i]
            )
            for i, ((c, kind), out) in enumerate(zip(late, late_refs))
        ]
        for move in late_moves:
            move.start()
        other = SeqGather(seq_size, tok2, rows, ts, tr, own=tok_swap)
        other.start()
        tok2[rows_at(me, rows), :] = tok_swap[...]
        everything = dict(zip(early, early_refs)) | dict(zip(late, late_refs))
        loads = [
            pltpu.make_async_copy(everything[p], w, load_sem.at[i])
            for i, (p, w) in enumerate(zip(pieces, weights))
        ]
        for load in loads[: len(early)]:
            load.start()
        held = dict(zip(pieces, weights))

        def row_copy(plane, i, slot):
            return pltpu.make_async_copy(
                cots[plane].at[rows_at(i, big), :], cot_rows.at[slot], row_sem.at[slot]
            )

        def stage(plane, these, base):
            token_ref = (tok_ref, tok2)[plane]

            @pl.loop(0, steps)
            def _(i):
                slot = lax.rem(i + base, 2)

                @pl.when(i + 1 < steps)
                def _():
                    row_copy(plane, i + 1, 1 - slot).start()

                tokens = token_ref[rows_at(i, big), :]
                row_copy(plane, i, slot).wait()
                r = pl.ds(pl.multiple_of(plane * length + i * big, big), big)
                for c in these:
                    gate_w, up_w = held[c, "gate"], held[c, "up"]
                    gate = dot_nn(tokens, gate_w.reshape(width, block)[...])
                    up = dot_nn(tokens, up_w.reshape(width, block)[...])
                    d_act = dot_nt(cot_rows[slot, :, :part], held[c, "down"][0])
                    for z in range(1, shard_size):
                        lanes = slice(z * part, (z + 1) * part)
                        d_act += dot_nt(cot_rows[slot, :, lanes], held[c, "down"][z])
                    sig = jax.nn.sigmoid(gate)
                    silu = gate * sig
                    act_ref[c, r, :] = (silu * up).astype(bf16)
                    slope = sig * (1.0 + gate * (1.0 - sig))
                    dg_ref[c, r, :] = (d_act * up * slope).astype(bf16)
                    du_ref[c, r, :] = (d_act * silu).astype(bf16)

        def col_copy(z, slot):
            lanes = slice(z * part, (z + 1) * part)
            return [
                pltpu.make_async_copy(
                    cots[plane].at[:, lanes],
                    cot_cols.at[slot, pl.ds(plane * length, length), :],
                    col_sem.at[slot, plane],
                )
                for plane in (0, 1)
            ]

        def grad(c):
            for source, where in ((act_ref, 2), (dg_ref, 0), (du_ref, 1)):
                xt[where] = jnp.transpose(source[c])
            for copy in col_copy(0, 0):
                copy.start()
            for z in range(shard_size):
                lanes = slice(z * part, (z + 1) * part)
                if z + 1 < shard_size:
                    for copy in col_copy(z + 1, (z + 1) % 2):
                        copy.start()
                for which in (0, 1):
                    total = dot_nn(xt[which, :, :length], tok_ref[:, lanes])
                    total += dot_nn(xt[which, :, length:], tok2[:, lanes])
                    grads[3 * c + which][z] = total.astype(bf16)
                for copy in col_copy(z, z % 2):
                    copy.wait()
                grads[3 * c + 2][z] = dot_nn(xt[2], cot_cols[z % 2]).astype(bf16)

        sum_moves = [
            ShardExchange(shard_size, lambda j, g=g: g.at[j], out, sum_s.at[i], sum_r.at[i])
            for i, (g, out) in enumerate(zip(grads, sum_refs))
        ]

        row_copy(0, 0, 0).start()
        first_chunks = [c for c in range(chunks) if all((c, k) in early for k in ("gate", "up", "down"))]
        later_chunks = [c for c in range(chunks) if c not in first_chunks]
        for load in loads[: len(early)]:
            load.wait()
        stage(0, first_chunks, 0)
        row_copy(1, 0, 0).start()
        other.forwards()
        other.finish()
        stage(1, first_chunks, 0)
        for c in first_chunks:
            grad(c)
            for move in sum_moves[3 * c : 3 * c + 3]:
                move.start()
        if later_chunks:
            row_copy(0, 0, 0).start()
            for move in late_moves:
                move.wait_recv()
            for load in loads[len(early) :]:
                load.start()
            for load in loads[len(early) :]:
                load.wait()
            stage(0, later_chunks, 0)
            row_copy(1, 0, 0).start()
            stage(1, later_chunks, 0)
            for c in later_chunks:
                grad(c)
                for move in sum_moves[3 * c : 3 * c + 3]:
                    move.start()
        for move in late_moves:
            move.wait_send()
        for move in sum_moves:
            move.wait()

    piece = array((shard_size, block, part))
    act = array((chunks, 2 * length, block))
    late_shapes = [piece_shape(kind, shard_size, part, block) for _, kind in late]
    all_shapes = [piece_shape(kind, shard_size, part, block) for _, kind in pieces]
    outs = pl.pallas_call(
        kernel,
        name="mlp",
        out_shape=[act] * 3
        + [piece] * len(pieces)
        + [array(s) for s in late_shapes]
        + [piece] * sums,
        in_specs=in_vmem(2) + in_any(2 + len(early) + 3),
        out_specs=in_vmem(3 + len(pieces)) + in_any(len(late) + sums),
        scratch_shapes=[
            VMEM((length, width), bf16),
            VMEM((2, big, width), bf16),
            VMEM((2, 2 * length, part), bf16),
            VMEM((3, block, 2 * length), bf16),
        ]
        + [VMEM(s, bf16) for s in all_shapes]
        + [DMA((seq_size,))] * 2
        + [DMA((max(1, len(late)), shard_size))] * 2
        + [DMA((max(1, sums), shard_size))] * 2
        + [DMA((2,)), DMA((2, 2)), DMA((len(pieces),))],
        compiler_params=kernel_params(2),
    )(tok, tok_other, cot, cot_other, *pieces_in, *mlp_weights)
    outs = list(outs)
    first = 3 + len(pieces)
    second = first + len(late)
    return outs[:3], outs[3:first], outs[first:second], outs[second:]


def mlp_back(d_gate, d_up, gate, up, hidden, cot, gains_all, grads):
    seq_size, shard_size = lax.axis_size("seq"), lax.axis_size("shard")
    rows, width = hidden.shape
    chunks = len(gate)
    length = rows * seq_size
    part = width // shard_size
    count = len(grads)
    shared = length > 2048

    def kernel(*refs):
        take = Refs(refs)
        dg_ref, du_ref, hidden_ref, cot_ref, gains_ref = take(5)
        gate_refs, up_refs = take(chunks), take(chunks)
        grad_refs = take(count)
        d_hidden_ref, d_gain_ref, d_attn_all = take(3)
        sum_refs = take(count)
        terms = take(1 if shared else 2)
        arrived = take(2)
        scatter_sems = [take(2), take(2)]
        other_ref, swap_ref, d_attn_ref = take(3)
        ns, nr, swap_sem, own_sem, sum_s, sum_r = take(6)

        me = lax.axis_index("seq")
        entry_barrier(seq_neighbours(seq_size), shard_size)
        moves = [
            ShardExchange(shard_size, lambda j, g=g: g.at[j], out, sum_s.at[i], sum_r.at[i])
            for i, (g, out) in enumerate(zip(grad_refs, sum_refs))
        ]
        for move in moves[:1]:
            move.start()
        swap = PairSwap(other_ref, swap_ref, swap_sem).copy
        scatters = [
            SeqScatter(seq_size, terms[0 if shared else i], arrived[i], *scatter_sems[i])
            for i in range(2)
        ]

        def term(plane):
            scatter = scatters[plane]

            def compute(mask):
                tokens = scatter.tokens(mask, plane * length)
                for z in range(shard_size):
                    total = None
                    for c in range(chunks):
                        both = dot_nt(dg_ref[c, tokens, :], gate_refs[c][z])
                        both += dot_nt(du_ref[c, tokens, :], up_refs[c][z])
                        total = both if total is None else total + both
                    scatter.put(mask, slice(z * part, (z + 1) * part), total)

            return compute

        here, there = scatters
        there.send_terms(term(1), merge=True)
        if shared:
            there.merge_inner()
            there.merge(other_ref)
            swap.start()
            there.finish()
            here.send_terms(term(0), merge=True)
        else:
            here.send_terms(term(0))
            there.merge_inner()
            here.merge_leaves()
            there.merge(other_ref)
            swap.start()
        for move in moves[1:]:
            move.start()
        here.merge_inner()
        here.merge(d_hidden_ref)
        swap.wait()
        d_normed = d_hidden_ref[...] + swap_ref[...].astype(f32)
        values = hidden_ref[...]
        gain = jnp.concatenate([gains_ref[z, 1:2, :] for z in range(shard_size)], axis=1)
        d_values, d_gain = norm_back(values, inverse_rms(values), gain, d_normed)
        d_hidden = cot_ref[...].astype(f32) + d_values
        d_attn_ref[...] = d_hidden.astype(bf16)
        gather = SeqGather(seq_size, d_attn_all, rows, ns, nr, own=d_attn_ref)
        gather.start()
        own = pltpu.make_async_copy(d_attn_ref, d_attn_all.at[rows_at(me, rows), :], own_sem)
        own.start()
        d_hidden_ref[...] = d_hidden
        d_gain_ref[...] = d_gain
        gather.forwards()
        own.wait()
        gather.finish()
        for scatter in scatters[: 1 if shared else 2]:
            scatter.finish()
        for move in moves:
            move.wait()

    scatter = scatter_scratch(seq_size, rows, width)
    outs = pl.pallas_call(
        kernel,
        name="mlp_back",
        out_shape=[
            array((rows, width), f32),
            array((1, width), f32),
            array((length, width)),
        ]
        + [array(g.shape) for g in grads],
        in_specs=in_vmem(5 + 2 * chunks) + in_any(count),
        out_specs=in_vmem(2) + in_any(1 + count),
        scratch_shapes=scatter[:1] * (1 if shared else 2)
        + scatter[1:2] * 2
        + [DMA((seq_size,))] * 4
        + [VMEM((rows, width), bf16)] * 3
        + [DMA((seq_size,))] * 2
        + [DMA((2,)), DMA]
        + [DMA((max(1, count), shard_size))] * 2,
        compiler_params=kernel_params(3),
    )(d_gate, d_up, hidden, cot, gains_all, *gate, *up, *grads)
    return outs[:3], list(outs[3:])


class OutputSum:
    def __init__(self, scatter, act, down_refs, base=0):
        self.scatter, self.act, self.down_refs, self.base = scatter, act, down_refs, base

    def compute(self, mask):
        tokens = self.scatter.tokens(mask, self.base)
        shards, _, part = self.down_refs[0].shape
        for z in range(shards):
            total = None
            for c, down in enumerate(self.down_refs):
                one = dot_nn(self.act[c, tokens, :], down[z])
                total = one if total is None else total + one
            self.scatter.put(mask, slice(z * part, (z + 1) * part), total)


def attend_back(d_attn, wo, mixed, q, k, v, lse, table, normed, grads, activ, down):
    seq_size, shard_size = lax.axis_size("seq"), lax.axis_size("shard")
    length, width = d_attn.shape
    rows = length // seq_size
    cols = q.shape[1]
    part = wo.shape[2]
    big = row_step(length, 512)
    block = row_step(length, 256)
    scale = 1.0 / math.sqrt(HD)
    pair = 2 * HD
    count = len(grads)
    chunks = len(down)

    def kernel(*refs):
        take = Refs(refs)
        da_ref, wo_ref, mixed_ref, q_ref, k_ref, v_ref, lse_ref, t_ref, n_ref = take(9)
        down_refs = take(chunks)
        grad_refs = take(count)
        act_all = take(1)[0] if chunks else None
        dq_ref, dk_ref, dv_ref, gq_ref, gk_ref, gv_ref = take(6)
        if chunks:
            swap_ref = take(1)[0]
        sum_refs = take(count + 1)
        do_ref, kt_ref, dk_acc, dv_acc, xt_ref, go_ref, sum_s, sum_r = take(8)

        if chunks:
            terms, arrived, ss, sr, act_ref, other_ref, act_sem, swap_sem = take(8)
            act_copy = pltpu.make_async_copy(
                act_all.at[:, pl.ds(length, length), :], act_ref, act_sem
            )
            act_copy.start()
        entry_barrier(seq_neighbours(seq_size) if chunks else [], shard_size)
        moves = [
            ShardExchange(shard_size, lambda j, g=g: g.at[j], out, sum_s.at[i], sum_r.at[i])
            for i, (g, out) in enumerate(zip(grad_refs + [go_ref], sum_refs))
        ]
        for move in moves[:-1]:
            move.start()
        if chunks:
            swap = PairSwap(other_ref, swap_ref, swap_sem).copy
            act_copy.wait()
            out_sum = OutputSum(SeqScatter(seq_size, terms, arrived, ss, sr), act_ref, down_refs)
            out_sum.scatter.send_terms(out_sum.compute, merge=True)

        xt_ref[...] = jnp.transpose(mixed_ref[...])
        for z in range(shard_size):
            go_ref[z] = dot_nn(xt_ref[...], da_ref[:, z * part : (z + 1) * part]).astype(bf16)
        if not chunks:
            moves[-1].start()

        @pl.loop(0, length // big)
        def _(i):
            r = rows_at(i, big)
            total = dot_nt(da_ref[r, :part], wo_ref[0])
            for z in range(1, shard_size):
                total += dot_nt(da_ref[r, z * part : (z + 1) * part], wo_ref[z])
            do_ref[r, :] = total.astype(bf16)

        kt_ref[...] = jnp.transpose(k_ref[...])
        if chunks:
            out_sum.scatter.merge_inner()

        def heads(hp, lanes):
            dk_acc[...] = jnp.zeros_like(dk_acc)
            dv_acc[...] = jnp.zeros_like(dv_acc)
            for i in range(length // block):
                first, last = i * block, (i + 1) * block
                q2 = q_ref[first:last, lanes]
                do2 = do_ref[first:last, lanes]
                keys = k_ref[:last, lanes]
                values = v_ref[:last, lanes]
                dqt, dk_add, dv_add = None, None, None
                for head in (0, 1):
                    keep = head_lanes(head, q2.shape)
                    qm = jnp.where(keep, q2, jnp.zeros_like(q2))
                    dom = jnp.where(keep, do2, jnp.zeros_like(do2))
                    st = dot_nt(keys, qm)
                    row = lse_ref[pl.ds(hp * 2 + head, 1), first:last]
                    p = jnp.exp(st - row)
                    r = lax.broadcasted_iota(jnp.int32, (block, block), 0)
                    c = lax.broadcasted_iota(jnp.int32, (block, block), 1)
                    tail = jnp.where(r <= c, p[first:], 0.0)
                    p = tail if i == 0 else jnp.concatenate([p[:first], tail], axis=0)
                    dp = dot_nt(values, dom)
                    inner = jnp.sum(dp * p, axis=0, keepdims=True)
                    ds = (p * (dp - inner)).astype(bf16)
                    dv_one = dot_nn(p.astype(bf16), dom)
                    dk_one = dot_nn(ds, qm)
                    dv_add = dv_one if head == 0 else dv_add + dv_one
                    dk_add = dk_one if head == 0 else dk_add + dk_one
                    dqt_one = dot_nn(kt_ref[lanes, :last], ds)
                    if head == 0:
                        dqt = dqt_one
                    else:
                        sub = lax.broadcasted_iota(jnp.int32, dqt.shape, 0)
                        dqt = jnp.where(sub < HD, dqt, dqt_one)
                dk_acc[:last, :] += dk_add
                dv_acc[:last, :] += dv_add
                dq = (jnp.transpose(dqt) * scale).astype(bf16).astype(f32)
                dq_ref[first:last, lanes] = turn(dq, t_ref[first:last, :], True).astype(bf16)
            dv_ref[:, lanes] = dv_acc[...].astype(bf16)

            @pl.loop(0, length // big)
            def _(i):
                r = rows_at(i, big)
                dk = dk_acc[r, :].astype(bf16).astype(f32)
                dk_ref[r, lanes] = turn(dk, t_ref[r, :], True).astype(bf16)

        if chunks:
            for hp in range(cols // pair):
                heads(hp, slice(hp * pair, (hp + 1) * pair))
                if hp == 0:
                    out_sum.scatter.merge(other_ref)
                    swap.start()
                    moves[-1].start()
        else:

            @pl.loop(0, cols // pair)
            def _(hp):
                heads(hp, rows_at(hp, pair))

        for source, out in ((dq_ref, gq_ref), (dk_ref, gk_ref), (dv_ref, gv_ref)):
            xt_ref[...] = jnp.transpose(source[...])
            for z in range(shard_size):
                out[z] = dot_nn(xt_ref[...], n_ref[:, z * part : (z + 1) * part]).astype(bf16)
        if chunks:
            swap.wait()
            out_sum.scatter.finish()
        for move in moves:
            move.wait()

    grad = array((shard_size, cols, part))
    scratch = [
        VMEM((length, cols), bf16),
        VMEM((cols, length), bf16),
        VMEM((length, pair), f32),
        VMEM((length, pair), f32),
        VMEM((cols, length), bf16),
        VMEM((shard_size, cols, part), bf16),
    ] + [DMA((count + 1, shard_size))] * 2
    if chunks:
        scratch += scatter_scratch(seq_size, rows, width)
        scratch += [VMEM((chunks, length, activ.shape[2]), bf16), VMEM((rows, width), bf16)]
        scratch += [DMA, DMA((2,))]
    outs = pl.pallas_call(
        kernel,
        name="attend_back",
        out_shape=[array((length, cols))] * 3
        + [grad] * 3
        + [array((rows, width))] * (1 if chunks else 0)
        + [array(g.shape) for g in grads]
        + [grad],
        in_specs=in_vmem(9 + chunks) + in_any(count + (1 if chunks else 0)),
        out_specs=in_vmem(7 if chunks else 6) + in_any(count + 1),
        scratch_shapes=scratch,
        compiler_params=kernel_params(4),
    )(d_attn, wo, mixed, q, k, v, lse, table, normed, *down, *grads, *([activ] if chunks else []))
    outs = list(outs)
    other = outs.pop(6) if chunks else None
    return outs[:3], outs[3:6], other, outs[6:]


def output_parts(activ, down, hidden):
    seq_size, shard_size = lax.axis_size("seq"), lax.axis_size("shard")
    rows, width = hidden.shape
    length = rows * seq_size
    chunks = len(down)

    def kernel(*refs):
        take = Refs(refs)
        act_ref, hidden_ref = take(2)
        down_refs = take(chunks)
        out_ref, terms, first, second = take(4)
        sems = [take(2), take(2)]
        total_ref, other_ref, swap_ref, swap_sem = take(4)
        entry_barrier(seq_neighbours(seq_size), shard_size)
        there, here = (
            OutputSum(SeqScatter(seq_size, terms, arrived, *sem), act_ref, down_refs, base)
            for arrived, sem, base in ((first, sems[0], length), (second, sems[1], 0))
        )
        there.scatter.run(there.compute, other_ref)
        swap = PairSwap(other_ref, swap_ref, swap_sem).copy
        swap.start()
        there.scatter.finish()
        here.scatter.run(here.compute, total_ref)
        swap.wait()
        out_ref[...] = (total_ref[...] + swap_ref[...].astype(f32) + hidden_ref[...]).astype(bf16)
        here.scatter.finish()

    scatter = scatter_scratch(seq_size, rows, width)
    return pl.pallas_call(
        kernel,
        name="output_parts",
        out_shape=array((rows, width)),
        in_specs=in_vmem(2 + chunks),
        out_specs=in_vmem(1)[0],
        scratch_shapes=scatter[:2]
        + scatter[1:2]
        + [DMA((seq_size,))] * 4
        + [VMEM((rows, width), f32), VMEM((rows, width), bf16), VMEM((rows, width), bf16)]
        + [DMA((2,))],
        compiler_params=kernel_params(6),
    )(activ, hidden, *down)


def finish(
    d_qkv, attn_weights, g_qkv, x, d_hidden, gains_all, d_gain_two, sums, g_output, block,
    output_of,
):
    seq_size, shard_size = lax.axis_size("seq"), lax.axis_size("shard")
    rows, width = x.shape
    part = width // shard_size
    cols = d_qkv[0].shape[1]
    length = rows * seq_size
    pieces = len(sums)
    half = pieces // 3 * block
    activ, down, hidden, other = output_of or (None, [], None, None)
    chunks = len(down)
    pairs = shard_size // 2

    def kernel(*refs):
        take = Refs(refs)
        x_ref, d_hidden_ref, gains_ref, gain2_ref = take(4)
        d_refs, w_refs, g_refs = take(3), take(3), take(3)
        down_refs = take(chunks)
        hidden_ref, other_ref = take(2) if chunks else (None, None)
        act_all = take(1)[0] if chunks else None
        sum_refs, go_ref = take(pieces), take(1)[0]
        d_inputs_ref, gain_ref = take(2)
        qkv_refs = take(3)
        output_ref = take(1)[0] if chunks else None
        wo_ref, wg_ref, wu_ref, wd_ref = take(4)
        total_ref, gain_mine, gain_shards, gain_line, gain_seq = take(5)
        gs, gr, hs, hr = take(4)
        in_terms, in_arrived, in_s, in_r = take(4)
        firsts, middles, seconds, reduce_sems = take(4)
        held, wide, tall, load_sem, store_sem = take(5)
        if chunks:
            out_terms, out_arrived, out_s, out_r, act_ref, act_sem, out_total = take(7)
            act_copy = pltpu.make_async_copy(act_all.at[:, pl.ds(0, length), :], act_ref, act_sem)
            act_copy.start()

        me = lax.axis_index("seq")
        entry_barrier(range(1, seq_size), shard_size)
        reduces = [
            PairReduce(
                shard_size, g_refs[i], firsts.at[i], middles.at[i], seconds.at[i], reduce_sems.at[i]
            )
            for i in range(3)
        ]
        for reduce in reduces:
            reduce.start()
        in_sum = SeqScatter(seq_size, in_terms, in_arrived, in_s, in_r)

        def inputs_term(mask):
            tokens = in_sum.tokens(mask)
            for z in range(shard_size):
                total = None
                for d_ref, w_ref in zip(d_refs, w_refs):
                    term = dot_nt(d_ref[tokens, :], w_ref[z])
                    total = term if total is None else total + term
                in_sum.put(mask, slice(z * part, (z + 1) * part), total)

        in_sum.send_terms(inputs_term, merge=True)
        if chunks:
            act_copy.wait()
            out_sum = OutputSum(
                SeqScatter(seq_size, out_terms, out_arrived, out_s, out_r), act_ref, down_refs
            )
            out_sum.scatter.send_terms(out_sum.compute)

        loads = [
            pltpu.make_async_copy(source, held.at[i % 2], load_sem.at[i % 2])
            for i, source in enumerate(sum_refs)
        ]
        stores = []

        def store(staging, target, value):
            turn_of = sum(1 for s in stores if s[0] is staging)
            slot = turn_of % 2
            sem = store_sem.at[0 if staging is wide else 1, slot]
            if turn_of >= 2:
                [s for s in stores if s[0] is staging][-2][1].wait()
            staging[slot] = value
            copy = pltpu.make_async_copy(staging.at[slot], target, sem)
            copy.start()
            stores.append((staging, copy))

        def collect(i):
            if i + 1 < pieces:
                loads[i + 1].start()
            loads[i].wait()
            for parity in (0, 1):
                total = held[i % 2, parity].astype(f32)
                for p in range(1, pairs):
                    total = total + held[i % 2, 2 * p + parity].astype(f32)
                start = parity * half + i // 3 * block
                if i % 3 == 2:
                    store(wide, wd_ref.at[start : start + block, :], total)
                else:
                    target = (wg_ref, wu_ref)[i % 3]
                    store(tall, target.at[:, start : start + block], jnp.transpose(total))

        loads[0].start()
        third = (pieces + 2) // 3
        in_sum.merge_inner()
        reduces[0].middle()
        if chunks:
            out_sum.scatter.merge_leaves()
        for i in range(third):
            collect(i)
        reduces[1].middle()
        in_sum.merge(total_ref)
        values = x_ref[...].astype(f32)
        gain = jnp.concatenate([gains_ref[z, 0:1, :] for z in range(shard_size)], axis=1)
        d_values, d_gain = norm_back(values, inverse_rms(values), gain, total_ref[...])
        d_inputs_ref[...] = (d_hidden_ref[...] + d_values).astype(bf16)
        for z in range(shard_size):
            lanes = slice(z * part, (z + 1) * part)
            gain_mine[z, 0:1, :] = d_gain[:, lanes]
            gain_mine[z, 1:2, :] = gain2_ref[0:1, lanes]
            gain_mine[z, 2:, :] = jnp.zeros((6, part), f32)
        line = ShardExchange(shard_size, lambda j: gain_mine.at[j], gain_shards, gs, gr)
        line.start()
        for i in range(third, 2 * third):
            collect(i)
        reduces[2].middle()
        if chunks:
            out_sum.scatter.merge_inner()
        line.wait()
        gain_line[...] = sum(gain_shards[z] for z in range(shard_size))

        def to_seq(step):
            return pltpu.make_async_remote_copy(
                src_ref=gain_line,
                dst_ref=gain_seq.at[step],
                send_sem=hs.at[step],
                recv_sem=hr.at[step],
                device_id={"seq": jnp.bitwise_xor(me, step)},
                device_id_type=MESH,
            )

        for step in range(1, seq_size):
            to_seq(step).start()
        for i in range(2 * third, pieces):
            collect(i)
        wo_ref[...] = sum(go_ref[z].astype(f32) for z in range(shard_size))
        if chunks:
            out_sum.scatter.merge(out_total)
            output_ref[...] = (
                out_total[...] + other_ref[...].astype(f32) + hidden_ref[...]
            ).astype(bf16)
        for reduce, out in zip(reduces, qkv_refs):
            out[...] = jnp.transpose(reduce.total())
        for step in range(1, seq_size):
            to_seq(step).wait()
        gain_ref[...] = gain_line[...] + sum(gain_seq[step] for step in range(1, seq_size))
        for staging in (wide, tall):
            for _, copy in [s for s in stores if s[0] is staging][-2:]:
                copy.wait()
        for reduce in reduces:
            reduce.finish()
        in_sum.finish()
        if chunks:
            out_sum.scatter.finish()

    scratch = [
        VMEM((rows, width), f32),
        VMEM((shard_size, 8, part), f32),
        VMEM((shard_size, 8, part), f32),
        VMEM((8, part), f32),
        VMEM((seq_size, 8, part), f32),
    ]
    scratch += [DMA((shard_size,))] * 2 + [DMA((seq_size,))] * 2
    scratch += scatter_scratch(seq_size, rows, width)
    scratch += [VMEM((3, pairs, cols, part), bf16)] * 3 + [DMA((3, 4, pairs))]
    scratch += [
        VMEM((2, shard_size, block, part), bf16),
        VMEM((2, block, part), f32),
        VMEM((2, part, block), f32),
        DMA((2,)),
        DMA((2, 2)),
    ]
    if chunks:
        scratch += scatter_scratch(seq_size, rows, width)
        scratch += [VMEM((chunks, length, block), bf16), DMA, VMEM((rows, width), f32)]
    extra = 1 if chunks else 0
    units = 2 * half
    outs = pl.pallas_call(
        kernel,
        name="finish",
        out_shape=[array((rows, width)), array((8, part), f32)]
        + [array((part, cols), f32)] * 3
        + [array((rows, width))] * extra
        + [array((cols, part), f32)]
        + [array((part, units), f32)] * 2
        + [array((units, part), f32)],
        in_specs=in_vmem(13 + chunks + 2 * extra) + in_any(extra + pieces) + in_vmem(1),
        out_specs=in_vmem(6 + extra) + in_any(3),
        scratch_shapes=scratch,
        compiler_params=kernel_params(5),
    )(
        x, d_hidden, gains_all, d_gain_two, *d_qkv, *attn_weights, *g_qkv, *down,
        *([hidden, other, activ] if chunks else []), *sums, g_output,
    )
    outs = list(outs)
    output = outs.pop(5) if chunks else None
    return outs, output


def rotation_table(position_ids):
    half = HD // 2
    freqs = theta_base ** (-(jnp.arange(half, dtype=f32) * 2.0) / HD)
    angles = position_ids.astype(f32)[:, None] * freqs[None, :]
    cosine, sine = jnp.cos(angles), jnp.sin(angles)
    return jnp.concatenate([cosine, cosine, -sine, sine], axis=1)


EARLY = 4
SUMS = (1, 4)
SWAP_FIRST = False


def body(
    inputs,
    positions,
    attn_gain,
    w_query,
    w_key,
    w_value,
    w_output,
    mlp_gain,
    w_gate,
    w_up,
    w_down,
    cotangent,
):
    shard_size = lax.axis_size("shard")
    x, cot = inputs[0], cotangent[0]
    gains = jnp.pad(jnp.stack([attn_gain, mlp_gain]).astype(f32), ((0, 6), (0, 0)))
    table = rotation_table(positions[0])
    half = w_gate.shape[1] // 2
    block = row_step(half, 256)
    chunks = half // block
    pieces = weight_pieces(chunks)
    early, late = pieces[:EARLY], pieces[EARLY:]
    mlp_weights = (w_gate, w_up, w_down)
    held, early_weights = forward(
        x, gains, table, cot, (w_query, w_key, w_value, w_output), mlp_weights, early, block
    )
    normed, tables, gains_all, wq, wk, wv, wo, q, k, v, mixed, lse, hidden = held[:13]
    cot_all, cot_other, tok, tok_other = held[13:]
    acts, grads, late_weights, sums = mlp(
        tok, tok_other, cot_all, cot_other, early_weights, mlp_weights, late, chunks, block,
        min(SUMS[0], len(pieces)),
    )
    activ, d_gate, d_up = acts
    weights = dict(zip(pieces, early_weights + late_weights))

    def kind(name):
        return [weights[c, name] for c in range(chunks)]

    done = len(sums)
    more = min(SUMS[1], len(pieces) - done)
    (d_hidden, d_gain_two, d_attn), moved = mlp_back(
        d_gate, d_up, kind("gate"), kind("up"), hidden, cot, gains_all, grads[done : done + more]
    )
    sums += moved
    done += more
    down = kind("down")
    together = tok.shape[0] <= 2048
    d_qkv, g_qkv, other, moved = attend_back(
        d_attn, wo, mixed, q, k, v, lse, tables, normed, grads[done:], activ,
        down if together else [],
    )
    sums += moved[:-1]
    results, output = finish(
        d_qkv, (wq, wk, wv), g_qkv, x, d_hidden, gains_all, d_gain_two, sums, moved[-1], block,
        (activ, down, hidden, other) if together else None,
    )
    if not together:
        output = output_parts(activ, down, hidden)
    d_inputs, gain_sums, g_query, g_key, g_value, g_output, g_gate, g_up, g_down = results
    return (
        output[None],
        d_inputs[None],
        gain_sums[0],
        g_query,
        g_key,
        g_value,
        g_output,
        gain_sums[1],
        g_gate,
        g_up,
        g_down,
    )


def solution(mesh):
    in_specs = (
        P("shard", "seq", None),
        P("shard", "seq"),
        P("shard"),
        P("shard", "seq"),
        P("shard", "seq"),
        P("shard", "seq"),
        P("seq", "shard"),
        P("shard"),
        P("shard", "seq"),
        P("shard", "seq"),
        P("seq", "shard"),
        P("shard", "seq", None),
    )
    out_specs = (
        P("shard", "seq", None),
        P("shard", "seq", None),
        P("shard"),
        P("shard", "seq"),
        P("shard", "seq"),
        P("shard", "seq"),
        P("seq", "shard"),
        P("shard"),
        P("shard", "seq"),
        P("shard", "seq"),
        P("seq", "shard"),
    )
    return jax.shard_map(body, mesh=mesh, in_specs=in_specs, out_specs=out_specs, check_vma=False)
```

time: 1250 us -> 587 us (0.47)
  waiting for transfers between devices: 869 us -> 0 us
  Pallas kernels: 0 us -> 560 us
  matrix products: 227 us -> 0 us
  other arithmetic: 68.5 us -> 2.52 us
  blocking collectives: 35.1 us -> 0 us
  between operations: 15.4 us -> 1.17 us
    pallas_call x0 -> x5, Pallas kernels: none -> 560 us  [the longest x1 207 us: forward(): pl.pallas_call(kernel, name='forward_attention', out_shape=[tokens, array...]
    reduce_scatter x9 -> x0, waiting for transfers between devices: 438 us -> none  [the longest x4 248 us: seq_partials(): lax.psum_scatter(term(jnp.int32(0), row_count * lax.axis_size('seq')).ast...]
    all_gather x9 -> x0, waiting for transfers between devices: 402 us -> none  [the longest x1 76.2 us: body(): up_cols = lax.all_gather(w_up, 'shard', axis=0, tiled=True)]
    dot_general x36 -> x0, matrix products: 227 us -> none  [the longest x5 57.3 us: product_right_t(): lax.dot_general(left, right, (((1,), (1,)), ((), ())), preferred_element_...]
    convert_element_type x13 -> x1, other arithmetic: 34.8 us -> 0.68 us  [rotation_table(): angles = position_ids.astype(f32)[:, None] * freqs[None, :]]
    unnamed x20 -> x0, waiting for transfers between devices: 29.2 us -> none
    reduce_sum x7 -> x0, other arithmetic: 17.4 us -> none  [the longest x3 10.6 us: one_block(): totals = jnp.sum(expo, axis=-1, keepdims=True)]
    all_gather x1 -> x0, blocking collectives: 13.6 us -> none  [body(): lax.all_gather(jnp.stack([attn_gain, mlp_gain]), 'shard', axis=1, tiled=T...]
  transfers between devices with their start and end apart: 19 -> 0, of which waited for: 17 -> 0; matrix products, arithmetic and copies ran while one was open for 21% -> 0% of each run, Pallas kernels for 0% -> 0%
where the time goes in v3:
time: 587 us; the launch traced here: 579 us
  Pallas kernels  560 us (95%)
  local copies, waits for them, and re-layouts  15.4 us (3%)
    pallas_call x1, Pallas kernels, forward(): pl.pallas_call(kernel, name='forward_attention', out_shape=[tokens, array...  207 us
    pallas_call x1, Pallas kernels, mlp_back(): pl.pallas_call(kernel, name='mlp_back', out_shape=[array((rows, width), f...  118 us
    pallas_call x1, Pallas kernels, mlp(): pl.pallas_call(kernel, name='mlp', out_shape=[act] * 3 + [piece] * len(pi...  83.8 us
    pallas_call x1, Pallas kernels, attend_back(): pl.pallas_call(kernel, name='attend_back', out_shape=[array((length, cols...  79.4 us
    pallas_call x1, Pallas kernels, finish(): pl.pallas_call(kernel, name='finish', out_shape=[array((rows, width)), ar...  72.1 us
    unnamed x23, local copies, waits for them, and re-layouts  12.6 us

profile of v3, /device:TPU:0, one launch (start us, length us, event | category | flops | bytes accessed | tf_op | source)
XLA Modules:
  0.0 578.7 jit_solution(17113521406489327876)
XLA Ops:
  0.7 0.7 convert_element_type.13
  1.3 0.7 stack.9
  2.0 0.7 stack.10
  2.7 0.6 fusion.4.refs_1_
  3.3 0.4 multiply_cosine_fusion
  3.7 0.8 pad_maximum_fusion.refs_2_
  4.5 206.8 %forward_attention.1 = (bf16[1536,2048]{1,0:T(8,128)(2,1)}, f32[1536,128]{1,0:T(8,128)}, f32[4,8,512]{2,1,0:T(8,128)}, bf16[4,512,256]{2,1,0:T(8,128)(2,1)}, bf1...) custom-call(bf16[192,2048]{1,0:T(8,128)(2,1)} %bitcast.9, ...), custom_call_target="tpu_custom_call" | custom-call | tf_op jit(solution)/shard_map/forward_attention/pallas_call | solution.py:719
  211.4 83.8 %mlp.1 = (bf16[2,3072,256]{2,1,0:T(8,128)(2,1)}, bf16[2,3072,256]{2,1,0:T(8,128)(2,1)}, bf16[2,3072,256]{2,1,0:T(8,128)(2,1)}, bf16[4,256,512]{2,1,0:T(8,128)(2,...) custom-call(bf16[1536,2048]{1,0:T(8,128)(2,1)} %get-tuple-element.69, ...), custom_call_target="tpu_custom_call" | custom-call | tf_op jit(solution)/shard_map/mlp/pallas_call | solution.py:909
  295.2 117.6 %mlp_back.1 = (f32[192,2048]{1,0:T(8,128)}, f32[1,2048]{1,0:T(1,128)}, bf16[1536,2048]{1,0:T(8,128)(2,1)}, bf16[4,256,512]{2,1,0:T(8,128)(2,1)}, bf16[4,256,512]...) custom-call(bf16[2,3072,256]{2,1,0:T(8,128)(2,1)} %get-tuple-element.77.refs_0_, ...), custom_call_target="tpu_custom_call" | custom-call | tf_op jit(solution)/shard_map/mlp_back/pallas_call | solution.py:1028
  412.7 79.4 %attend_back.1 = (bf16[1536,256]{1,0:T(8,128)(2,1)}, bf16[1536,256]{1,0:T(8,128)(2,1)}, bf16[1536,256]{1,0:T(8,128)(2,1)}, bf16[4,256,512]{2,1,0:T(8,128)(2,1)},...) custom-call(bf16[1536,2048]{1,0:T(8,128)(2,1)} %get-tuple-element.88, ...), custom_call_target="tpu_custom_call" | custom-call | tf_op jit(solution)/shard_map/attend_back/pallas_call | solution.py:1210
  492.1 72.1 %finish.1 = (bf16[192,2048]{1,0:T(8,128)(2,1)}, f32[8,512]{1,0:T(8,128)}, f32[512,256]{1,0:T(8,128)}, f32[512,256]{1,0:T(8,128)}, f32[512,256]{1,0:T(8,128)}, /*...) custom-call(bf16[192,2048]{1,0:T(8,128)(2,1)} %bitcast.10, ...), custom_call_target="tpu_custom_call" | custom-call | tf_op jit(solution)/shard_map/finish/pallas_call | solution.py:1454
  564.3 0.0 copy-start.6
  564.3 0.0 copy-start.5
  564.3 1.4 fusion.5
  565.7 2.1 copy.33
  567.9 2.2 copy.34
  570.1 0.8 copy.35
  570.9 0.8 copy.36
  571.7 0.8 copy.37
  572.5 0.8 copy.38
  573.3 1.3 copy.39
  574.6 1.3 copy.40
  575.9 1.0 copy-done
  577.0 1.3 copy.41
  (12 shorter events, 0.0 us)
Async XLA Ops:
  564.3 5.9 %copy-start.6 = (f32[512,256]{1,0:T(8,128)S(1)}, f32[512,256]{1,0:T(8,128)}, u32[]{:S(2)}) copy-start(f32[512,256]{1,0:T(8,128)} %get-tuple-element.146) | copy-start | bytes 1572868
  564.3 6.6 %copy-start.5 = (f32[512,256]{1,0:T(8,128)S(1)}, f32[512,256]{1,0:T(8,128)}, u32[]{:S(2)}) copy-start(f32[512,256]{1,0:T(8,128)} %get-tuple-element.147) | copy-start | bytes 1572868
  564.3 7.4 %copy-start.4 = (f32[512,256]{1,0:T(8,128)S(1)}, f32[512,256]{1,0:T(8,128)}, u32[]{:S(2)}) copy-start(f32[512,256]{1,0:T(8,128)} %get-tuple-element.148) | copy-start | bytes 1572868
  565.7 6.8 %copy-start.3 = (f32[256,512]{1,0:T(8,128)S(1)}, f32[256,512]{1,0:T(8,128)}, u32[]{:S(2)}) copy-start(f32[256,512]{1,0:T(8,128)} %get-tuple-element.149) | copy-start | bytes 1572868
  567.9 5.4 copy-start.2
  571.7 2.9 copy-start.1
  574.6 2.3 copy-start

commit v4 on v3

--- a/solution.py
+++ b/solution.py
@@ -361,6 +361,26 @@
             self.source(self.k), self.out.at[self.k], self.send_sem.at[0]
         )
 
+    def inner(self, step):
+        target = lax.rem(self.k + step, self.size)
+        beside = jnp.abs(target - self.k) == 1
+        return jnp.logical_and(beside, target // 2 != self.k // 2)
+
+    def start_inner(self):
+        for step in (1, self.size - 1):
+
+            @pl.when(self.inner(step))
+            def _():
+                self.copy(step).start()
+
+    def start_outer(self):
+        self.local().start()
+        for step in range(1, self.size):
+
+            @pl.when(jnp.logical_not(self.inner(step)))
+            def _():
+                self.copy(step).start()
+
     def start(self):
         self.local().start()
         for step in range(1, self.size):
@@ -451,6 +471,29 @@
             device_id={"shard": jnp.bitwise_xor(mine, 1)},
             device_id_type=MESH,
         )
+
+
+class Moves:
+    def __init__(self, sems):
+        self.sems, self.copies = sems, []
+
+    def start(self, source, target):
+        copy = pltpu.make_async_copy(source, target, self.sems.at[len(self.copies)])
+        copy.start()
+        self.copies.append(copy)
+        return copy
+
+    def wait(self, count=None):
+        count = len(self.copies) if count is None else count
+        for copy in [c for c in self.copies if c is not None][:count]:
+            copy.wait()
+        left = [i for i, c in enumerate(self.copies) if c is not None][:count]
+        for i in left:
+            self.copies[i] = None
+
+
+def held(arrays):
+    return [VMEM(a.shape, a.dtype) for a in arrays]
 
 
 class Refs:
@@ -544,15 +587,19 @@
         x_ref, gains_ref, table_ref, cot_ref = take(4)
         own_weights = take(4)
         mlp_refs = dict(zip(("gate", "up", "down"), take(3)))
-        normed_all, table_all, gains_all = take(3)
-        full_weights = take(4)
-        q_ref, k_ref, v_ref, o_ref, lse_ref, hidden_ref = take(6)
+        normed_out, table_all, gains_all = take(3)
+        weights_out = take(4)
+        heads_out = take(4)
+        lse_ref, hidden_ref = take(2)
         cot_all, cot_other, tok_all, tok_other = take(4)
         piece_refs = take(len(pieces))
         terms, arrived, ss, sr = take(4)
-        normed_ref = take(1)[0]
+        normed_ref, normed_all = take(2)
+        full_weights, heads_held = take(4), take(4)
+        q_ref, k_ref, v_ref, o_ref = heads_held
+        out_sems = take(1)[0]
         ns, nr, ts, tr, cs, cr, ds, dr, ms, mr = take(10)
-        gs, gr, wo_s, wo_r, line_s, line_r, line_c, piece_s, piece_r, local_sem, swap_sem = take(11)
+        gs, gr, line_s, line_r, line_c, piece_s, piece_r, local_sem, swap_sem = take(9)
 
         me, mine = lax.axis_index("seq"), lax.axis_index("shard")
         entry_barrier(seq_neighbours(seq_size), shard_size)
@@ -560,7 +607,7 @@
         gain.start()
         lines = [
             LineGather(shard_size, own, out, line_s.at[i], line_r.at[i], line_c.at[i])
-            for i, (own, out) in enumerate(zip(own_weights[:3], full_weights))
+            for i, (own, out) in enumerate(zip(own_weights, full_weights))
         ]
         wq_all, wk_all, wv_all, wo_all = full_weights
         exchanges = [
@@ -576,10 +623,7 @@
         cots = SeqGather(seq_size, cot_all, rows, cs, cr, own=cot_ref)
         cots_other = SeqGather(seq_size, cot_other, rows, ds, dr)
         swap_cot = PairSwap(cot_ref, cot_other.at[mine_rows, :], swap_sem.at[0]).copy
-        wo_move = ShardExchange(shard_size, lambda j: own_weights[3], wo_all, wo_s, wo_r)
-        if SWAP_FIRST:
-            swap_cot.start()
-        for line in lines:
+        for line in lines[:3]:
             line.step(0)
         own_cot.start()
         table_all[mine_rows, :] = table_ref[...]
@@ -592,30 +636,38 @@
             normed_all[mine_rows, lanes] = (scaled[:, lanes] * gains_all[z, 0:1, :]).astype(bf16)
         normed.start()
         tables.forwards()
-        for line in lines:
+        for line in lines[:3]:
             line.step(1)
+        for exchange in exchanges:
+            exchange.start_inner()
         near, far = split_masks(seq_size)
         for mask in near:
             normed.forward(mask)
         cots.start()
         for step in range(2, shard_size):
-            for line in lines:
+            for line in lines[:3]:
                 line.step(step)
             if step == 2:
-                wo_move.start()
-                if not SWAP_FIRST:
-                    swap_cot.start()
-                for exchange in exchanges[:3]:
-                    exchange.start()
+                swap_cot.start()
+                lines[3].step(0)
                 for mask in far:
                     normed.forward(mask)
         tables.finish()
         normed.finish()
+        outs = Moves(out_sems)
+        outs.start(normed_all, normed_out)
+        for held_weight, out in list(zip(full_weights, weights_out))[:3]:
+            outs.start(held_weight, out)
         for mask in near:
             cots.forward(mask)
-        if SWAP_FIRST:
-            swap_cot.wait_recv()
-            cots_other.start()
+        lines[3].step(1)
+
+        def start_pieces(point):
+            if point == START:
+                for exchange in exchanges[:AHEAD]:
+                    exchange.start_outer()
+
+        start_pieces(0)
 
         wq, wk, wv = (w.reshape(width, cols) for w in (wq_all, wk_all, wv_all))
 
@@ -631,10 +683,11 @@
 
         for mask in far:
             cots.forward(mask)
-
-        @pl.loop(0, cols // pair)
-        def _(hp):
-            lanes = rows_at(hp, pair)
+        start_pieces(1)
+        for step in range(2, shard_size - 1):
+            lines[3].step(step)
+
+        def attend(hp, lanes):
             for i in range(length // query):
                 first, last = i * query, (i + 1) * query
                 q2 = q_ref[first:last, lanes]
@@ -657,10 +710,26 @@
                     lse_ref[pl.ds(hp * 2 + head, 1), first:last] = lse[0:1, :]
                 o_ref[first:last, lanes] = out.astype(bf16)
 
-        for mask in near:
-            if SWAP_FIRST:
-                cots_other.forward(mask)
-        wo_move.wait_recv()
+        if cols == 2 * pair:
+            attend(0, slice(0, pair))
+            swap_cot.wait_recv()
+            cots_other.start()
+            start_pieces(2)
+            attend(1, slice(pair, cols))
+        else:
+
+            @pl.loop(0, cols // pair)
+            def _(hp):
+                attend(hp, rows_at(hp, pair))
+
+            swap_cot.wait_recv()
+            cots_other.start()
+            start_pieces(2)
+        lines[3].step(shard_size - 1)
+        start_pieces(3)
+        outs.start(full_weights[3], weights_out[3])
+        for held_heads, out in zip(heads_held, heads_out):
+            outs.start(held_heads, out)
         scatter = SeqScatter(seq_size, terms, arrived, ss, sr)
 
         def compute(mask):
@@ -668,10 +737,13 @@
             for z in range(shard_size):
                 scatter.put(mask, slice(z * part, (z + 1) * part), dot_nn(tokens, wo_all[z]))
 
-        scatter.run(compute, hidden_ref)
+        scatter.send_terms(compute, merge=True)
+        for mask in near:
+            cots_other.forward(mask)
+        scatter.merge_inner()
+        scatter.merge(hidden_ref)
         for mask in far:
-            if SWAP_FIRST:
-                cots_other.forward(mask)
+            cots_other.forward(mask)
         hidden = hidden_ref[...] + x_ref[...].astype(f32)
         hidden_ref[...] = hidden
         scaled = hidden * inverse_rms(hidden)
@@ -684,19 +756,13 @@
         toks.start()
         own_tok = pltpu.make_async_copy(normed_ref, tok_all.at[mine_rows, :], local_sem.at[1])
         own_tok.start()
-        for exchange in exchanges[3:]:
-            exchange.start()
+        for exchange in exchanges[AHEAD:]:
+            exchange.start_outer()
         for mask in near:
             toks.forward(mask)
-        if not SWAP_FIRST:
-            swap_cot.wait_recv()
-            cots_other.start()
         for mask in far:
             toks.forward(mask)
-        if not SWAP_FIRST:
-            cots_other.forwards()
         swap_cot.wait_send()
-        wo_move.wait_send()
         gain.wait_send()
         scatter.finish()
         own_cot.wait()
@@ -709,6 +775,7 @@
         cots_other.finish()
         for exchange in exchanges:
             exchange.wait()
+        outs.wait()
 
     weight = array((shard_size, part, cols))
     out_weight = array((shard_size, cols, part))
@@ -740,13 +807,15 @@
         ]
         + [array(s) for s in shapes],
         in_specs=in_vmem(3) + in_any(1) + in_vmem(4) + in_any(3),
-        out_specs=in_vmem(13) + in_any(4 + count),
+        out_specs=in_any(1) + in_vmem(2) + in_any(8) + in_vmem(2) + in_any(4 + count),
         scratch_shapes=scatter_scratch(seq_size, rows, width)
-        + [VMEM((rows, width), bf16)]
+        + [VMEM((rows, width), bf16), VMEM((length, width), bf16)]
+        + held([weight] * 3 + [out_weight] + [heads] * 4)
+        + [DMA((9,))]
         + [DMA((seq_size,))] * 10
-        + [DMA((shard_size,))] * 4
-        + [DMA((3, 2, shard_size - 1))] * 2
-        + [DMA((3,))]
+        + [DMA((shard_size,))] * 2
+        + [DMA((4, 2, shard_size - 1))] * 2
+        + [DMA((4,))]
         + [DMA((count, shard_size))] * 2
         + [DMA((2,)), DMA((2, 2))],
         compiler_params=kernel_params(1),
@@ -766,16 +835,22 @@
 
     def kernel(*refs):
         take = Refs(refs)
-        tok_ref, tok_swap = take(2)
+        tok_swap, tok_hbm = take(2)
         cots = take(2)
         early_refs = take(len(early))
         mlp_refs = dict(zip(("gate", "up", "down"), take(3)))
-        act_ref, dg_ref, du_ref = take(3)
-        grads = take(len(pieces))
+        acts_out = take(3)
+        grads_out = take(len(pieces))
         late_refs = take(len(late))
         sum_refs = take(sums)
         tok2, cot_rows, cot_cols, xt = take(4)
         weights = take(len(pieces))
+        act_ref, dg_ref, du_ref = take(3)
+        grads = take(len(pieces))
+        tok_ref, tok_sem, out_sems = take(3)
+        tok_copy = pltpu.make_async_copy(tok_hbm, tok_ref, tok_sem)
+        tok_copy.start()
+        outs = Moves(out_sems)
         ts, tr, late_s, late_r, sum_s, sum_r, row_sem, col_sem, load_sem = take(9)
 
         me, mine = lax.axis_index("seq"), lax.axis_index("shard")
@@ -863,6 +938,15 @@
                     copy.wait()
                 grads[3 * c + 2][z] = dot_nn(xt[2], cot_cols[z % 2]).astype(bf16)
 
+        def put_acts(these):
+            for c in these:
+                for ref, out in zip((act_ref, dg_ref, du_ref), acts_out):
+                    outs.start(ref.at[c], out.at[c])
+
+        def put_grads(c):
+            for i in range(max(sums, 3 * c), 3 * c + 3):
+                outs.start(grads[i], grads_out[i])
+
         sum_moves = [
             ShardExchange(shard_size, lambda j, g=g: g.at[j], out, sum_s.at[i], sum_r.at[i])
             for i, (g, out) in enumerate(zip(grads, sum_refs))
@@ -873,13 +957,16 @@
         later_chunks = [c for c in range(chunks) if c not in first_chunks]
         for load in loads[: len(early)]:
             load.wait()
+        tok_copy.wait()
         stage(0, first_chunks, 0)
         row_copy(1, 0, 0).start()
         other.forwards()
         other.finish()
         stage(1, first_chunks, 0)
+        put_acts(first_chunks)
         for c in first_chunks:
             grad(c)
+            put_grads(c)
             for move in sum_moves[3 * c : 3 * c + 3]:
                 move.start()
         if later_chunks:
@@ -893,14 +980,17 @@
             stage(0, later_chunks, 0)
             row_copy(1, 0, 0).start()
             stage(1, later_chunks, 0)
+            put_acts(later_chunks)
             for c in later_chunks:
                 grad(c)
+                put_grads(c)
                 for move in sum_moves[3 * c : 3 * c + 3]:
                     move.start()
         for move in late_moves:
             move.wait_send()
         for move in sum_moves:
             move.wait()
+        outs.wait()
 
     piece = array((shard_size, block, part))
     act = array((chunks, 2 * length, block))
@@ -913,8 +1003,8 @@
         + [piece] * len(pieces)
         + [array(s) for s in late_shapes]
         + [piece] * sums,
-        in_specs=in_vmem(2) + in_any(2 + len(early) + 3),
-        out_specs=in_vmem(3 + len(pieces)) + in_any(len(late) + sums),
+        in_specs=in_vmem(1) + in_any(3 + len(early) + 3),
+        out_specs=in_any(3 + len(pieces) + len(late) + sums),
         scratch_shapes=[
             VMEM((length, width), bf16),
             VMEM((2, big, width), bf16),
@@ -922,12 +1012,14 @@
             VMEM((3, block, 2 * length), bf16),
         ]
         + [VMEM(s, bf16) for s in all_shapes]
+        + held([act] * 3 + [piece] * len(pieces))
+        + [VMEM((length, width), bf16), DMA, DMA((3 * chunks + len(pieces),))]
         + [DMA((seq_size,))] * 2
         + [DMA((max(1, len(late)), shard_size))] * 2
         + [DMA((max(1, sums), shard_size))] * 2
         + [DMA((2,)), DMA((2, 2)), DMA((len(pieces),))],
         compiler_params=kernel_params(2),
-    )(tok, tok_other, cot, cot_other, *pieces_in, *mlp_weights)
+    )(tok_other, tok, cot, cot_other, *pieces_in, *mlp_weights)
     outs = list(outs)
     first = 3 + len(pieces)
     second = first + len(late)
@@ -945,8 +1037,8 @@
 
     def kernel(*refs):
         take = Refs(refs)
-        dg_ref, du_ref, hidden_ref, cot_ref, gains_ref = take(5)
-        gate_refs, up_refs = take(chunks), take(chunks)
+        sources = take(2 + 2 * chunks)
+        hidden_ref, cot_ref, gains_ref = take(3)
         grad_refs = take(count)
         d_hidden_ref, d_gain_ref, d_attn_all = take(3)
         sum_refs = take(count)
@@ -955,6 +1047,12 @@
         scatter_sems = [take(2), take(2)]
         other_ref, swap_ref, d_attn_ref = take(3)
         ns, nr, swap_sem, own_sem, sum_s, sum_r = take(6)
+        loaded, load_sems = take(2 + 2 * chunks), take(1)[0]
+        dg_ref, du_ref = loaded[:2]
+        gate_refs, up_refs = loaded[2 : 2 + chunks], loaded[2 + chunks :]
+        loads = Moves(load_sems)
+        for source, target in zip(sources, loaded):
+            loads.start(source, target)
 
         me = lax.axis_index("seq")
         entry_barrier(seq_neighbours(seq_size), shard_size)
@@ -962,9 +1060,10 @@
             ShardExchange(shard_size, lambda j, g=g: g.at[j], out, sum_s.at[i], sum_r.at[i])
             for i, (g, out) in enumerate(zip(grad_refs, sum_refs))
         ]
-        for move in moves[:1]:
+        for move in moves[:BEFORE]:
             move.start()
         swap = PairSwap(other_ref, swap_ref, swap_sem).copy
+        loads.wait()
         scatters = [
             SeqScatter(seq_size, terms[0 if shared else i], arrived[i], *scatter_sems[i])
             for i in range(2)
@@ -999,7 +1098,7 @@
             here.merge_leaves()
             there.merge(other_ref)
             swap.start()
-        for move in moves[1:]:
+        for move in moves[BEFORE:]:
             move.start()
         here.merge_inner()
         here.merge(d_hidden_ref)
@@ -1025,6 +1124,7 @@
             move.wait()
 
     scatter = scatter_scratch(seq_size, rows, width)
+    inputs = [d_gate, d_up, *gate, *up]
     outs = pl.pallas_call(
         kernel,
         name="mlp_back",
@@ -1034,7 +1134,7 @@
             array((length, width)),
         ]
         + [array(g.shape) for g in grads],
-        in_specs=in_vmem(5 + 2 * chunks) + in_any(count),
+        in_specs=in_any(2 + 2 * chunks) + in_vmem(3) + in_any(count),
         out_specs=in_vmem(2) + in_any(1 + count),
         scratch_shapes=scatter[:1] * (1 if shared else 2)
         + scatter[1:2] * 2
@@ -1042,9 +1142,11 @@
         + [VMEM((rows, width), bf16)] * 3
         + [DMA((seq_size,))] * 2
         + [DMA((2,)), DMA]
-        + [DMA((max(1, count), shard_size))] * 2,
+        + [DMA((max(1, count), shard_size))] * 2
+        + held(inputs)
+        + [DMA((len(inputs),))],
         compiler_params=kernel_params(3),
-    )(d_gate, d_up, hidden, cot, gains_all, *gate, *up, *grads)
+    )(*inputs, hidden, cot, gains_all, *grads)
     return outs[:3], list(outs[3:])
 
 
@@ -1078,8 +1180,7 @@
 
     def kernel(*refs):
         take = Refs(refs)
-        da_ref, wo_ref, mixed_ref, q_ref, k_ref, v_ref, lse_ref, t_ref, n_ref = take(9)
-        down_refs = take(chunks)
+        sources = take(9 + chunks)
         grad_refs = take(count)
         act_all = take(1)[0] if chunks else None
         dq_ref, dk_ref, dv_ref, gq_ref, gk_ref, gv_ref = take(6)
@@ -1087,6 +1188,13 @@
             swap_ref = take(1)[0]
         sum_refs = take(count + 1)
         do_ref, kt_ref, dk_acc, dv_acc, xt_ref, go_ref, sum_s, sum_r = take(8)
+        loaded, load_sems = take(9 + chunks), take(1)[0]
+        da_ref, wo_ref, mixed_ref, q_ref, k_ref, v_ref, lse_ref, t_ref, n_ref = loaded[:9]
+        down_refs = loaded[9:]
+        loads = Moves(load_sems)
+        first = list(range(9, 9 + chunks)) + [0, 2]
+        for i in first + [1, 3, 4, 5, 6, 7, 8]:
+            loads.start(sources[i], loaded[i])
 
         if chunks:
             terms, arrived, ss, sr, act_ref, other_ref, act_sem, swap_sem = take(8)
@@ -1104,14 +1212,16 @@
         if chunks:
             swap = PairSwap(other_ref, swap_ref, swap_sem).copy
             act_copy.wait()
+            loads.wait(chunks)
             out_sum = OutputSum(SeqScatter(seq_size, terms, arrived, ss, sr), act_ref, down_refs)
             out_sum.scatter.send_terms(out_sum.compute, merge=True)
 
+        loads.wait(2)
         xt_ref[...] = jnp.transpose(mixed_ref[...])
         for z in range(shard_size):
             go_ref[z] = dot_nn(xt_ref[...], da_ref[:, z * part : (z + 1) * part]).astype(bf16)
-        if not chunks:
-            moves[-1].start()
+        moves[-1].start()
+        loads.wait(6)
 
         @pl.loop(0, length // big)
         def _(i):
@@ -1177,13 +1287,13 @@
                 if hp == 0:
                     out_sum.scatter.merge(other_ref)
                     swap.start()
-                    moves[-1].start()
         else:
 
             @pl.loop(0, cols // pair)
             def _(hp):
                 heads(hp, rows_at(hp, pair))
 
+        loads.wait()
         for source, out in ((dq_ref, gq_ref), (dk_ref, gk_ref), (dv_ref, gv_ref)):
             xt_ref[...] = jnp.transpose(source[...])
             for z in range(shard_size):
@@ -1203,6 +1313,8 @@
         VMEM((cols, length), bf16),
         VMEM((shard_size, cols, part), bf16),
     ] + [DMA((count + 1, shard_size))] * 2
+    inputs = [d_attn, wo, mixed, q, k, v, lse, table, normed, *down]
+    scratch += held(inputs) + [DMA((len(inputs),))]
     if chunks:
         scratch += scatter_scratch(seq_size, rows, width)
         scratch += [VMEM((chunks, length, activ.shape[2]), bf16), VMEM((rows, width), bf16)]
@@ -1215,11 +1327,11 @@
         + [array((rows, width))] * (1 if chunks else 0)
         + [array(g.shape) for g in grads]
         + [grad],
-        in_specs=in_vmem(9 + chunks) + in_any(count + (1 if chunks else 0)),
+        in_specs=in_any(9 + chunks + count + (1 if chunks else 0)),
         out_specs=in_vmem(7 if chunks else 6) + in_any(count + 1),
         scratch_shapes=scratch,
         compiler_params=kernel_params(4),
-    )(d_attn, wo, mixed, q, k, v, lse, table, normed, *down, *grads, *([activ] if chunks else []))
+    )(*inputs, *grads, *([activ] if chunks else []))
     outs = list(outs)
     other = outs.pop(6) if chunks else None
     return outs[:3], outs[3:6], other, outs[6:]
@@ -1286,8 +1398,7 @@
     def kernel(*refs):
         take = Refs(refs)
         x_ref, d_hidden_ref, gains_ref, gain2_ref = take(4)
-        d_refs, w_refs, g_refs = take(3), take(3), take(3)
-        down_refs = take(chunks)
+        sources = take(9 + chunks)
         hidden_ref, other_ref = take(2) if chunks else (None, None)
         act_all = take(1)[0] if chunks else None
         sum_refs, go_ref = take(pieces), take(1)[0]
@@ -1299,7 +1410,13 @@
         gs, gr, hs, hr = take(4)
         in_terms, in_arrived, in_s, in_r = take(4)
         firsts, middles, seconds, reduce_sems = take(4)
-        held, wide, tall, load_sem, store_sem = take(5)
+        received, wide, tall, load_sem, store_sem = take(5)
+        loaded, in_sems = take(9 + chunks), take(1)[0]
+        d_refs, w_refs, g_refs = loaded[:3], loaded[3:6], loaded[6:9]
+        down_refs = loaded[9:]
+        ins = Moves(in_sems)
+        for i in [6, 7, 8, 0, 1, 2, 3, 4, 5] + list(range(9, 9 + chunks)):
+            ins.start(sources[i], loaded[i])
         if chunks:
             out_terms, out_arrived, out_s, out_r, act_ref, act_sem, out_total = take(7)
             act_copy = pltpu.make_async_copy(act_all.at[:, pl.ds(0, length), :], act_ref, act_sem)
@@ -1313,8 +1430,10 @@
             )
             for i in range(3)
         ]
+        ins.wait(3)
         for reduce in reduces:
             reduce.start()
+        ins.wait(6)
         in_sum = SeqScatter(seq_size, in_terms, in_arrived, in_s, in_r)
 
         def inputs_term(mask):
@@ -1329,13 +1448,14 @@
         in_sum.send_terms(inputs_term, merge=True)
         if chunks:
             act_copy.wait()
+            ins.wait()
             out_sum = OutputSum(
                 SeqScatter(seq_size, out_terms, out_arrived, out_s, out_r), act_ref, down_refs
             )
             out_sum.scatter.send_terms(out_sum.compute)
 
         loads = [
-            pltpu.make_async_copy(source, held.at[i % 2], load_sem.at[i % 2])
+            pltpu.make_async_copy(source, received.at[i % 2], load_sem.at[i % 2])
             for i, source in enumerate(sum_refs)
         ]
         stores = []
@@ -1356,9 +1476,9 @@
                 loads[i + 1].start()
             loads[i].wait()
             for parity in (0, 1):
-                total = held[i % 2, parity].astype(f32)
+                total = received[i % 2, parity].astype(f32)
                 for p in range(1, pairs):
-                    total = total + held[i % 2, 2 * p + parity].astype(f32)
+                    total = total + received[i % 2, 2 * p + parity].astype(f32)
                 start = parity * half + i // 3 * block
                 if i % 3 == 2:
                     store(wide, wd_ref.at[start : start + block, :], total)
@@ -1446,6 +1566,8 @@
         DMA((2,)),
         DMA((2, 2)),
     ]
+    inputs = [*d_qkv, *attn_weights, *g_qkv, *down]
+    scratch += held(inputs) + [DMA((len(inputs),))]
     if chunks:
         scratch += scatter_scratch(seq_size, rows, width)
         scratch += [VMEM((chunks, length, block), bf16), DMA, VMEM((rows, width), f32)]
@@ -1460,12 +1582,16 @@
         + [array((cols, part), f32)]
         + [array((part, units), f32)] * 2
         + [array((units, part), f32)],
-        in_specs=in_vmem(13 + chunks + 2 * extra) + in_any(extra + pieces) + in_vmem(1),
+        in_specs=in_vmem(4)
+        + in_any(9 + chunks)
+        + in_vmem(2 * extra)
+        + in_any(extra + pieces)
+        + in_vmem(1),
         out_specs=in_vmem(6 + extra) + in_any(3),
         scratch_shapes=scratch,
         compiler_params=kernel_params(5),
     )(
-        x, d_hidden, gains_all, d_gain_two, *d_qkv, *attn_weights, *g_qkv, *down,
+        x, d_hidden, gains_all, d_gain_two, *inputs,
         *([hidden, other, activ] if chunks else []), *sums, g_output,
     )
     outs = list(outs)
@@ -1482,8 +1608,10 @@
 
 
 EARLY = 4
+AHEAD = 4
+BEFORE = 2
 SUMS = (1, 4)
-SWAP_FIRST = False
+START = 3
 
 
 def body(

time: 587 us -> 540 us (0.920)
  Pallas kernels: 560 us -> 518 us
    pallas_call x1, Pallas kernels: 79.4 us -> 63.5 us  [attend_back(): pl.pallas_call(kernel, name='attend_back', out_shape=[array((length, cols...]
    pallas_call x1, Pallas kernels: 207 us -> 193 us  [forward(): pl.pallas_call(kernel, name='forward_attention', out_shape=[tokens, array...]
where the time goes in v4:
time: 540 us; the launch traced here: 536 us
  Pallas kernels  518 us (96%)
  local copies, waits for them, and re-layouts  15.4 us (3%)
    pallas_call x1, Pallas kernels, forward(): pl.pallas_call(kernel, name='forward_attention', out_shape=[tokens, array...  193 us
    pallas_call x1, Pallas kernels, mlp_back(): pl.pallas_call(kernel, name='mlp_back', out_shape=[array((rows, width), f...  112 us
    pallas_call x1, Pallas kernels, mlp(): pl.pallas_call(kernel, name='mlp', out_shape=[act] * 3 + [piece] * len(pi...  80.5 us
    pallas_call x1, Pallas kernels, finish(): pl.pallas_call(kernel, name='finish', out_shape=[array((rows, width)), ar...  68.9 us
    pallas_call x1, Pallas kernels, attend_back(): pl.pallas_call(kernel, name='attend_back', out_shape=[array((length, cols...  63.5 us
    unnamed x23, local copies, waits for them, and re-layouts  12.6 us

profile of v4, /device:TPU:0, one launch (start us, length us, event | category | flops | bytes accessed | tf_op | source)
XLA Modules:
  0.0 536.5 jit_solution(5075971261533689411)
XLA Ops:
  0.7 0.7 convert_element_type.13
  1.3 0.7 stack.9
  2.0 0.7 stack.10
  2.7 0.6 fusion.4.refs_1_
  3.3 0.4 multiply_cosine_fusion
  3.7 0.8 pad_maximum_fusion.refs_2_
  4.5 192.9 %forward_attention.1 = (bf16[1536,2048]{1,0:T(8,128)(2,1)}, f32[1536,128]{1,0:T(8,128)}, f32[4,8,512]{2,1,0:T(8,128)}, bf16[4,512,256]{2,1,0:T(8,128)(2,1)}, bf1...) custom-call(bf16[192,2048]{1,0:T(8,128)(2,1)} %bitcast.9, ...), custom_call_target="tpu_custom_call" | custom-call | tf_op jit(solution)/shard_map/forward_attention/pallas_call | solution.py:786
  197.4 80.5 %mlp.1 = (bf16[2,3072,256]{2,1,0:T(8,128)(2,1)}, bf16[2,3072,256]{2,1,0:T(8,128)(2,1)}, bf16[2,3072,256]{2,1,0:T(8,128)(2,1)}, bf16[4,256,512]{2,1,0:T(8,128)(2,...) custom-call(bf16[192,2048]{1,0:T(8,128)(2,1)} %get-tuple-element.69., ...), custom_call_target="tpu_custom_call" | custom-call | tf_op jit(solution)/shard_map/mlp/pallas_call | solution.py:999
  277.9 111.9 %mlp_back.1 = (f32[192,2048]{1,0:T(8,128)}, f32[1,2048]{1,0:T(1,128)}, bf16[1536,2048]{1,0:T(8,128)(2,1)}, bf16[4,256,512]{2,1,0:T(8,128)(2,1)}, bf16[4,256,512]...) custom-call(bf16[2,3072,256]{2,1,0:T(8,128)(2,1)} %get-tuple-element.77.refs_0_, ...), custom_call_target="tpu_custom_call" | custom-call | tf_op jit(solution)/shard_map/mlp_back/pallas_call | solution.py:1128
  389.8 63.5 %attend_back.1 = (bf16[1536,256]{1,0:T(8,128)(2,1)}, bf16[1536,256]{1,0:T(8,128)(2,1)}, bf16[1536,256]{1,0:T(8,128)(2,1)}, bf16[4,256,512]{2,1,0:T(8,128)(2,1)},...) custom-call(bf16[1536,2048]{1,0:T(8,128)(2,1)} %get-tuple-element.88, ...), custom_call_target="tpu_custom_call" | custom-call | tf_op jit(solution)/shard_map/attend_back/pallas_call | solution.py:1322
  453.3 68.9 %finish.1 = (bf16[192,2048]{1,0:T(8,128)(2,1)}, f32[8,512]{1,0:T(8,128)}, f32[512,256]{1,0:T(8,128)}, f32[512,256]{1,0:T(8,128)}, f32[512,256]{1,0:T(8,128)}, /*...) custom-call(bf16[192,2048]{1,0:T(8,128)(2,1)} %bitcast.10, ...), custom_call_target="tpu_custom_call" | custom-call | tf_op jit(solution)/shard_map/finish/pallas_call | solution.py:1576
  522.2 0.0 copy-start.6
  522.2 0.0 copy-start.5
  522.2 1.4 fusion.5
  523.7 2.1 copy.33
  525.8 2.2 copy.34
  528.1 0.8 copy.35
  528.8 0.8 copy.36
  529.6 0.8 copy.37
  530.4 0.8 copy.38
  531.2 1.3 copy.39
  532.6 1.3 copy.40
  533.9 1.0 copy-done
  534.9 1.3 copy.41
  (12 shorter events, 0.0 us)
Async XLA Ops:
  522.2 5.9 %copy-start.6 = (f32[512,256]{1,0:T(8,128)S(1)}, f32[512,256]{1,0:T(8,128)}, u32[]{:S(2)}) copy-start(f32[512,256]{1,0:T(8,128)} %get-tuple-element.146) | copy-start | bytes 1572868
  522.2 6.6 %copy-start.5 = (f32[512,256]{1,0:T(8,128)S(1)}, f32[512,256]{1,0:T(8,128)}, u32[]{:S(2)}) copy-start(f32[512,256]{1,0:T(8,128)} %get-tuple-element.147) | copy-start | bytes 1572868
  522.2 7.4 %copy-start.4 = (f32[512,256]{1,0:T(8,128)S(1)}, f32[512,256]{1,0:T(8,128)}, u32[]{:S(2)}) copy-start(f32[512,256]{1,0:T(8,128)} %get-tuple-element.148) | copy-start | bytes 1572868
  523.7 6.8 %copy-start.3 = (f32[256,512]{1,0:T(8,128)S(1)}, f32[256,512]{1,0:T(8,128)}, u32[]{:S(2)}) copy-start(f32[256,512]{1,0:T(8,128)} %get-tuple-element.149) | copy-start | bytes 1572868
  525.8 5.4 %copy-start.2 = (f32[512,1024]{1,0:T(8,128)S(1)}, f32[512,1024]{1,0:T(8,128)}, u32[]{:S(2)}) copy-start(f32[512,1024]{1,0:T(8,128)} %get-tuple-element.151) | copy-start | bytes 6291460
  529.6 2.9 copy-start.1
  532.6 2.3 copy-start

commit v5 on v4

--- a/solution.py
+++ b/solution.py
@@ -330,9 +330,10 @@
 
 
 class ShardExchange:
-    def __init__(self, size, source, out, send_sem, recv_sem):
+    def __init__(self, size, source, out, send_sem, recv_sem, bounce=None, bounce_sem=None):
         self.size, self.source, self.out = size, source, out
         self.send_sem, self.recv_sem = send_sem, recv_sem
+        self.bounce, self.bounce_sem = bounce, bounce_sem
         self.k = lax.axis_index("shard")
 
     def copy(self, step):
@@ -357,9 +358,22 @@
         )
 
     def local(self):
-        return pltpu.make_async_copy(
-            self.source(self.k), self.out.at[self.k], self.send_sem.at[0]
-        )
+        source = self.source(self.k) if self.bounce is None else self.bounce
+        return pltpu.make_async_copy(source, self.out.at[self.k], self.send_sem.at[0])
+
+    def lift(self):
+        return pltpu.make_async_copy(self.source(self.k), self.bounce, self.bounce_sem)
+
+    def start_local(self):
+        if self.bounce is None:
+            self.local().start()
+        else:
+            self.lift().start()
+
+    def settle(self):
+        if self.bounce is not None:
+            self.lift().wait()
+            self.local().start()
 
     def inner(self, step):
         target = lax.rem(self.k + step, self.size)
@@ -374,7 +388,7 @@
                 self.copy(step).start()
 
     def start_outer(self):
-        self.local().start()
+        self.start_local()
         for step in range(1, self.size):
 
             @pl.when(jnp.logical_not(self.inner(step)))
@@ -382,7 +396,7 @@
                 self.copy(step).start()
 
     def start(self):
-        self.local().start()
+        self.start_local()
         for step in range(1, self.size):
             self.copy(step).start()
 
@@ -598,6 +612,7 @@
         full_weights, heads_held = take(4), take(4)
         q_ref, k_ref, v_ref, o_ref = heads_held
         out_sems = take(1)[0]
+        bounces, bounce_sems = take(len(pieces)), take(1)[0]
         ns, nr, ts, tr, cs, cr, ds, dr, ms, mr = take(10)
         gs, gr, line_s, line_r, line_c, piece_s, piece_r, local_sem, swap_sem = take(9)
 
@@ -612,7 +627,8 @@
         wq_all, wk_all, wv_all, wo_all = full_weights
         exchanges = [
             ShardExchange(
-                shard_size, piece_source(kind, mlp_refs, c, block), out, piece_s.at[i], piece_r.at[i]
+                shard_size, piece_source(kind, mlp_refs, c, block), out, piece_s.at[i],
+                piece_r.at[i], bounces[i], bounce_sems.at[i],
             )
             for i, ((c, kind), out) in enumerate(zip(pieces, piece_refs))
         ]
@@ -740,6 +756,8 @@
         scatter.send_terms(compute, merge=True)
         for mask in near:
             cots_other.forward(mask)
+        for exchange in exchanges[:AHEAD]:
+            exchange.settle()
         scatter.merge_inner()
         scatter.merge(hidden_ref)
         for mask in far:
@@ -773,6 +791,8 @@
         own_tok.wait()
         toks.finish()
         cots_other.finish()
+        for exchange in exchanges[AHEAD:]:
+            exchange.settle()
         for exchange in exchanges:
             exchange.wait()
         outs.wait()
@@ -806,12 +826,14 @@
             array((rows, width)),
         ]
         + [array(s) for s in shapes],
-        in_specs=in_vmem(3) + in_any(1) + in_vmem(4) + in_any(3),
+        in_specs=in_vmem(8) + in_any(3),
         out_specs=in_any(1) + in_vmem(2) + in_any(8) + in_vmem(2) + in_any(4 + count),
         scratch_shapes=scatter_scratch(seq_size, rows, width)
         + [VMEM((rows, width), bf16), VMEM((length, width), bf16)]
         + held([weight] * 3 + [out_weight] + [heads] * 4)
         + [DMA((9,))]
+        + [VMEM(s[1:], bf16) for s in shapes]
+        + [DMA((count,))]
         + [DMA((seq_size,))] * 10
         + [DMA((shard_size,))] * 2
         + [DMA((4, 2, shard_size - 1))] * 2
@@ -848,6 +870,7 @@
         act_ref, dg_ref, du_ref = take(3)
         grads = take(len(pieces))
         tok_ref, tok_sem, out_sems = take(3)
+        bounces, bounce_sems = take(len(late)), take(1)[0]
         tok_copy = pltpu.make_async_copy(tok_hbm, tok_ref, tok_sem)
         tok_copy.start()
         outs = Moves(out_sems)
@@ -857,7 +880,8 @@
         entry_barrier(seq_neighbours(seq_size), shard_size)
         late_moves = [
             ShardExchange(
-                shard_size, piece_source(kind, mlp_refs, c, block), out, late_s.at[i], late_r.at[i]
+                shard_size, piece_source(kind, mlp_refs, c, block), out, late_s.at[i], late_r.at[i],
+                bounces[i], bounce_sems.at[i],
             )
             for i, ((c, kind), out) in enumerate(zip(late, late_refs))
         ]
@@ -958,6 +982,8 @@
         for load in loads[: len(early)]:
             load.wait()
         tok_copy.wait()
+        for move in late_moves:
+            move.settle()
         stage(0, first_chunks, 0)
         row_copy(1, 0, 0).start()
         other.forwards()
@@ -1014,6 +1040,8 @@
         + [VMEM(s, bf16) for s in all_shapes]
         + held([act] * 3 + [piece] * len(pieces))
         + [VMEM((length, width), bf16), DMA, DMA((3 * chunks + len(pieces),))]
+        + [VMEM(s[1:], bf16) for s in late_shapes]
+        + [DMA((max(1, len(late)),))]
         + [DMA((seq_size,))] * 2
         + [DMA((max(1, len(late)), shard_size))] * 2
         + [DMA((max(1, sums), shard_size))] * 2
@@ -1048,6 +1076,7 @@
         other_ref, swap_ref, d_attn_ref = take(3)
         ns, nr, swap_sem, own_sem, sum_s, sum_r = take(6)
         loaded, load_sems = take(2 + 2 * chunks), take(1)[0]
+        bounces, bounce_sems = take(count), take(1)[0]
         dg_ref, du_ref = loaded[:2]
         gate_refs, up_refs = loaded[2 : 2 + chunks], loaded[2 + chunks :]
         loads = Moves(load_sems)
@@ -1057,11 +1086,14 @@
         me = lax.axis_index("seq")
         entry_barrier(seq_neighbours(seq_size), shard_size)
         moves = [
-            ShardExchange(shard_size, lambda j, g=g: g.at[j], out, sum_s.at[i], sum_r.at[i])
+            ShardExchange(
+                shard_size, lambda j, g=g: g.at[j], out, sum_s.at[i], sum_r.at[i], bounces[i],
+                bounce_sems.at[i],
+            )
             for i, (g, out) in enumerate(zip(grad_refs, sum_refs))
         ]
         for move in moves[:BEFORE]:
-            move.start()
+            move.start_outer()
         swap = PairSwap(other_ref, swap_ref, swap_sem).copy
         loads.wait()
         scatters = [
@@ -1098,8 +1130,10 @@
             here.merge_leaves()
             there.merge(other_ref)
             swap.start()
+        for move in moves:
+            move.start_inner()
         for move in moves[BEFORE:]:
-            move.start()
+            move.start_outer()
         here.merge_inner()
         here.merge(d_hidden_ref)
         swap.wait()
@@ -1111,6 +1145,8 @@
         d_attn_ref[...] = d_hidden.astype(bf16)
         gather = SeqGather(seq_size, d_attn_all, rows, ns, nr, own=d_attn_ref)
         gather.start()
+        for move in moves:
+            move.settle()
         own = pltpu.make_async_copy(d_attn_ref, d_attn_all.at[rows_at(me, rows), :], own_sem)
         own.start()
         d_hidden_ref[...] = d_hidden
@@ -1144,7 +1180,9 @@
         + [DMA((2,)), DMA]
         + [DMA((max(1, count), shard_size))] * 2
         + held(inputs)
-        + [DMA((len(inputs),))],
+        + [DMA((len(inputs),))]
+        + [VMEM(g.shape[1:], bf16) for g in grads]
+        + [DMA((max(1, count),))],
         compiler_params=kernel_params(3),
     )(*inputs, hidden, cot, gains_all, *grads)
     return outs[:3], list(outs[3:])
@@ -1189,6 +1227,7 @@
         sum_refs = take(count + 1)
         do_ref, kt_ref, dk_acc, dv_acc, xt_ref, go_ref, sum_s, sum_r = take(8)
         loaded, load_sems = take(9 + chunks), take(1)[0]
+        bounces, bounce_sems = take(count), take(1)[0]
         da_ref, wo_ref, mixed_ref, q_ref, k_ref, v_ref, lse_ref, t_ref, n_ref = loaded[:9]
         down_refs = loaded[9:]
         loads = Moves(load_sems)
@@ -1204,11 +1243,16 @@
             act_copy.start()
         entry_barrier(seq_neighbours(seq_size) if chunks else [], shard_size)
         moves = [
-            ShardExchange(shard_size, lambda j, g=g: g.at[j], out, sum_s.at[i], sum_r.at[i])
-            for i, (g, out) in enumerate(zip(grad_refs + [go_ref], sum_refs))
+            ShardExchange(
+                shard_size, lambda j, g=g: g.at[j], out, sum_s.at[i], sum_r.at[i], bounce,
+                bounce_sems.at[i],
+            )
+            for i, (g, out, bounce) in enumerate(
+                zip(grad_refs + [go_ref], sum_refs, bounces + [None])
+            )
         ]
         for move in moves[:-1]:
-            move.start()
+            move.start_outer()
         if chunks:
             swap = PairSwap(other_ref, swap_ref, swap_sem).copy
             act_copy.wait()
@@ -1220,7 +1264,7 @@
         xt_ref[...] = jnp.transpose(mixed_ref[...])
         for z in range(shard_size):
             go_ref[z] = dot_nn(xt_ref[...], da_ref[:, z * part : (z + 1) * part]).astype(bf16)
-        moves[-1].start()
+        moves[-1].start_outer()
         loads.wait(6)
 
         @pl.loop(0, length // big)
@@ -1232,6 +1276,8 @@
             do_ref[r, :] = total.astype(bf16)
 
         kt_ref[...] = jnp.transpose(k_ref[...])
+        for move in moves:
+            move.settle()
         if chunks:
             out_sum.scatter.merge_inner()
 
@@ -1287,7 +1333,11 @@
                 if hp == 0:
                     out_sum.scatter.merge(other_ref)
                     swap.start()
+                    for move in moves:
+                        move.start_inner()
         else:
+            for move in moves:
+                move.start_inner()
 
             @pl.loop(0, cols // pair)
             def _(hp):
@@ -1315,6 +1365,7 @@
     ] + [DMA((count + 1, shard_size))] * 2
     inputs = [d_attn, wo, mixed, q, k, v, lse, table, normed, *down]
     scratch += held(inputs) + [DMA((len(inputs),))]
+    scratch += [VMEM(g.shape[1:], bf16) for g in grads] + [DMA((count + 1,))]
     if chunks:
         scratch += scatter_scratch(seq_size, rows, width)
         scratch += [VMEM((chunks, length, activ.shape[2]), bf16), VMEM((rows, width), bf16)]
@@ -1466,7 +1517,7 @@
             sem = store_sem.at[0 if staging is wide else 1, slot]
             if turn_of >= 2:
                 [s for s in stores if s[0] is staging][-2][1].wait()
-            staging[slot] = value
+            staging[slot] = value.astype(bf16)
             copy = pltpu.make_async_copy(staging.at[slot], target, sem)
             copy.start()
             stores.append((staging, copy))
@@ -1529,14 +1580,14 @@
             to_seq(step).start()
         for i in range(2 * third, pieces):
             collect(i)
-        wo_ref[...] = sum(go_ref[z].astype(f32) for z in range(shard_size))
+        wo_ref[...] = sum(go_ref[z].astype(f32) for z in range(shard_size)).astype(bf16)
         if chunks:
             out_sum.scatter.merge(out_total)
             output_ref[...] = (
                 out_total[...] + other_ref[...].astype(f32) + hidden_ref[...]
             ).astype(bf16)
         for reduce, out in zip(reduces, qkv_refs):
-            out[...] = jnp.transpose(reduce.total())
+            out[...] = jnp.transpose(reduce.total()).astype(bf16)
         for step in range(1, seq_size):
             to_seq(step).wait()
         gain_ref[...] = gain_line[...] + sum(gain_seq[step] for step in range(1, seq_size))
@@ -1561,8 +1612,8 @@
     scratch += [VMEM((3, pairs, cols, part), bf16)] * 3 + [DMA((3, 4, pairs))]
     scratch += [
         VMEM((2, shard_size, block, part), bf16),
-        VMEM((2, block, part), f32),
-        VMEM((2, part, block), f32),
+        VMEM((2, block, part), bf16),
+        VMEM((2, part, block), bf16),
         DMA((2,)),
         DMA((2, 2)),
     ]
@@ -1577,11 +1628,11 @@
         kernel,
         name="finish",
         out_shape=[array((rows, width)), array((8, part), f32)]
-        + [array((part, cols), f32)] * 3
+        + [array((part, cols))] * 3
         + [array((rows, width))] * extra
-        + [array((cols, part), f32)]
-        + [array((part, units), f32)] * 2
-        + [array((units, part), f32)],
+        + [array((cols, part))]
+        + [array((part, units))] * 2
+        + [array((units, part))],
         in_specs=in_vmem(4)
         + in_any(9 + chunks)
         + in_vmem(2 * extra)
@@ -1597,6 +1648,39 @@
     outs = list(outs)
     output = outs.pop(5) if chunks else None
     return outs, output
+
+
+def widen(rows, grads, gains):
+    part = gains.shape[1]
+
+    def kernel(*refs):
+        take = Refs(refs)
+        grad_refs, row_refs, gain_ref = take(len(grads)), take(len(rows)), take(1)[0]
+        row_outs, grad_outs, gain_outs = take(len(rows)), take(len(grads)), take(2)
+        low, high, load_sems, store_sems = take(len(grads)), take(len(grads)), *take(2)
+        loads, stores = Moves(load_sems), Moves(store_sems)
+        for source, target in zip(grad_refs, low):
+            loads.start(source, target)
+        for source, target in zip(row_refs, row_outs):
+            target[...] = source[...]
+        for i, out in enumerate(gain_outs):
+            out[...] = gain_ref[i : i + 1, :]
+        for a, b, out in zip(low, high, grad_outs):
+            loads.wait(1)
+            b[...] = a[...].astype(f32)
+            stores.start(b, out)
+        stores.wait()
+
+    wide = [array(g.shape, f32) for g in grads]
+    return pl.pallas_call(
+        kernel,
+        name="widen",
+        out_shape=[array(r.shape) for r in rows] + wide + [array((1, part), f32)] * 2,
+        in_specs=in_any(len(grads)) + in_vmem(len(rows) + 1),
+        out_specs=in_vmem(len(rows)) + in_any(len(grads)) + in_vmem(2),
+        scratch_shapes=held(grads) + held(wide) + [DMA((len(grads),)), DMA((len(grads),))],
+        compiler_params=kernel_params(),
+    )(*grads, *rows, gains)
 
 
 def rotation_table(position_ids):
@@ -1673,19 +1757,15 @@
     )
     if not together:
         output = output_parts(activ, down, hidden)
-    d_inputs, gain_sums, g_query, g_key, g_value, g_output, g_gate, g_up, g_down = results
+    d_inputs, gain_sums, *grads = results
+    output, d_inputs, *grads, gain_one, gain_two = widen([output, d_inputs], grads, gain_sums)
     return (
         output[None],
         d_inputs[None],
-        gain_sums[0],
-        g_query,
-        g_key,
-        g_value,
-        g_output,
-        gain_sums[1],
-        g_gate,
-        g_up,
-        g_down,
+        gain_one.reshape(-1),
+        *grads[:4],
+        gain_two.reshape(-1),
+        *grads[4:],
     )
 
 

time: 540 us -> 521 us (0.965)
  local copies, waits for them, and re-layouts: 15.4 us -> 1.36 us
    unnamed x23 -> x0, local copies, waits for them, and re-layouts: 12.6 us -> none
    pallas_call x0 -> x1, Pallas kernels: none -> 6.97 us  [widen(): pl.pallas_call(kernel, name='widen', out_shape=[array(r.shape) for r in r...]
    pallas_call x1, Pallas kernels: 112 us -> 105 us  [mlp_back(): pl.pallas_call(kernel, name='mlp_back', out_shape=[array((rows, width), f...]
    pallas_call x1, Pallas kernels: 63.5 us -> 57.9 us  [attend_back(): pl.pallas_call(kernel, name='attend_back', out_shape=[array((length, cols...]
where the time goes in v5:
time: 521 us; the launch traced here: 518 us
  Pallas kernels  513 us (98%)
    pallas_call x1, Pallas kernels, forward(): pl.pallas_call(kernel, name='forward_attention', out_shape=[tokens, array...  193 us
    pallas_call x1, Pallas kernels, mlp_back(): pl.pallas_call(kernel, name='mlp_back', out_shape=[array((rows, width), f...  105 us
    pallas_call x1, Pallas kernels, mlp(): pl.pallas_call(kernel, name='mlp', out_shape=[act] * 3 + [piece] * len(pi...  80.6 us
    pallas_call x1, Pallas kernels, finish(): pl.pallas_call(kernel, name='finish', out_shape=[array((rows, width)), ar...  69.7 us
    pallas_call x1, Pallas kernels, attend_back(): pl.pallas_call(kernel, name='attend_back', out_shape=[array((length, cols...  57.9 us

profile of v5, /device:TPU:0, one launch (start us, length us, event | category | flops | bytes accessed | tf_op | source)
XLA Modules:
  0.0 518.3 jit_solution(15398618984523645120)
XLA Ops:
  0.7 0.7 convert_element_type.13
  1.3 0.7 stack.9
  2.0 0.7 stack.10
  2.7 0.6 fusion.4.refs_1_
  3.3 0.4 multiply_cosine_fusion
  3.7 0.8 pad_maximum_fusion.refs_2_
  4.5 193.1 %forward_attention.1 = (bf16[1536,2048]{1,0:T(8,128)(2,1)}, f32[1536,128]{1,0:T(8,128)}, f32[4,8,512]{2,1,0:T(8,128)}, bf16[4,512,256]{2,1,0:T(8,128)(2,1)}, bf1...) custom-call(bf16[192,2048]{1,0:T(8,128)(2,1)} %bitcast.9, ...), custom_call_target="tpu_custom_call" | custom-call | tf_op jit(solution)/shard_map/forward_attention/pallas_call | solution.py:806
  197.6 80.6 %mlp.1 = (bf16[2,3072,256]{2,1,0:T(8,128)(2,1)}, bf16[2,3072,256]{2,1,0:T(8,128)(2,1)}, bf16[2,3072,256]{2,1,0:T(8,128)(2,1)}, bf16[4,256,512]{2,1,0:T(8,128)(2,...) custom-call(bf16[192,2048]{1,0:T(8,128)(2,1)} %get-tuple-element.80., ...), custom_call_target="tpu_custom_call" | custom-call | tf_op jit(solution)/shard_map/mlp/pallas_call | solution.py:1025
  278.2 105.2 %mlp_back.1 = (f32[192,2048]{1,0:T(8,128)}, f32[1,2048]{1,0:T(1,128)}, bf16[1536,2048]{1,0:T(8,128)(2,1)}, bf16[4,256,512]{2,1,0:T(8,128)(2,1)}, bf16[4,256,512]...) custom-call(bf16[2,3072,256]{2,1,0:T(8,128)(2,1)} %get-tuple-element.88.refs_0_, ...), custom_call_target="tpu_custom_call" | custom-call | tf_op jit(solution)/shard_map/mlp_back/pallas_call | solution.py:1164
  383.4 57.9 %attend_back.1 = (bf16[1536,256]{1,0:T(8,128)(2,1)}, bf16[1536,256]{1,0:T(8,128)(2,1)}, bf16[1536,256]{1,0:T(8,128)(2,1)}, bf16[4,256,512]{2,1,0:T(8,128)(2,1)},...) custom-call(bf16[1536,2048]{1,0:T(8,128)(2,1)} %get-tuple-element.99, ...), custom_call_target="tpu_custom_call" | custom-call | tf_op jit(solution)/shard_map/attend_back/pallas_call | solution.py:1373
  441.3 69.7 %finish.1 = (bf16[192,2048]{1,0:T(8,128)(2,1)}, f32[8,512]{1,0:T(8,128)}, bf16[512,256]{1,0:T(8,128)(2,1)}, bf16[512,256]{1,0:T(8,128)(2,1)}, bf16[512,256]{1,0:...) custom-call(bf16[192,2048]{1,0:T(8,128)(2,1)} %bitcast.10, ...), custom_call_target="tpu_custom_call" | custom-call | tf_op jit(solution)/shard_map/finish/pallas_call | solution.py:1627
  511.0 7.0 %widen.1 = (bf16[192,2048]{1,0:T(8,128)(2,1)}, bf16[192,2048]{1,0:T(8,128)(2,1)}, f32[512,256]{1,0:T(8,128)}, f32[512,256]{1,0:T(8,128)}, f32[512,256]{1,0:T(8,1...) custom-call(bf16[512,256]{1,0:T(8,128)(2,1)} %get-tuple-element.128., ...), custom_call_target="tpu_custom_call" | custom-call | tf_op jit(solution)/shard_map/widen/pallas_call | solution.py:1675
  (1 shorter events, 0.0 us)

commit v6 on v5

--- a/solution.py
+++ b/solution.py
@@ -641,6 +641,7 @@
         swap_cot = PairSwap(cot_ref, cot_other.at[mine_rows, :], swap_sem.at[0]).copy
         for line in lines[:3]:
             line.step(0)
+        swap_cot.start()
         own_cot.start()
         table_all[mine_rows, :] = table_ref[...]
         tables.start()
@@ -664,10 +665,11 @@
             for line in lines[:3]:
                 line.step(step)
             if step == 2:
-                swap_cot.start()
                 lines[3].step(0)
                 for mask in far:
                     normed.forward(mask)
+                swap_cot.wait_recv()
+                cots_other.start()
         tables.finish()
         normed.finish()
         outs = Moves(out_sems)
@@ -728,8 +730,8 @@
 
         if cols == 2 * pair:
             attend(0, slice(0, pair))
-            swap_cot.wait_recv()
-            cots_other.start()
+            for mask in near:
+                cots_other.forward(mask)
             start_pieces(2)
             attend(1, slice(pair, cols))
         else:
@@ -738,9 +740,11 @@
             def _(hp):
                 attend(hp, rows_at(hp, pair))
 
-            swap_cot.wait_recv()
-            cots_other.start()
+            for mask in near:
+                cots_other.forward(mask)
             start_pieces(2)
+        for mask in far:
+            cots_other.forward(mask)
         lines[3].step(shard_size - 1)
         start_pieces(3)
         outs.start(full_weights[3], weights_out[3])
@@ -754,14 +758,10 @@
                 scatter.put(mask, slice(z * part, (z + 1) * part), dot_nn(tokens, wo_all[z]))
 
         scatter.send_terms(compute, merge=True)
-        for mask in near:
-            cots_other.forward(mask)
         for exchange in exchanges[:AHEAD]:
             exchange.settle()
         scatter.merge_inner()
         scatter.merge(hidden_ref)
-        for mask in far:
-            cots_other.forward(mask)
         hidden = hidden_ref[...] + x_ref[...].astype(f32)
         hidden_ref[...] = hidden
         scaled = hidden * inverse_rms(hidden)
@@ -1695,7 +1695,7 @@
 AHEAD = 4
 BEFORE = 2
 SUMS = (1, 4)
-START = 3
+START = 2
 
 
 def body(

time: 521 us -> 507 us (0.973)
  Pallas kernels: 513 us -> 499 us
    pallas_call x1, Pallas kernels: 193 us -> 183 us  [forward(): pl.pallas_call(kernel, name='forward_attention', out_shape=[tokens, array...]
where the time goes in v6:
time: 507 us; the launch traced here: 504 us
  Pallas kernels  499 us (98%)
    pallas_call x1, Pallas kernels, forward(): pl.pallas_call(kernel, name='forward_attention', out_shape=[tokens, array...  183 us
    pallas_call x1, Pallas kernels, mlp_back(): pl.pallas_call(kernel, name='mlp_back', out_shape=[array((rows, width), f...  101 us
    pallas_call x1, Pallas kernels, mlp(): pl.pallas_call(kernel, name='mlp', out_shape=[act] * 3 + [piece] * len(pi...  80.4 us
    pallas_call x1, Pallas kernels, finish(): pl.pallas_call(kernel, name='finish', out_shape=[array((rows, width)), ar...  68.5 us
    pallas_call x1, Pallas kernels, attend_back(): pl.pallas_call(kernel, name='attend_back', out_shape=[array((length, cols...  58.9 us

profile of v6, /device:TPU:0, one launch (start us, length us, event | category | flops | bytes accessed | tf_op | source)
XLA Modules:
  0.0 503.9 jit_solution(7852563390426207302)
XLA Ops:
  0.7 0.7 convert_element_type.13
  1.3 0.7 stack.9
  2.0 0.7 stack.10
  2.7 0.6 fusion.4.refs_1_
  3.3 0.4 multiply_cosine_fusion
  3.7 0.8 pad_maximum_fusion.refs_2_
  4.5 183.0 %forward_attention.1 = (bf16[1536,2048]{1,0:T(8,128)(2,1)}, f32[1536,128]{1,0:T(8,128)}, f32[4,8,512]{2,1,0:T(8,128)}, bf16[4,512,256]{2,1,0:T(8,128)(2,1)}, bf1...) custom-call(bf16[192,2048]{1,0:T(8,128)(2,1)} %bitcast.9, ...), custom_call_target="tpu_custom_call" | custom-call | tf_op jit(solution)/shard_map/forward_attention/pallas_call | solution.py:806
  187.6 80.4 %mlp.1 = (bf16[2,3072,256]{2,1,0:T(8,128)(2,1)}, bf16[2,3072,256]{2,1,0:T(8,128)(2,1)}, bf16[2,3072,256]{2,1,0:T(8,128)(2,1)}, bf16[4,256,512]{2,1,0:T(8,128)(2,...) custom-call(bf16[192,2048]{1,0:T(8,128)(2,1)} %get-tuple-element.80., ...), custom_call_target="tpu_custom_call" | custom-call | tf_op jit(solution)/shard_map/mlp/pallas_call | solution.py:1025
  268.0 101.3 %mlp_back.1 = (f32[192,2048]{1,0:T(8,128)}, f32[1,2048]{1,0:T(1,128)}, bf16[1536,2048]{1,0:T(8,128)(2,1)}, bf16[4,256,512]{2,1,0:T(8,128)(2,1)}, bf16[4,256,512]...) custom-call(bf16[2,3072,256]{2,1,0:T(8,128)(2,1)} %get-tuple-element.88.refs_0_, ...), custom_call_target="tpu_custom_call" | custom-call | tf_op jit(solution)/shard_map/mlp_back/pallas_call | solution.py:1164
  369.3 58.9 %attend_back.1 = (bf16[1536,256]{1,0:T(8,128)(2,1)}, bf16[1536,256]{1,0:T(8,128)(2,1)}, bf16[1536,256]{1,0:T(8,128)(2,1)}, bf16[4,256,512]{2,1,0:T(8,128)(2,1)},...) custom-call(bf16[1536,2048]{1,0:T(8,128)(2,1)} %get-tuple-element.99, ...), custom_call_target="tpu_custom_call" | custom-call | tf_op jit(solution)/shard_map/attend_back/pallas_call | solution.py:1373
  428.2 68.5 %finish.1 = (bf16[192,2048]{1,0:T(8,128)(2,1)}, f32[8,512]{1,0:T(8,128)}, bf16[512,256]{1,0:T(8,128)(2,1)}, bf16[512,256]{1,0:T(8,128)(2,1)}, bf16[512,256]{1,0:...) custom-call(bf16[192,2048]{1,0:T(8,128)(2,1)} %bitcast.10, ...), custom_call_target="tpu_custom_call" | custom-call | tf_op jit(solution)/shard_map/finish/pallas_call | solution.py:1627
  496.6 7.0 %widen.1 = (bf16[192,2048]{1,0:T(8,128)(2,1)}, bf16[192,2048]{1,0:T(8,128)(2,1)}, f32[512,256]{1,0:T(8,128)}, f32[512,256]{1,0:T(8,128)}, f32[512,256]{1,0:T(8,1...) custom-call(bf16[512,256]{1,0:T(8,128)(2,1)} %get-tuple-element.128., ...), custom_call_target="tpu_custom_call" | custom-call | tf_op jit(solution)/shard_map/widen/pallas_call | solution.py:1675
  (1 shorter events, 0.0 us)

commit v7 on v6

--- a/solution.py
+++ b/solution.py
@@ -586,7 +586,7 @@
     return [m for m in masks if popcount(m) == 1], [m for m in masks if popcount(m) > 1]
 
 
-def forward(x, gains, table, cot, attn_weights, mlp_weights, pieces, block):
+def forward(x, gain_one, gain_two, table, cot, attn_weights, mlp_weights, pieces, block):
     seq_size, shard_size = lax.axis_size("seq"), lax.axis_size("shard")
     rows, width = x.shape
     part, cols = attn_weights[0].shape
@@ -598,7 +598,7 @@
 
     def kernel(*refs):
         take = Refs(refs)
-        x_ref, gains_ref, table_ref, cot_ref = take(4)
+        x_ref, gain_one_ref, gain_two_ref, table_ref, cot_ref = take(5)
         own_weights = take(4)
         mlp_refs = dict(zip(("gate", "up", "down"), take(3)))
         normed_out, table_all, gains_all = take(3)
@@ -612,11 +612,14 @@
         full_weights, heads_held = take(4), take(4)
         q_ref, k_ref, v_ref, o_ref = heads_held
         out_sems = take(1)[0]
-        bounces, bounce_sems = take(len(pieces)), take(1)[0]
+        bounces, bounce_sems, gains_ref = take(len(pieces)), *take(2)
         ns, nr, ts, tr, cs, cr, ds, dr, ms, mr = take(10)
         gs, gr, line_s, line_r, line_c, piece_s, piece_r, local_sem, swap_sem = take(9)
 
         me, mine = lax.axis_index("seq"), lax.axis_index("shard")
+        gains_ref[...] = jnp.zeros_like(gains_ref)
+        gains_ref[0:1, :] = gain_one_ref[...].astype(f32).reshape(1, part)
+        gains_ref[1:2, :] = gain_two_ref[...].astype(f32).reshape(1, part)
         entry_barrier(seq_neighbours(seq_size), shard_size)
         gain = ShardExchange(shard_size, lambda j: gains_ref, gains_all, gs, gr)
         gain.start()
@@ -809,7 +812,7 @@
         out_shape=[
             tokens,
             array((length, table.shape[1]), f32),
-            array((shard_size,) + gains.shape, f32),
+            array((shard_size, 8, part), f32),
             weight,
             weight,
             weight,
@@ -826,14 +829,14 @@
             array((rows, width)),
         ]
         + [array(s) for s in shapes],
-        in_specs=in_vmem(8) + in_any(3),
+        in_specs=in_vmem(9) + in_any(3),
         out_specs=in_any(1) + in_vmem(2) + in_any(8) + in_vmem(2) + in_any(4 + count),
         scratch_shapes=scatter_scratch(seq_size, rows, width)
         + [VMEM((rows, width), bf16), VMEM((length, width), bf16)]
         + held([weight] * 3 + [out_weight] + [heads] * 4)
         + [DMA((9,))]
         + [VMEM(s[1:], bf16) for s in shapes]
-        + [DMA((count,))]
+        + [DMA((count,)), VMEM((8, part), f32)]
         + [DMA((seq_size,))] * 10
         + [DMA((shard_size,))] * 2
         + [DMA((4, 2, shard_size - 1))] * 2
@@ -841,7 +844,7 @@
         + [DMA((count, shard_size))] * 2
         + [DMA((2,)), DMA((2, 2))],
         compiler_params=kernel_params(1),
-    )(x, gains, table, cot, *attn_weights, *mlp_weights)
+    )(x, gain_one, gain_two, table, cot, *attn_weights, *mlp_weights)
     return outs[:17], list(outs[17:])
 
 
@@ -1714,7 +1717,6 @@
 ):
     shard_size = lax.axis_size("shard")
     x, cot = inputs[0], cotangent[0]
-    gains = jnp.pad(jnp.stack([attn_gain, mlp_gain]).astype(f32), ((0, 6), (0, 0)))
     table = rotation_table(positions[0])
     half = w_gate.shape[1] // 2
     block = row_step(half, 256)
@@ -1723,7 +1725,7 @@
     early, late = pieces[:EARLY], pieces[EARLY:]
     mlp_weights = (w_gate, w_up, w_down)
     held, early_weights = forward(
-        x, gains, table, cot, (w_query, w_key, w_value, w_output), mlp_weights, early, block
+        x, attn_gain, mlp_gain, table, cot, (w_query, w_key, w_value, w_output), mlp_weights, early, block
     )
     normed, tables, gains_all, wq, wk, wv, wo, q, k, v, mixed, lse, hidden = held[:13]
     cot_all, cot_other, tok, tok_other = held[13:]

time: 507 us -> 505 us (level)
  no operation moved by 1% of the time
where the time goes in v7:
time: 505 us; the launch traced here: 502 us
  Pallas kernels  499 us (99%)
    pallas_call x1, Pallas kernels, forward(): pl.pallas_call(kernel, name='forward_attention', out_shape=[tokens, array...  183 us
    pallas_call x1, Pallas kernels, mlp_back(): pl.pallas_call(kernel, name='mlp_back', out_shape=[array((rows, width), f...  101 us
    pallas_call x1, Pallas kernels, mlp(): pl.pallas_call(kernel, name='mlp', out_shape=[act] * 3 + [piece] * len(pi...  80.4 us
    pallas_call x1, Pallas kernels, finish(): pl.pallas_call(kernel, name='finish', out_shape=[array((rows, width)), ar...  68.5 us
    pallas_call x1, Pallas kernels, attend_back(): pl.pallas_call(kernel, name='attend_back', out_shape=[array((length, cols...  58.8 us

profile of v7, /device:TPU:0, one launch (start us, length us, event | category | flops | bytes accessed | tf_op | source)
XLA Modules:
  0.0 502.0 jit_solution(11359591696933351483)
XLA Ops:
  0.7 0.7 convert_element_type.10
  1.3 0.4 multiply_cosine_fusion
  1.8 0.8 pad_maximum_fusion.refs_3_
  2.6 183.1 %forward_attention.1 = (bf16[1536,2048]{1,0:T(8,128)(2,1)}, f32[1536,128]{1,0:T(8,128)}, f32[4,8,512]{2,1,0:T(8,128)}, bf16[4,512,256]{2,1,0:T(8,128)(2,1)}, bf1...) custom-call(bf16[192,2048]{1,0:T(8,128)(2,1)} %bitcast.9, ...), custom_call_target="tpu_custom_call" | custom-call | tf_op jit(solution)/shard_map/forward_attention/pallas_call | solution.py:809
  185.7 80.4 %mlp.1 = (bf16[2,3072,256]{2,1,0:T(8,128)(2,1)}, bf16[2,3072,256]{2,1,0:T(8,128)(2,1)}, bf16[2,3072,256]{2,1,0:T(8,128)(2,1)}, bf16[4,256,512]{2,1,0:T(8,128)(2,...) custom-call(bf16[192,2048]{1,0:T(8,128)(2,1)} %get-tuple-element.80., ...), custom_call_target="tpu_custom_call" | custom-call | tf_op jit(solution)/shard_map/mlp/pallas_call | solution.py:1028
  266.1 101.3 %mlp_back.1 = (f32[192,2048]{1,0:T(8,128)}, f32[1,2048]{1,0:T(1,128)}, bf16[1536,2048]{1,0:T(8,128)(2,1)}, bf16[4,256,512]{2,1,0:T(8,128)(2,1)}, bf16[4,256,512]...) custom-call(bf16[2,3072,256]{2,1,0:T(8,128)(2,1)} %get-tuple-element.88.refs_0_, ...), custom_call_target="tpu_custom_call" | custom-call | tf_op jit(solution)/shard_map/mlp_back/pallas_call | solution.py:1167
  367.4 58.8 %attend_back.1 = (bf16[1536,256]{1,0:T(8,128)(2,1)}, bf16[1536,256]{1,0:T(8,128)(2,1)}, bf16[1536,256]{1,0:T(8,128)(2,1)}, bf16[4,256,512]{2,1,0:T(8,128)(2,1)},...) custom-call(bf16[1536,2048]{1,0:T(8,128)(2,1)} %get-tuple-element.99, ...), custom_call_target="tpu_custom_call" | custom-call | tf_op jit(solution)/shard_map/attend_back/pallas_call | solution.py:1376
  426.3 68.5 %finish.1 = (bf16[192,2048]{1,0:T(8,128)(2,1)}, f32[8,512]{1,0:T(8,128)}, bf16[512,256]{1,0:T(8,128)(2,1)}, bf16[512,256]{1,0:T(8,128)(2,1)}, bf16[512,256]{1,0:...) custom-call(bf16[192,2048]{1,0:T(8,128)(2,1)} %bitcast.10, ...), custom_call_target="tpu_custom_call" | custom-call | tf_op jit(solution)/shard_map/finish/pallas_call | solution.py:1630
  494.8 7.0 %widen.1 = (bf16[192,2048]{1,0:T(8,128)(2,1)}, bf16[192,2048]{1,0:T(8,128)(2,1)}, f32[512,256]{1,0:T(8,128)}, f32[512,256]{1,0:T(8,128)}, f32[512,256]{1,0:T(8,1...) custom-call(bf16[512,256]{1,0:T(8,128)(2,1)} %get-tuple-element.128., ...), custom_call_target="tpu_custom_call" | custom-call | tf_op jit(solution)/shard_map/widen/pallas_call | solution.py:1678
  (1 shorter events, 0.0 us)
